TPU v7x, 32 devices: a whole 2x2x4 slice. The times are simulated.
32 devices in a mesh: dp: 8 (over z, y), tensor: 4 (over x, core).
Axes of the slice: x: 2, y: 2, z: 4, core: 2. Of those that a mesh axis runs over, the one named last changes fastest.
Arguments:
- layer_input: bfloat16 [16384, 2048], P(('dp', 'tensor')), may hold values from -6 to 6
- seq_lens: int32 [8, 4], P('dp'), may hold values from 1 to 2045, as said below
- ln_gain: float32 [2048], replicated, may hold values from 0.5 to 1.5
- ln_bias: float32 [2048], replicated, may hold values from -1.25 to 1.25
- w_qkv: bfloat16 [2048, 3, 2048], P('dp', None, 'tensor'), may hold values from -0.125 to 0.125
- b_qkv: float32 [3, 2048], P(None, 'tensor'), may hold values from -3 to 3
- w_dense: bfloat16 [2048, 2048], P('tensor', 'dp'), may hold values from -0.375 to 0.375
- b_dense: float32 [2048], replicated, may hold values from -1.75 to 1.75
- w_fc1: bfloat16 [2048, 8192], P('dp', 'tensor'), may hold values from -0.125 to 0.125
- b_fc1: float32 [8192], P('tensor'), may hold values from -3 to 3
- w_fc2: bfloat16 [8192, 2048], P('tensor', 'dp'), may hold values from -0.0625 to 0.0625
- b_fc2: float32 [2048], replicated, may hold values from -1.75 to 1.75
- cotangent: bfloat16 [16384, 2048], P(('dp', 'tensor')), may hold values from -6 to 6
Outputs:
- layer_output: bfloat16 [16384, 2048], P(('dp', 'tensor'))
- grad_x: float32 [16384, 2048], P(('dp', 'tensor'))
- grad_ln_gain: float32 [2048], replicated
- grad_ln_bias: float32 [2048], replicated
- grad_w_qkv: float32 [2048, 3, 2048], P('dp', None, 'tensor')
- grad_b_qkv: float32 [3, 2048], P(None, 'tensor')
- grad_w_dense: float32 [2048, 2048], P('tensor', 'dp')
- grad_b_dense: float32 [2048], replicated
- grad_w_fc1: float32 [2048, 8192], P('dp', 'tensor')
- grad_b_fc1: float32 [8192], P('tensor')
- grad_w_fc2: float32 [8192, 2048], P('tensor', 'dp')
- grad_b_fc2: float32 [2048], replicated
Inputs may be any that keep to these rules, and one draw needn't show every extreme that they name: `seq_lens`: in each group, one sequence, which one drawn from the seed, starts within the first 512 rows and ends within the last 512 rows of the group; the lengths of a group sum to at most 2048, leaving fewer than 129 padding rows. The first group has no padding and all its sequences but the long one have length 1.
All inputs are finite; a program needn't handle non-finite values.
Results may differ from a plain program's by a relative error of at most 0.01.
Values may be sent and summed in bfloat16 or wider, within the bound.
A program may use at most 256 MiB of HBM per device.

v0:
```python
import math

import jax
import jax.numpy as jnp
from jax import lax
from jax.sharding import PartitionSpec as P

HEAD = 64
ROT = 32


EPS = 1e-05


def layout(seq_row, total_rows):
    count = seq_row.shape[0]
    ends = jnp.cumsum(seq_row)
    starts = ends - seq_row
    rows = jnp.arange(total_rows, dtype=jnp.int32)
    segment = jnp.sum((rows[:, None] >= ends[None, :]).astype(jnp.int32), axis=1)
    start_all = jnp.concatenate([starts, ends[-1:]])
    labels = jnp.arange(count + 1, dtype=jnp.int32)
    first = jnp.sum(jnp.where(segment[:, None] == labels[None, :], start_all[None, :], 0), axis=1)
    return (segment, rows - first)


def rotary_tables(position):
    steps = jnp.arange(ROT // 2, dtype=jnp.float32)
    inverse = jnp.exp(-math.log(10000.0) * 2.0 * steps / ROT)
    angle = position.astype(jnp.float32)[:, None] * inverse[None, :]
    return (jnp.cos(angle)[:, None, :], jnp.sin(angle)[:, None, :])


def apply_rotary(heads, cosine, sine):
    half = ROT // 2
    first = heads[..., :half]
    second = heads[..., half:ROT]
    turned = jnp.concatenate(
        [first * cosine - second * sine, second * cosine + first * sine], axis=-1
    )
    return jnp.concatenate([turned, heads[..., ROT:]], axis=-1)


def norm_piece(rows, gain, shift):
    mean = jnp.mean(rows, axis=1, keepdims=True)
    centred = rows - mean
    var = jnp.mean(centred * centred, axis=1, keepdims=True)
    return centred * lax.rsqrt(var + EPS) * gain + shift


def smooth_gate(values):
    return jax.nn.gelu(values, approximate=True)


def local(
    layer_input,
    seq_lens,
    ln_gain,
    ln_bias,
    w_qkv,
    b_qkv,
    w_dense,
    b_dense,
    w_fc1,
    b_fc1,
    w_fc2,
    b_fc2,
    cotangent,
):
    own_rows = layer_input.shape[0]
    group_rows = own_rows * lax.axis_size("tensor")
    first_row = lax.axis_index("tensor") * own_rows
    scale = 1.0 / math.sqrt(HEAD)
    x_float = layer_input.astype(jnp.float32)
    normed_own = norm_piece(x_float, ln_gain, ln_bias)
    normed = lax.all_gather(normed_own.astype(jnp.bfloat16), "tensor", axis=0, tiled=True)
    wq_all, wd_all, w1_all, w2_all = (
        lax.all_gather(w_qkv, "dp", axis=0, tiled=True),
        lax.all_gather(w_dense, "dp", axis=1, tiled=True),
        lax.all_gather(w_fc1, "dp", axis=0, tiled=True),
        lax.all_gather(w_fc2, "dp", axis=1, tiled=True),
    )
    segment, position = layout(seq_lens[0], group_rows)
    cosine, sine = rotary_tables(position)
    mixed = (
        jnp.einsum("rd,dce->rce", normed, wq_all, preferred_element_type=jnp.float32) + b_qkv[None]
    )
    width = mixed.shape[2]
    heads = width // HEAD
    query = apply_rotary(mixed[:, 0].reshape(group_rows, heads, HEAD), cosine, sine).astype(
        jnp.bfloat16
    )
    key = apply_rotary(mixed[:, 1].reshape(group_rows, heads, HEAD), cosine, sine).astype(
        jnp.bfloat16
    )
    value = mixed[:, 2].reshape(group_rows, heads, HEAD).astype(jnp.bfloat16)
    block = min(512, group_rows)
    starts = jnp.arange(group_rows // block, dtype=jnp.int32) * block
    columns = jnp.arange(group_rows, dtype=jnp.int32)

    def scores_for(start):
        q_blk = lax.dynamic_slice_in_dim(query, start, block, 0)
        seg_blk = lax.dynamic_slice_in_dim(segment, start, block, 0)
        raw = jnp.einsum("qhd,khd->hqk", q_blk, key, preferred_element_type=jnp.float32) * scale
        rows_idx = start + jnp.arange(block, dtype=jnp.int32)
        allowed = (seg_blk[:, None] == segment[None, :]) & (columns[None, :] <= rows_idx[:, None])
        return (jnp.where(allowed[None], raw, -1e30), q_blk)

    def forward_block(start):
        masked, q_blk = scores_for(start)
        top = jnp.max(masked, axis=2, keepdims=True)
        weights = jnp.exp(masked - top)
        total = jnp.sum(weights, axis=2, keepdims=True)
        prob = (weights / total).astype(jnp.bfloat16)
        result = jnp.einsum("hqk,khd->qhd", prob, value, preferred_element_type=jnp.float32)
        return (result, (top + jnp.log(total))[..., 0])

    pieces, log_totals = lax.map(forward_block, starts)
    attended = pieces.reshape(group_rows, width).astype(jnp.bfloat16)
    pre = jnp.dot(normed, w1_all, preferred_element_type=jnp.float32) + b_fc1[None]
    act = smooth_gate(pre).astype(jnp.bfloat16)
    partial_value = jnp.dot(attended, wd_all, preferred_element_type=jnp.float32) + jnp.dot(
        act, w2_all, preferred_element_type=jnp.float32
    )
    branch = lax.psum_scatter(partial_value, "tensor", scatter_dimension=0, tiled=True)
    output = (x_float + branch + b_dense + b_fc2).astype(jnp.bfloat16)
    own_index = first_row + jnp.arange(own_rows, dtype=jnp.int32)
    used = jnp.sum(seq_lens[0])
    valid = (own_index < used).astype(jnp.float32)[:, None]
    grad_out = cotangent.astype(jnp.float32) * valid
    grad_rows = lax.all_gather(grad_out.astype(jnp.bfloat16), "tensor", axis=0, tiled=True)
    wq_back, wd_back, w1_back, w2_back = (
        lax.all_gather(w_qkv, "dp", axis=0, tiled=True),
        lax.all_gather(w_dense, "dp", axis=1, tiled=True),
        lax.all_gather(w_fc1, "dp", axis=0, tiled=True),
        lax.all_gather(w_fc2, "dp", axis=1, tiled=True),
    )
    grad_att = jnp.einsum("rd,ad->ra", grad_rows, wd_back, preferred_element_type=jnp.float32)
    grad_att = grad_att.astype(jnp.bfloat16).reshape(group_rows, heads, HEAD)
    grad_act = jnp.einsum("rd,fd->rf", grad_rows, w2_back, preferred_element_type=jnp.float32)
    gate_pull = jax.vjp(smooth_gate, pre)[1]
    grad_pre = gate_pull(grad_act)[0].astype(jnp.bfloat16)
    grad_bias_fc1 = jnp.sum(grad_pre, axis=0, dtype=jnp.float32)

    def backward_block(carry, item):
        grad_key, grad_value = carry
        start, log_blk = item
        masked, q_blk = scores_for(start)
        prob = jnp.exp(masked - log_blk[..., None])
        g_blk = lax.dynamic_slice_in_dim(grad_att, start, block, 0)
        grad_prob = jnp.einsum("qhd,khd->hqk", g_blk, value, preferred_element_type=jnp.float32)
        inner = jnp.sum(prob * grad_prob, axis=2, keepdims=True)
        grad_scores = (prob * (grad_prob - inner)).astype(jnp.bfloat16)
        grad_q = (
            jnp.einsum("hqk,khd->qhd", grad_scores, key, preferred_element_type=jnp.float32) * scale
        )
        grad_key = (
            grad_key
            + jnp.einsum("hqk,qhd->khd", grad_scores, q_blk, preferred_element_type=jnp.float32)
            * scale
        )
        grad_value = grad_value + jnp.einsum(
            "hqk,qhd->khd", prob.astype(jnp.bfloat16), g_blk, preferred_element_type=jnp.float32
        )
        return ((grad_key, grad_value), grad_q)

    empty = jnp.zeros((group_rows, heads, HEAD), jnp.float32)
    (grad_key, grad_value), grad_query = lax.scan(
        backward_block, (empty, empty), (starts, log_totals)
    )
    grad_query = apply_rotary(grad_query.reshape(group_rows, heads, HEAD), cosine, -sine)
    grad_key = apply_rotary(grad_key, cosine, -sine)
    grad_mixed = jnp.stack(
        [
            grad_query.reshape(group_rows, width),
            grad_key.reshape(group_rows, width),
            grad_value.reshape(group_rows, width),
        ],
        axis=1,
    ).astype(jnp.bfloat16)
    grad_bias_qkv = jnp.sum(grad_mixed, axis=0, dtype=jnp.float32)
    grad_normed = jnp.einsum("rce,dce->rd", grad_mixed, wq_back, preferred_element_type=jnp.float32)
    grad_normed = grad_normed + jnp.einsum(
        "rf,df->rd", grad_pre, w1_back, preferred_element_type=jnp.float32
    )
    grad_normed_own = lax.psum_scatter(grad_normed, "tensor", scatter_dimension=0, tiled=True)
    norm_pull = jax.vjp(norm_piece, x_float, ln_gain, ln_bias)[1]
    grad_x_norm, grad_gain, grad_shift = norm_pull(grad_normed_own)
    grad_x = grad_x_norm + grad_out
    grad_out_sum = jnp.sum(grad_out, axis=0)
    grad_gain, grad_shift, grad_out_sum = lax.psum(
        (grad_gain, grad_shift, grad_out_sum), ("dp", "tensor")
    )
    grad_bias_qkv, grad_bias_fc1 = lax.psum((grad_bias_qkv, grad_bias_fc1), "dp")
    grad_qkv = jnp.einsum("rd,rce->dce", normed, grad_mixed, preferred_element_type=jnp.float32)
    grad_fc1 = jnp.einsum("rd,rf->df", normed, grad_pre, preferred_element_type=jnp.float32)
    grad_dense = jnp.einsum("ra,rd->ad", attended, grad_rows, preferred_element_type=jnp.float32)
    grad_fc2 = jnp.einsum("rf,rd->fd", act, grad_rows, preferred_element_type=jnp.float32)
    own_qkv, own_dense, own_fc1, own_fc2 = (
        lax.psum_scatter(grad_qkv, "dp", scatter_dimension=0, tiled=True),
        lax.psum_scatter(grad_dense, "dp", scatter_dimension=1, tiled=True),
        lax.psum_scatter(grad_fc1, "dp", scatter_dimension=0, tiled=True),
        lax.psum_scatter(grad_fc2, "dp", scatter_dimension=1, tiled=True),
    )
    return (
        output,
        grad_x,
        grad_gain,
        grad_shift,
        own_qkv,
        grad_bias_qkv,
        own_dense,
        grad_out_sum,
        own_fc1,
        grad_bias_fc1,
        own_fc2,
        grad_out_sum,
    )


def solution(mesh):
    in_specs = (
        P(("dp", "tensor"), None),
        P("dp", None),
        P(),
        P(),
        P("dp", None, "tensor"),
        P(None, "tensor"),
        P("tensor", "dp"),
        P(),
        P("dp", "tensor"),
        P("tensor"),
        P("tensor", "dp"),
        P(),
        P(("dp", "tensor"), None),
    )
    out_specs = (
        P(("dp", "tensor"), None),
        P(("dp", "tensor"), None),
        P(),
        P(),
        P("dp", None, "tensor"),
        P(None, "tensor"),
        P("tensor", "dp"),
        P(),
        P("dp", "tensor"),
        P("tensor"),
        P("tensor", "dp"),
        P(),
    )
    return jax.shard_map(local, mesh=mesh, in_specs=in_specs, out_specs=out_specs, check_vma=False)
```

profile of v0, /device:TPU:0, one launch (start us, length us, event | category | flops | bytes accessed | tf_op | source)
XLA Modules:
  0.0 2227.0 jit_solution(2966658703319847249)
XLA Ops:
  26.0 87.3 %all-gather.9.cloned.1.call-done = bf16[2048,3,512]{0,2,1:T(8,128)(2,1)} async-done(((bf16[256,3,512]{0,2,1:T(8,128)(2,1)}), bf16[2048,3,512]{0,2,1:T(8,128)(2,1)}) %all-gather.9.cloned.1.call-update) | async-done | bytes 6291472 | tf_op jit(solution)/shard_map/all_gather | solution.py:78
  113.3 58.6 %all-gather.7.cloned.1.call-done = bf16[2048,2048]{1,0:T(8,128)(2,1)} async-done(((bf16[512,2048]{1,0:T(8,128)(2,1)}), bf16[2048,2048]{1,0:T(8,128)(2,1)}) %all-gather.7.cloned.1.call-update) | async-done | bytes 8388624 | tf_op jit(solution)/shard_map/all_gather | solution.py:76
  195.0 206.9 %while.28 = (s32[]{:T(128)}, bf16[4,512,8,64]{1,3,2,0:T(8,128)(2,1)}, f32[4,8,512]{2,1,0:T(8,128)S(1)}, s32[4]{0:T(128)S(1)}, s32[2048]{0:T(1024)S(1)}, /*index=...) while((s32[]{:T(128)}, ...), condition=%wide.region_8.9_spmd.clone, body=%wide.region_5.8_spmd.clone.sunk | while | flops 2251289088 | bytes 110774960 | solution.py:118
  411.8 542.6 %while.29 = (s32[]{:T(128)}, f32[2048,8,64]{0,2,1:T(8,128)}, f32[2048,8,64]{0,2,1:T(8,128)}, f32[4,512,8,64]{1,0,3,2:T(4,128)}, s32[4]{0:T(128)S(1)}, /*index=5*...) while((s32[]{:T(128)}, f32[2048,8,64]{0,2,1:T(8,128)}, ...), condition=%wide.region_13.14_spmd.clone, body=%wide.region_11.13_spmd.clone.sunk | while | flops 5452853760 | bytes 284264640 | solution.py:168
  434.2 26.4 %multiply_reduce_fusion.2 = (f32[8,512]{1,0:T(8,128)S(1)}, f32[8,512,2048]{2,1,0:T(8,128)}) fusion(f32[8,512,2048]{2,1,0:T(8,128)} %fusion.130, f32[8,512]{1,0:T(8,128)S(1)} %dynamic-slice_bitcast_fusion.2, bf16[2048,8,64]{0,2,1:T(8,128)(2,1)S(1)} %get-tuple-element.452, bf16[2048,8,64]{0,2,1:T(8,128)(2,1)} %get-tuple-element.450, ...), kind=kOutput, calls=%fused_computation.20.clone.1 | convolution fusion | flops 1115680768 | bytes 70811648 | tf_op jit(solution)/shard_map/while/body/eval_jaxpr/qhd,khd->hqk/dot_general | solution.py:104
  460.6 28.3 %multiply_convert_fusion.5 = bf16[8,512,2048]{2,1,0:T(8,128)(2,1)} fusion(f32[8,512,2048]{2,1,0:T(8,128)} %get-tuple-element.382, f32[8,512,2048]{2,1,0:T(8,128)} %fusion.130, f32[8,512]{1,0:T(8,128)S(1)} %get-tuple-element.383), kind=kLoop, calls=%fused_computation.19.clone.1 | loop fusion | flops 25165824 | bytes 83902464 | tf_op jit(solution)/shard_map/while/body/eval_jaxpr/convert_element_type | solution.py:153
  568.8 26.3 %multiply_reduce_fusion.2 = (f32[8,512]{1,0:T(8,128)S(1)}, f32[8,512,2048]{2,1,0:T(8,128)}) fusion(f32[8,512,2048]{2,1,0:T(8,128)} %fusion.130, f32[8,512]{1,0:T(8,128)S(1)} %dynamic-slice_bitcast_fusion.2, bf16[2048,8,64]{0,2,1:T(8,128)(2,1)S(1)} %get-tuple-element.452, bf16[2048,8,64]{0,2,1:T(8,128)(2,1)} %get-tuple-element.450, ...), kind=kOutput, calls=%fused_computation.20.clone.1 | convolution fusion | flops 1115680768 | bytes 70811648 | tf_op jit(solution)/shard_map/while/body/eval_jaxpr/qhd,khd->hqk/dot_general | solution.py:104
  595.1 27.4 %multiply_convert_fusion.5 = bf16[8,512,2048]{2,1,0:T(8,128)(2,1)} fusion(f32[8,512,2048]{2,1,0:T(8,128)} %get-tuple-element.382, f32[8,512,2048]{2,1,0:T(8,128)} %fusion.130, f32[8,512]{1,0:T(8,128)S(1)} %get-tuple-element.383), kind=kLoop, calls=%fused_computation.19.clone.1 | loop fusion | flops 25165824 | bytes 83902464 | tf_op jit(solution)/shard_map/while/body/eval_jaxpr/convert_element_type | solution.py:153
  704.7 26.3 %multiply_reduce_fusion.2 = (f32[8,512]{1,0:T(8,128)S(1)}, f32[8,512,2048]{2,1,0:T(8,128)}) fusion(f32[8,512,2048]{2,1,0:T(8,128)} %fusion.130, f32[8,512]{1,0:T(8,128)S(1)} %dynamic-slice_bitcast_fusion.2, bf16[2048,8,64]{0,2,1:T(8,128)(2,1)S(1)} %get-tuple-element.452, bf16[2048,8,64]{0,2,1:T(8,128)(2,1)} %get-tuple-element.450, ...), kind=kOutput, calls=%fused_computation.20.clone.1 | convolution fusion | flops 1115680768 | bytes 70811648 | tf_op jit(solution)/shard_map/while/body/eval_jaxpr/qhd,khd->hqk/dot_general | solution.py:104
  731.0 27.4 %multiply_convert_fusion.5 = bf16[8,512,2048]{2,1,0:T(8,128)(2,1)} fusion(f32[8,512,2048]{2,1,0:T(8,128)} %get-tuple-element.382, f32[8,512,2048]{2,1,0:T(8,128)} %fusion.130, f32[8,512]{1,0:T(8,128)S(1)} %get-tuple-element.383), kind=kLoop, calls=%fused_computation.19.clone.1 | loop fusion | flops 25165824 | bytes 83902464 | tf_op jit(solution)/shard_map/while/body/eval_jaxpr/convert_element_type | solution.py:153
  840.5 26.2 %multiply_reduce_fusion.2 = (f32[8,512]{1,0:T(8,128)S(1)}, f32[8,512,2048]{2,1,0:T(8,128)}) fusion(f32[8,512,2048]{2,1,0:T(8,128)} %fusion.130, f32[8,512]{1,0:T(8,128)S(1)} %dynamic-slice_bitcast_fusion.2, bf16[2048,8,64]{0,2,1:T(8,128)(2,1)S(1)} %get-tuple-element.452, bf16[2048,8,64]{0,2,1:T(8,128)(2,1)} %get-tuple-element.450, ...), kind=kOutput, calls=%fused_computation.20.clone.1 | convolution fusion | flops 1115680768 | bytes 70811648 | tf_op jit(solution)/shard_map/while/body/eval_jaxpr/qhd,khd->hqk/dot_general | solution.py:104
  866.7 27.4 %multiply_convert_fusion.5 = bf16[8,512,2048]{2,1,0:T(8,128)(2,1)} fusion(f32[8,512,2048]{2,1,0:T(8,128)} %get-tuple-element.382, f32[8,512,2048]{2,1,0:T(8,128)} %fusion.130, f32[8,512]{1,0:T(8,128)S(1)} %get-tuple-element.383), kind=kLoop, calls=%fused_computation.19.clone.1 | loop fusion | flops 25165824 | bytes 83902464 | tf_op jit(solution)/shard_map/while/body/eval_jaxpr/convert_element_type | solution.py:153
  1022.4 36.3 %convert_reduce_fusion = (f32[2048]{0:T(1024)}, bf16[2048,2048]{1,0:T(8,128)(2,1)}) fusion(f32[2048,2048]{1,0:T(8,128)} %fusion.69, f32[2048]{0:T(1024)S(1)} %copy-done.26, bf16[2048,2048]{1,0:T(8,128)(2,1)} %all-gather.17.cloned.1.call-done, bf16[2048,2048]{1,0:T(8,128)(2,1)} %all-gather.15.cloned.1.call-done), kind=kOutput, calls=%fused_computation.51 | convolution fusion | flops 17276336128 | bytes 41959424 | tf_op jit(solution)/shard_map/rd,fd->rf/dot_general | solution.py:140
  1058.7 26.4 %bitcast_add_fusion.2 = f32[2048,2048]{1,0:T(8,128)} fusion(f32[2048,2048,1]{1,0,2:T(8,128)} %fusion.62, bf16[2048,2048]{1,0:T(8,128)(2,1)} %get-tuple-element.233, bf16[2048,2048]{1,0:T(8,128)(2,1)} %all-gather.13.cloned.1.call-done), kind=kOutput, calls=%fused_computation.50 | convolution fusion | flops 17184063488 | bytes 50331648 | tf_op jit(solution)/shard_map/rf,df->rd/dot_general | solution.py:183
  1100.6 33.0 %convolution_add_fusion = f32[2048,2048]{1,0:T(8,128)} fusion(f32[2048,2048]{1,0:T(8,128)} %fusion.68, bf16[2048,2048]{1,0:T(8,128)(2,1)} %all-gather.15.cloned.1.call-done, f32[2048,2048]{1,0:T(8,128)} %fusion.69, f32[2048]{0:T(1024)S(1)} %copy-done.26), kind=kOutput, calls=%fused_computation.54 | convolution fusion | flops 17226006528 | bytes 58728448 | tf_op jit(solution)/shard_map/dot_general | solution.py:122
  1164.9 24.6 %fusion.71 = f32[2048,2048]{1,0:T(8,128)} fusion(bf16[2048,2048]{1,0:T(8,128)(2,1)} %all-gather.7.cloned.1.call-done, bf16[2048,2048]{1,0:T(8,128)(2,1)} %get-tuple-element.233), kind=kOutput, calls=%fused_computation.128 | convolution fusion | flops 17179869184 | bytes 33554432 | tf_op jit(solution)/shard_map/rd,rf->df/dot_general | solution.py:196
  1189.5 27.1 %fusion.64 = f32[2048,2048]{1,0:T(8,128)} fusion(bf16[2048,2048]{1,0:T(8,128)(2,1)} %all-gather.17.cloned.1.call-done, f32[2048,2048]{1,0:T(8,128)} %fusion.69, f32[2048]{0:T(1024)S(1)} %copy-done.26), kind=kOutput, calls=%fused_computation.122 | convolution fusion | flops 17221812224 | bytes 41951232 | tf_op jit(solution)/shard_map/rf,rd->fd/dot_general | solution.py:198
  1220.9 38.0 %all-reduce.1 = (f32[3,512]{1,0:T(4,128)}, f32[2048]{0:T(1024)}) all-reduce(f32[3,512]{1,0:T(4,128)S(1)} %convert_reduce_fusion.1, f32[2048]{0:T(1024)S(1)} %copy-done.22), channel_id=1, replica_groups=mesh['dp'=8,'tensor'=4] {'dp'}, use_global_device_ids=true, to_apply=%region_23.24 | all-reduce | flops 3584 | bytes 28672 | tf_op jit(solution)/shard_map/psum | solution.py:194
  1264.5 76.2 %reduce-scatter.7.cloned.1.call-done = f32[512,2048]{1,0:T(8,128)} async-done(((f32[2048,2048]{1,0:T(8,128)}), f32[512,2048]{1,0:T(8,128)}) %reduce-scatter.7.cloned.1.call-update) | async-done | bytes 4194320 | tf_op jit(solution)/shard_map/reduce_scatter | solution.py:125
  1347.8 42.1 %all-reduce = (f32[2048]{0:T(1024)}, f32[2048]{0:T(1024)}, f32[2048]{0:T(1024)S(1)}) all-reduce(f32[2048]{0:T(1024)S(1)} %get-tuple-element.185, f32[2048]{0:T(1024)S(1)} %get-tuple-element.187, f32[2048]{0:T(1024)S(1)} %get-tuple-element.248), channel_id=1, replica_groups=mesh['dp'=8,'tensor'=4] {'dp','tensor'}, use_global_device_ids=true, to_apply=%region_18.19 | all-reduce | flops 6144 | bytes 49152 | tf_op jit(solution)/shard_map/psum | solution.py:191
  1389.9 44.7 %reduce-scatter.13.cloned.1.call-done = f32[512,256]{1,0:T(8,128)} async-done(((f32[512,2048]{1,0:T(8,128)}), f32[512,256]{1,0:T(8,128)}) %reduce-scatter.13.cloned.1.call-update) | async-done | bytes 524304 | tf_op jit(solution)/shard_map/reduce_scatter | solution.py:201
  1434.6 212.0 %reduce-scatter.11.cloned.1.call-done = f32[256,3,512]{2,0,1:T(8,128)} async-done(((f32[2048,3,512]{2,0,1:T(8,128)}), f32[256,3,512]{2,0,1:T(8,128)}) %reduce-scatter.11.cloned.1.call-update) | async-done | bytes 1572880 | tf_op jit(solution)/shard_map/reduce_scatter | solution.py:200
  1646.7 286.7 %reduce-scatter.15.cloned.1.call-done = f32[256,2048]{1,0:T(8,128)} async-done(((f32[2048,2048]{1,0:T(8,128)}), f32[256,2048]{1,0:T(8,128)}) %reduce-scatter.15.cloned.1.call-update) | async-done | bytes 2097168 | tf_op jit(solution)/shard_map/reduce_scatter | solution.py:202
  1933.3 286.0 %reduce-scatter.17.cloned.1.call-done = f32[2048,256]{1,0:T(8,128)} async-done(((f32[2048,2048]{1,0:T(8,128)}), f32[2048,256]{1,0:T(8,128)}) %reduce-scatter.17.cloned.1.call-update) | async-done | bytes 2097168 | tf_op jit(solution)/shard_map/reduce_scatter | solution.py:203
  (217 shorter events, 700.8 us)
Async XLA Ops:
  7.2 106.1 %all-gather.9.cloned.1.call-start = ((), (), s32[]{:S(2)}) async-start(), calls=%async_computation.7 | async-start | bytes 7077888 | tf_op jit(solution)/shard_map/all_gather | solution.py:78
  9.7 162.3 %all-gather.7.cloned.1.call-start = ((), (), s32[]{:S(2)}) async-start(), calls=%async_computation.6 | async-start | bytes 10485760 | tf_op jit(solution)/shard_map/all_gather | solution.py:76
  15.8 386.1 %all-gather.11.cloned.1.call-start = ((), (), s32[]{:S(2)}) async-start(), calls=%async_computation.8 | async-start | bytes 2359296 | tf_op jit(solution)/shard_map/all_gather | solution.py:79
  16.5 385.4 %all-gather.17.cloned.1.call-start = ((), (), s32[]{:S(2)}) async-start(), calls=%async_computation.12 | async-start | bytes 10485760 | tf_op jit(solution)/shard_map/all_gather | solution.py:131
  18.5 153.5 %copy-start.25 = (f32[3,512]{1,0:T(4,128)S(1)}, f32[3,512]{1,0:T(4,128)}, u32[]{:S(2)}) copy-start(f32[3,512]{1,0:T(4,128)} %param.22) | copy-start | bytes 18436
  21.8 976.4 %all-gather.13.cloned.1.call-start = ((), (), s32[]{:S(2)}) async-start(), calls=%async_computation.9 | async-start | bytes 9437184 | tf_op jit(solution)/shard_map/all_gather | solution.py:80
  22.4 999.9 %all-gather.15.cloned.1.call-start = ((), (), s32[]{:S(2)}) async-start(), calls=%async_computation.10 | async-start | bytes 9437184 | tf_op jit(solution)/shard_map/all_gather | solution.py:81
  23.0 1236.0 %reduce-scatter.9.cloned.1.call-start = ((), (), s32[]{:S(2)}) async-start(), calls=%async_computation.13 | async-start | bytes 20971520 | tf_op jit(solution)/shard_map/reduce_scatter | solution.py:186
  26.0 166.8 %copy-start.6 = (f32[2048,16]{0,1:T(8,128)}, f32[2048,16]{0,1:T(8,128)S(1)}, u32[]{:S(2)}) copy-start(f32[2048,16]{0,1:T(8,128)S(1)} %get-tuple-element.257) | copy-start | bytes 393220
  998.2 24.1 %copy-start.26 = (f32[2048]{0:T(1024)S(1)}, f32[2048]{0:T(1024)}, u32[]{:S(2)}) copy-start(f32[2048]{0:T(1024)} %param.26) | copy-start | bytes 24580
  1085.1 255.5 %reduce-scatter.7.cloned.1.call-start = ((), (), s32[]{:S(2)}) async-start(), calls=%async_computation.11 | async-start | bytes 20971520 | tf_op jit(solution)/shard_map/reduce_scatter | solution.py:125
  1133.6 301.0 %reduce-scatter.13.cloned.1.call-start = ((), (), s32[]{:S(2)}) async-start(), calls=%async_computation.15 | async-start | bytes 4718592 | tf_op jit(solution)/shard_map/reduce_scatter | solution.py:201
  1143.2 503.5 %reduce-scatter.11.cloned.1.call-start = ((), (), s32[]{:S(2)}) async-start(), calls=%async_computation.14 | async-start | bytes 14155776 | tf_op jit(solution)/shard_map/reduce_scatter | solution.py:200
  1164.8 768.5 %reduce-scatter.15.cloned.1.call-start = ((), (), s32[]{:S(2)}) async-start(), calls=%async_computation.16 | async-start | bytes 18874368 | tf_op jit(solution)/shard_map/reduce_scatter | solution.py:202
  1189.5 1029.9 %reduce-scatter.17.cloned.1.call-start = ((), (), s32[]{:S(2)}) async-start(), calls=%async_computation.17 | async-start | bytes 18874368 | tf_op jit(solution)/shard_map/reduce_scatter | solution.py:203
  1216.6 42.4 %copy-start.2 = (bf16[512,2048]{1,0:T(8,128)(2,1)S(1)}, bf16[512,2048]{1,0:T(8,128)(2,1)}, u32[]{:S(2)}) copy-start(bf16[512,2048]{1,0:T(8,128)(2,1)} %param.17) | copy-start | bytes 6291460
  1216.6 42.4 %copy-start.10 = (f32[2048]{0:T(1024)S(1)}, f32[2048]{0:T(1024)}, u32[]{:S(2)}) copy-start(f32[2048]{0:T(1024)} %param.19) | copy-start | bytes 24580
  1216.6 42.4 %copy-start.12 = (f32[512]{0:T(512)S(1)}, f32[512]{0:T(512)}, u32[]{:S(2)}) copy-start(f32[512]{0:T(512)} %copy-done.11) | copy-start | bytes 6148
  1220.9 41.4 %copy-start.18 = (f32[512]{0:T(512)S(1)}, f32[512]{0:T(512)}, u32[]{:S(2)}) copy-start(f32[512]{0:T(512)} %copy-done.17) | copy-start | bytes 6148
  1220.9 41.4 %copy-start.14 = (f32[512]{0:T(512)S(1)}, f32[512]{0:T(512)}, u32[]{:S(2)}) copy-start(f32[512]{0:T(512)} %copy-done.13) | copy-start | bytes 6148
  1262.3 78.4 %copy-start.16 = (f32[512]{0:T(512)S(1)}, f32[512]{0:T(512)}, u32[]{:S(2)}) copy-start(f32[512]{0:T(512)} %copy-done.15) | copy-start | bytes 6148
  1262.3 78.4 %copy-start.20 = (f32[2048]{0:T(1024)S(1)}, f32[2048]{0:T(1024)}, u32[]{:S(2)}) copy-start(f32[2048]{0:T(1024)} %param.28) | copy-start | bytes 24580
  1262.3 78.4 %copy-start.21 = (f32[2048]{0:T(1024)S(1)}, f32[2048]{0:T(1024)}, u32[]{:S(2)}) copy-start(f32[2048]{0:T(1024)} %param.24) | copy-start | bytes 24580
  1389.9 830.1 %copy-start.23 = (f32[2048]{0:T(1024)}, f32[2048]{0:T(1024)S(1)}, u32[]{:S(2)}) copy-start(f32[2048]{0:T(1024)S(1)} %get-tuple-element.482) | copy-start | bytes 24580
  (16 other events, 61.8 us)
Sparse Core Ops, SparseCore 0:
  10.7 102.6 all-gather.8
  115.5 56.4 all-gather.6
  174.0 51.1 all-gather.10
  226.6 56.4 all-gather.16
  285.1 125.3 all-gather.12
  412.3 123.5 all-gather.14
  1085.2 126.4 reduce-scatter.8
  1214.5 126.0 reduce-scatter.6
  1344.9 89.7 reduce-scatter.12
  1439.1 207.5 reduce-scatter.10
  1651.5 281.7 reduce-scatter.14
  1937.6 281.7 reduce-scatter.16
where the time goes:
time: 2240 us; the launch traced here: 2230 us
  waiting for transfers between devices  1050 us (47%)
  matrix products  714 us (32%)
  other arithmetic  223 us (10%)
  local copies, waits for them, and re-layouts  125 us (6%)
  blocking collectives  80.1 us (4%)
    reduce_scatter x1, waiting for transfers between devices, local(): lax.psum_scatter(grad_fc1, 'dp', scatter_dimension=0, tiled=True)  287 us
    reduce_scatter x1, waiting for transfers between devices, local(): lax.psum_scatter(grad_fc2, 'dp', scatter_dimension=1, tiled=True)  286 us
    reduce_scatter x1, waiting for transfers between devices, local(): lax.psum_scatter(grad_qkv, 'dp', scatter_dimension=0, tiled=True)  212 us
    dot_general x8, matrix products, scores_for(): jnp.einsum('qhd,khd->hqk', q_blk, key, preferred_element_type=jnp.float32)  167 us
    convert_element_type x4, other arithmetic, backward_block(): grad_scores = (prob * (grad_prob - inner)).astype(jnp.bfloat16)  110 us
    dynamic_update_slice x8, local copies, waits for them, and re-layouts, local(): pieces, log_totals = lax.map(forward_block, starts)  88.3 us
    all_gather x1, waiting for transfers between devices, local(): lax.all_gather(w_qkv, 'dp', axis=0, tiled=True)  87.3 us
    reduce_scatter x1, waiting for transfers between devices, local(): lax.psum_scatter(partial_value, 'tensor', scatter_dimension=0, tiled=True)  76.2 us
  transfers between devices with their start and end apart: 12, of which 7 were waited for; matrix products, arithmetic and copies ran while one was open for 44% of the time, Pallas kernels for 0%

commit v1 on v0

v1 whole, which is shorter than its diff:
```python
import functools
import math

import jax
import jax.numpy as jnp
from jax import lax
from jax.experimental import pallas as pl
from jax.experimental.pallas import tpu as pltpu
from jax.sharding import PartitionSpec as P

HEAD = 64
ROT = 32
EPS = 1e-05
NEG = -1e30
LANES = 128
BF = jnp.bfloat16
F32 = jnp.float32
NT = (((1,), (1,)), ((), ()))
TN = (((0,), (0,)), ((), ()))
VMEM = 56 * 2**20


def swap(x, axis, bit):
    size = lax.axis_size(axis)
    return lax.ppermute(x, axis, [(i, i ^ bit) for i in range(size)])


def up(x, step):
    size = lax.axis_size("dp")
    return lax.ppermute(x, "dp", [(i, i + 2) for i in range(2 * (step - 1), size - 2)])


def down(x, step):
    size = lax.axis_size("dp")
    return lax.ppermute(x, "dp", [(i, i - 2) for i in range(2, size - 2 * (step - 1))])


def pick(x, index):
    return lax.dynamic_index_in_dim(x, index, 0, keepdims=False)


def place(buffer, block, *index):
    return lax.dynamic_update_slice(
        buffer, block.reshape((1,) * len(index) + block.shape), tuple(index) + (0,) * block.ndim
    )


def gather_line(pair, at, places):
    ups, downs = [pair], [pair]
    for step in range(1, places):
        ups.append(up(ups[-1], step))
        downs.append(down(downs[-1], step))
    out = jnp.zeros((places,) + pair.shape, pair.dtype)
    out = place(out, pair, at)
    for j in range(1, places):
        block = jnp.where(at + j < places, downs[j], ups[places - j])
        out = place(out, block, lax.rem(at + j, places))
    return out


def reduce_line(parts, places):
    add = lambda a, b: (a.astype(F32) + b.astype(F32)).astype(BF)
    going_up, going_down = parts[places - 1], parts[1]
    for distance in range(places - 1, 0, -1):
        size = lax.axis_size("dp")
        got_up = lax.ppermute(
            going_up, "dp", [(i, i + 2) for i in range(0, size - 2 * distance)]
        )
        got_down = lax.ppermute(
            going_down, "dp", [(i, i - 2) for i in range(2 * distance, size)]
        )
        if distance > 1:
            going_up = add(parts[distance - 1], got_up)
            going_down = add(parts[places - distance + 1], got_down)
    return parts[0].astype(F32) + got_up.astype(F32) + got_down.astype(F32)


def lanes_of(shape):
    return lax.broadcasted_iota(jnp.int32, shape, 1)


def turn(x, cosine, sine):
    lane = lanes_of(x.shape) % HEAD
    other = jnp.where(lane < ROT // 2, pltpu.roll(x, LANES - ROT // 2, 1), pltpu.roll(x, ROT // 2, 1))
    return x * cosine + other * sine


def qkv_kernel(pairs, h_ref, w_ref, b_ref, cos_ref, sin_ref, out_ref):
    acc = jnp.dot(h_ref[...], w_ref[...], preferred_element_type=F32) + b_ref[...]
    cosine, sine = cos_ref[...], sin_ref[...]
    for j in range(pairs):
        at = 3 * LANES * j
        q = turn(acc[:, at : at + LANES], cosine, sine).astype(BF)
        out_ref[:, at : at + LANES] = (q.astype(F32) * HEAD**-0.5).astype(BF)
        out_ref[:, at + LANES : at + 2 * LANES] = turn(
            acc[:, at + LANES : at + 2 * LANES], cosine, sine
        ).astype(BF)
        out_ref[:, at + 2 * LANES : at + 3 * LANES] = acc[:, at + 2 * LANES : at + 3 * LANES].astype(BF)


def qkv_call(h, w, bias, cosine, sine, block=512):
    rows, depth = h.shape
    columns = w.shape[1]
    return pl.pallas_call(
        functools.partial(qkv_kernel, columns // (3 * LANES)),
        grid=(rows // block,),
        in_specs=[
            pl.BlockSpec((block, depth), lambda i: (i, 0)),
            pl.BlockSpec((depth, columns), lambda i: (0, 0)),
            pl.BlockSpec((1, columns), lambda i: (0, 0)),
            pl.BlockSpec((block, LANES), lambda i: (i, 0)),
            pl.BlockSpec((block, LANES), lambda i: (i, 0)),
        ],
        out_specs=pl.BlockSpec((block, columns), lambda i: (i, 0)),
        out_shape=jax.ShapeDtypeStruct((rows, columns), BF),
        compiler_params=pltpu.CompilerParams(vmem_limit_bytes=VMEM),
        cost_estimate=pl.CostEstimate(
            flops=2 * rows * depth * columns, bytes_accessed=2 * rows * depth, transcendentals=0
        ),
    )(h, w, bias, cosine, sine)


def attend_kernel(rows, block, qkv_ref, aq_ref, ak_ref, o_ref, lse_ref):
    lane = lanes_of((rows, LANES))
    lane_q = lanes_of((block, LANES))
    one = jnp.where(lane % HEAD < 3, 1.0, 0.0).astype(BF)
    first = lane < HEAD
    keys = [jnp.where(half, qkv_ref[:, LANES : 2 * LANES], ak_ref[...]) for half in (first, ~first)]
    values = [jnp.where(half, qkv_ref[:, 2 * LANES :], one) for half in (first, ~first)]
    causal = lanes_of((block, block)) <= lax.broadcasted_iota(jnp.int32, (block, block), 0)
    for b in range(rows // block):
        here = pl.ds(b * block, block)
        lo, hi = b * block, (b + 1) * block
        outs, sums = [], []
        for side in (0, 1):
            half = (lane_q < HEAD) if side == 0 else (lane_q >= HEAD)
            q = jnp.where(half, qkv_ref[here, :LANES], aq_ref[here])
            s_near = lax.dot_general(q, keys[side][lo:hi], NT, preferred_element_type=F32)
            s_near = jnp.where(causal, s_near, NEG)
            top = jnp.max(s_near, axis=1, keepdims=True)
            if b:
                s_far = lax.dot_general(q, keys[side][:lo], NT, preferred_element_type=F32)
                top = jnp.maximum(top, jnp.max(s_far, axis=1, keepdims=True))
            o = jnp.dot(jnp.exp(s_near - top).astype(BF), values[side][lo:hi], preferred_element_type=F32)
            if b:
                o = o + jnp.dot(
                    jnp.exp(s_far - top).astype(BF), values[side][:lo], preferred_element_type=F32
                )
            at = HEAD if side == 0 else 0
            total = o[:, at : at + 1]
            outs.append(o / total)
            sums.append(top + jnp.log(total))
        o_ref[here] = jnp.where(lane_q < HEAD, outs[0], outs[1])
        lse_ref[here] = jnp.where(lane_q < HEAD, sums[0], sums[1])


def attend_cost(groups, pairs, rows, products):
    pairs_of = groups * pairs * 2 * rows * rows
    return pl.CostEstimate(
        flops=products * pairs_of * 256, bytes_accessed=groups * pairs * rows * 4096, transcendentals=pairs_of // 2
    )


def attend_call(qkv, aq, ak, rows, block=512):
    groups, pairs = qkv.shape[0] // rows, qkv.shape[1] // (3 * LANES)
    wide = pl.BlockSpec((rows, 3 * LANES), lambda g, j: (g, j))
    one = pl.BlockSpec((rows, LANES), lambda g, j: (g, j))
    aug = pl.BlockSpec((rows, LANES), lambda g, j: (g, 0))
    shape = jax.ShapeDtypeStruct((groups * rows, pairs * LANES), F32)
    return pl.pallas_call(
        functools.partial(attend_kernel, rows, block),
        grid=(groups, pairs),
        in_specs=[wide, aug, aug],
        out_specs=[one, one],
        out_shape=[shape, shape],
        compiler_params=pltpu.CompilerParams(vmem_limit_bytes=VMEM),
        cost_estimate=attend_cost(groups, pairs, rows, 2),
    )(qkv, aq, ak)


def split3(x):
    a = x.astype(BF).astype(F32)
    b = (x - a).astype(BF).astype(F32)
    return a, b, x - a - b


def attend_back_kernel(
    rows, block, qkv_ref, aq_ref, ak_ref, o_ref, lse_ref, go_ref, cos_ref, sin_ref, out_ref, dk_s, dv_s, dqt_s
):
    lane = lanes_of((rows, LANES))
    lane_k = lanes_of((block, LANES))
    one = jnp.where(lane % HEAD < 3, 1.0, 0.0).astype(BF)
    causal = lax.broadcasted_iota(jnp.int32, (block, block), 0) <= lanes_of((block, block))
    prod = o_ref[...] * go_ref[...].astype(F32)
    dq_first = None
    for side in (0, 1):
        half = (lane < HEAD) if side == 0 else (lane >= HEAD)
        delta = -jnp.sum(jnp.where(half, prod, 0.0), axis=1, keepdims=True)
        at = 0 if side == 0 else HEAD
        lse = -lse_ref[:, at : at + 1]
        q = jnp.where(half, qkv_ref[:, :LANES], aq_ref[...]).astype(F32)
        g = jnp.where(half, go_ref[...].astype(F32), 0.0)
        base = HEAD - at
        for i, (a, d) in enumerate(zip(split3(lse), split3(delta))):
            q = jnp.where(lane == base + 8 + i, a, q)
            g = jnp.where(lane == base + i, d, g)
        q, g = q.astype(BF), g.astype(BF)
        k = jnp.where(half, qkv_ref[:, LANES : 2 * LANES], ak_ref[...])
        v = jnp.where(half, qkv_ref[:, 2 * LANES :], one)
        kt = k.T
        for b in range(rows // block):
            lo, hi = b * block, (b + 1) * block
            here = pl.ds(lo, block)
            st = lax.dot_general(k[lo:hi], q[lo:], NT, preferred_element_type=F32)
            dpt = lax.dot_general(v[lo:hi], g[lo:], NT, preferred_element_type=F32)
            p = jnp.exp(st)
            near = jnp.where(causal, p[:, :block], 0.0)
            p = jnp.concatenate([near, p[:, block:]], axis=1) if hi < rows else near
            ds = (p * dpt).astype(BF)
            dv = jnp.dot(p.astype(BF), g[lo:], preferred_element_type=F32)
            dk = jnp.dot(ds, q[lo:], preferred_element_type=F32)
            dq = jnp.dot(kt[:, lo:hi], ds, preferred_element_type=F32)
            if side == 0:
                dk_s[here] = dk
                dv_s[here] = dv
            else:
                dk = jnp.where(lane_k < HEAD, dk_s[here], dk)
                dv = jnp.where(lane_k < HEAD, dv_s[here], dv)
                out_ref[here, LANES : 2 * LANES] = turn(dk, cos_ref[here], -sin_ref[here]).astype(BF)
                out_ref[here, 2 * LANES :] = dv.astype(BF)
            if b == 0:
                dqt_s[...] = dq
            else:
                dqt_s[:, lo:] += dq
        d = dqt_s[...].T * HEAD**-0.5
        if side == 0:
            dq_first = d
        else:
            d = jnp.where(lane < HEAD, dq_first, d)
            out_ref[:, :LANES] = turn(d, cos_ref[...], -sin_ref[...]).astype(BF)


def attend_back_call(qkv, aq, ak, o, lse, go, cosine, sine, rows, block=256):
    groups, pairs = qkv.shape[0] // rows, qkv.shape[1] // (3 * LANES)
    wide = pl.BlockSpec((rows, 3 * LANES), lambda g, j: (g, j))
    one = pl.BlockSpec((rows, LANES), lambda g, j: (g, j))
    aug = pl.BlockSpec((rows, LANES), lambda g, j: (g, 0))
    return pl.pallas_call(
        functools.partial(attend_back_kernel, rows, block),
        grid=(groups, pairs),
        in_specs=[wide, aug, aug, one, one, one, aug, aug],
        out_specs=wide,
        out_shape=jax.ShapeDtypeStruct(qkv.shape, BF),
        scratch_shapes=[
            pltpu.VMEM((rows, LANES), F32),
            pltpu.VMEM((rows, LANES), F32),
            pltpu.VMEM((LANES, rows), F32),
        ],
        compiler_params=pltpu.CompilerParams(vmem_limit_bytes=VMEM),
        cost_estimate=attend_cost(groups, pairs, rows, 5),
    )(qkv, aq, ak, o, lse, go, cosine, sine)


def rows_kernel(terms, added, dtype, index_ref, *refs):
    ins, out_ref = refs[:-1], refs[-1]
    acc = lax.dot_general(ins[0][...], ins[1][...], NT, preferred_element_type=F32)
    for i in range(1, terms):
        acc = acc + lax.dot_general(ins[2 * i][...], ins[2 * i + 1][...], NT, preferred_element_type=F32)
    for i in range(added):
        acc = acc + ins[2 * terms + i][...].astype(F32)
    out_ref[...] = acc.astype(dtype)


def rows_call(index, count, factors, part, parts, added, block, dtype):
    columns = factors[0][1].shape[0] // parts
    in_specs, args = [], []
    flops = 0
    for a, b in factors:
        depth = a.shape[1]
        in_specs.append(pl.BlockSpec((block, depth), lambda i, index: (index[i], 0)))
        in_specs.append(pl.BlockSpec((columns, depth), lambda i, index: (part, 0)))
        args += [a, b]
        flops += 2 * count * block * columns * depth
    for a in added:
        in_specs.append(pl.BlockSpec((block, columns), lambda i, index: (i, 0)))
        args.append(a)
    return pl.pallas_call(
        functools.partial(rows_kernel, len(factors), len(added), dtype),
        grid_spec=pltpu.PrefetchScalarGridSpec(
            num_scalar_prefetch=1,
            grid=(count,),
            in_specs=in_specs,
            out_specs=pl.BlockSpec((block, columns), lambda i, index: (i, 0)),
        ),
        out_shape=jax.ShapeDtypeStruct((count * block, columns), dtype),
        compiler_params=pltpu.CompilerParams(vmem_limit_bytes=VMEM),
        cost_estimate=pl.CostEstimate(flops=flops, bytes_accessed=4 * count * block * columns, transcendentals=0),
    )(index, *args)


def gelu_slope(z):
    c = math.sqrt(2.0 / math.pi)
    t = jnp.tanh(c * (z + 0.044715 * z * z * z))
    return 0.5 * (1.0 + t) + 0.5 * z * (1.0 - t * t) * c * (1.0 + 3.0 * 0.044715 * z * z)


def local(
    layer_input,
    seq_lens,
    ln_gain,
    ln_bias,
    w_qkv,
    b_qkv,
    w_dense,
    b_dense,
    w_fc1,
    b_fc1,
    w_fc2,
    b_fc2,
    cotangent,
):
    own, width = layer_input.shape
    ndp, nt = lax.axis_size("dp"), lax.axis_size("tensor")
    dp, t = lax.axis_index("dp"), lax.axis_index("tensor")
    half, at, places = dp % 2, dp // 2, ndp // 2
    chip, core = t // 2, t % 2
    group = own * nt
    shard = w_qkv.shape[0]
    q_width = w_qkv.shape[2] // 2
    f_width = w_fc1.shape[1] // 2
    pairs = q_width // LANES
    other = 1 - half

    wq = w_qkv.reshape(shard, 3, 2, pairs, LANES).transpose(2, 0, 3, 1, 4).reshape(2, shard, 3 * q_width)
    wd = w_dense.T.reshape(shard, 2, q_width).transpose(1, 0, 2)
    w1 = w_fc1.reshape(shard, 2, f_width).transpose(1, 0, 2)
    w2 = w_fc2.T.reshape(shard, 2, f_width).transpose(1, 0, 2)

    def gather_weight(w):
        theirs = swap(pick(w, other), "dp", 1)
        pair = jnp.zeros((2, shard, w.shape[2]), BF)
        pair = place(place(pair, pick(w, half), half), theirs, other)
        full = gather_line(pair.reshape(2 * shard, w.shape[2]), at, places)
        return full.reshape(width, w.shape[2])

    def gather_rows(a):
        mid = own // 2
        a_x = swap(a, "tensor", 2)
        a_y = swap(a, "dp", 1)
        a_c = swap(a, "tensor", 1)
        a_yx = jnp.concatenate([swap(a_x[:mid], "dp", 1), swap(a_y[mid:], "tensor", 2)], axis=0)
        out = jnp.zeros((2, nt, own, width), a.dtype)
        for block, g, x in ((a, half, chip), (a_x, half, 1 - chip), (a_y, other, chip), (a_yx, other, 1 - chip)):
            out = place(out, block, g, 2 * x + core)
            out = place(out, a_c if block is a else swap(block, "tensor", 1), g, 2 * x + 1 - core)
        return out.reshape(2 * group, width)

    xf = layer_input.astype(F32)
    mean = jnp.mean(xf, axis=1, keepdims=True)
    centred = xf - mean
    rstd = lax.rsqrt(jnp.mean(centred * centred, axis=1, keepdims=True) + EPS)
    x_hat = centred * rstd
    h_own = (x_hat * ln_gain + ln_bias).astype(BF)
    used = jnp.sum(seq_lens[0])
    valid = (t * own + jnp.arange(own, dtype=jnp.int32) < used).astype(F32)[:, None]
    gy = cotangent.astype(F32) * valid
    gb_own = gy.astype(BF)

    wq_all = gather_weight(wq)
    h = gather_rows(h_own)
    wd_all = gather_weight(wd)
    gb = gather_rows(gb_own)
    w1_all = gather_weight(w1)
    w2_all = gather_weight(w2)

    lens = jnp.zeros((2, seq_lens.shape[1]), jnp.int32)
    lens = place(place(lens, seq_lens[0], half), swap(seq_lens, "dp", 1)[0], other)
    ends = jnp.cumsum(lens, axis=1)
    rows = jnp.arange(group, dtype=jnp.int32)
    segment = jnp.sum((rows[None, :, None] >= ends[:, None, :]).astype(jnp.int32), axis=2)
    begins = jnp.concatenate([ends - lens, ends[:, -1:]], axis=1)
    labels = jnp.arange(begins.shape[1], dtype=jnp.int32)
    mine = segment[:, :, None] == labels
    position = rows[None] - jnp.sum(jnp.where(mine, begins[:, None, :], 0), axis=2)
    steps = jnp.arange(ROT // 2, dtype=F32)
    inverse = jnp.exp(-math.log(10000.0) * 2.0 * steps / ROT)
    angle = inverse[:, None] * position.reshape(1, 2 * group).astype(F32)
    cos16, sin16 = jnp.cos(angle).T, jnp.sin(angle).T
    still = jnp.zeros((2 * group, HEAD - ROT), F32)
    cosine = jnp.concatenate([cos16, cos16, still + 1.0] * 2, axis=1)
    sine = jnp.concatenate([-sin16, sin16, still] * 2, axis=1)
    lane = jnp.arange(LANES, dtype=jnp.int32) % HEAD
    same = segment.reshape(2 * group, 1) == lane[None, :]
    count = begins.shape[1]
    aq = jnp.where(same & (lane < count), NEG, 0.0).astype(BF)
    ak = jnp.where(~same & (lane < count) | (lane >= 8) & (lane < 11), 1.0, 0.0).astype(BF)

    bias_q = pick(b_qkv.reshape(3, 2, pairs, LANES).transpose(1, 2, 0, 3), half).reshape(1, 3 * q_width)
    bias_1 = pick(b_fc1.reshape(2, f_width), half)[None]

    qkv = qkv_call(h, wq_all, bias_q, cosine, sine)
    o_float, lse = attend_call(qkv, aq, ak, group)
    o = o_float.astype(BF)
    go = jnp.dot(gb, wd_all, preferred_element_type=F32).astype(BF)
    z = jnp.dot(h, w1_all, preferred_element_type=F32) + bias_1
    act = jax.nn.gelu(z, approximate=True).astype(BF)

    block = 2 * shard

    def reduce_weight(left, right):
        parts = []
        for j in range(places):
            columns = lax.dynamic_slice_in_dim(left, lax.rem(at + j, places) * block, block, 1)
            parts.append(lax.dot_general(columns, right, TN, preferred_element_type=F32))
        parts = parts[:1] + [x.astype(BF) for x in parts[1:]]
        total = reduce_line(parts, places).reshape(2, shard, right.shape[1])
        theirs = swap(pick(total, other).astype(BF), "dp", 1).astype(F32)
        out = jnp.zeros(total.shape, F32)
        return place(place(out, pick(total, half), half), theirs, other)

    g_wd = reduce_weight(gb, o)
    g_w2 = reduce_weight(gb, act)
    slope = gelu_slope(z)
    gz_float = jnp.dot(gb, w2_all, preferred_element_type=F32) * slope
    gz = gz_float.astype(BF)
    g_w1 = reduce_weight(h, gz)

    def scatter_rows(factors):
        size = own
        name = lambda g, x, c: g * nt + 2 * x + c

        def blocks(*names):
            return jnp.stack([jnp.asarray(n, jnp.int32) for n in names])

        outs = []
        for part in (0, 1):
            call = lambda index, n, added, dtype=BF: rows_call(index, n, factors, part, 2, added, size, dtype)
            p0, p1 = half, other
            x0, x1 = chip, 1 - chip
            order = [(p1, x1), (p1, x0), (p0, x1), (p0, x0)]
            if part == 1:
                order = [(p1, x1), (p0, x1), (p1, x0), (p0, x0)]
            given = call(blocks(*[name(g, x, 1 - core) for g, x in order]), 4, [])
            got = swap(given, "tensor", 1)
            mine = [name(g, x, core) for g, x in order]
            axes = (("dp", 1), ("tensor", 2)) if part == 0 else (("tensor", 2), ("dp", 1))
            given = call(blocks(*mine[:2]), 2, [got[: 2 * size]])
            got_1 = swap(given, *axes[0])
            given = call(blocks(mine[2]), 1, [got[2 * size : 3 * size], got_1[:size]])
            got_2 = swap(given, *axes[1])
            outs.append(call(blocks(mine[3]), 1, [got[3 * size :], got_1[size:], got_2], F32))
        return jnp.concatenate(outs, axis=1)

    branch = scatter_rows([(act, w2_all), (o, wd_all)])
    output = (xf + branch + b_dense + b_fc2).astype(BF)

    da = attend_back_call(qkv, aq, ak, o_float, lse, go, cosine, sine, group)
    dn = scatter_rows([(gz, w1_all), (da, wq_all)])
    g_wq = reduce_weight(h, da)

    scaled = dn * ln_gain
    m1 = jnp.mean(scaled, axis=1, keepdims=True)
    m2 = jnp.mean(scaled * x_hat, axis=1, keepdims=True)
    grad_x = rstd * (scaled - m1 - x_hat * m2) + gy

    def everywhere(x, axes):
        for axis in axes:
            bit = 1
            while bit < lax.axis_size(axis):
                x = x + swap(x, axis, bit)
                bit *= 2
        return x

    def both_halves(x):
        bit = 2
        while bit < ndp:
            x = x + swap(x, "dp", bit)
            bit *= 2
        out = jnp.zeros((2,) + x.shape, F32)
        return place(place(out, x, half), swap(x, "dp", 1), other)

    early = everywhere(jnp.sum(gy, axis=0, keepdims=True), ("tensor", "dp"))[0]
    late = jnp.stack([jnp.sum(dn * x_hat, axis=0), jnp.sum(dn, axis=0)])
    late = everywhere(late, ("tensor", "dp"))
    g_b1 = both_halves(jnp.sum(gz, axis=0, dtype=F32, keepdims=True)).reshape(2 * f_width)
    g_bq = both_halves(jnp.sum(da, axis=0, dtype=F32, keepdims=True))
    g_bq = g_bq.reshape(2, pairs, 3, LANES).transpose(2, 0, 1, 3).reshape(3, 2 * q_width)

    out_wq = g_wq.reshape(2, shard, pairs, 3, LANES).transpose(1, 3, 0, 2, 4).reshape(shard, 3, 2 * q_width)
    out_wd = g_wd.transpose(0, 2, 1).reshape(2 * q_width, shard)
    out_w1 = g_w1.transpose(1, 0, 2).reshape(shard, 2 * f_width)
    out_w2 = g_w2.transpose(0, 2, 1).reshape(2 * f_width, shard)
    return (
        output,
        grad_x,
        late[0],
        late[1],
        out_wq,
        g_bq,
        out_wd,
        early,
        out_w1,
        g_b1,
        out_w2,
        early,
    )


def solution(mesh):
    rows = P(("dp", "tensor"), None)
    in_specs = (
        rows,
        P("dp", None),
        P(),
        P(),
        P("dp", None, "tensor"),
        P(None, "tensor"),
        P("tensor", "dp"),
        P(),
        P("dp", "tensor"),
        P("tensor"),
        P("tensor", "dp"),
        P(),
        rows,
    )
    out_specs = (
        rows,
        rows,
        P(),
        P(),
        P("dp", None, "tensor"),
        P(None, "tensor"),
        P("tensor", "dp"),
        P(),
        P("dp", "tensor"),
        P("tensor"),
        P("tensor", "dp"),
        P(),
    )
    return jax.shard_map(local, mesh=mesh, in_specs=in_specs, out_specs=out_specs, check_vma=False)
```

time: 2240 us -> 1180 us (0.53)
  waiting for transfers between devices: 1050 us -> 358 us
  matrix products: 714 us -> 182 us
  Pallas kernels: 0 us -> 240 us
  starting transfers between devices: 0.49 us -> 154 us
  other arithmetic: 223 us -> 71 us
  blocking collectives: 80.1 us -> 0 us
  local copies, waits for them, and re-layouts: 125 us -> 159 us
    reduce_scatter x6 -> x0, waiting for transfers between devices: 906 us -> none  [the longest x1 287 us: local(): lax.psum_scatter(grad_fc1, 'dp', scatter_dimension=0, tiled=True)]
    dot_general x40 -> x19, matrix products: 714 us -> 182 us  [the longest x16 113 us: reduce_weight(): lax.dot_general(columns, right, TN, preferred_element_type=F32)]
    ppermute x0 -> x101, waiting for transfers between devices: none -> 358 us  [the longest x53 167 us: swap(): return lax.ppermute(x, axis, [(i, i ^ bit) for i in range(size)])]
    pallas_call x0 -> x19, Pallas kernels: none -> 240 us  [the longest x16 130 us: rows_call(): pl.pallas_call(functools.partial(rows_kernel, len(factors), len(added), d...]
    ppermute x0 -> x101, starting transfers between devices: none -> 154 us  [the longest x12 59.1 us: reduce_line(): lax.ppermute(going_up, 'dp', [(i, i + 2) for i in range(0, size - 2 * dis...]
    all_gather x6 -> x0, waiting for transfers between devices: 146 us -> none  [the longest x1 87.3 us: local(): lax.all_gather(w_qkv, 'dp', axis=0, tiled=True)]
    convert_element_type x8 -> x11, other arithmetic: 117 us -> 19.4 us  [the longest x8 13.2 us: reduce_line(): add = lambda a, b: (a.astype(F32) + b.astype(F32)).astype(BF)]
    psum x2 -> x0, blocking collectives: 80.1 us -> none  [the longest x1 42.1 us: local(): lax.psum((grad_gain, grad_shift, grad_out_sum), ('dp', 'tensor'))]
  transfers between devices with their start and end apart: 12 -> 101, of which waited for: 7 -> 33; matrix products, arithmetic and copies ran while one was open for 44% -> 22% of each run, Pallas kernels for 0% -> 15%
where the time goes in v1:
time: 1180 us; the launch traced here: 1170 us
  waiting for transfers between devices  358 us (30%)
  Pallas kernels  240 us (20%)
  matrix products  182 us (15%)
  local copies, waits for them, and re-layouts  159 us (13%)
  starting transfers between devices  154 us (13%)
  other arithmetic  71 us (6%)
    ppermute x53, waiting for transfers between devices, swap(): return lax.ppermute(x, axis, [(i, i ^ bit) for i in range(size)])  167 us
    pallas_call x16, Pallas kernels, rows_call(): pl.pallas_call(functools.partial(rows_kernel, len(factors), len(added), d...  130 us
    dot_general x16, matrix products, reduce_weight(): lax.dot_general(columns, right, TN, preferred_element_type=F32)  113 us
    ppermute x12, waiting for transfers between devices, down(): lax.ppermute(x, 'dp', [(i, i - 2) for i in range(2, size - 2 * (step - 1))])  111 us
    ppermute x12, waiting for transfers between devices, reduce_line(): lax.ppermute(going_up, 'dp', [(i, i + 2) for i in range(0, size - 2 * dis...  70 us
    ppermute x12, starting transfers between devices, reduce_line(): lax.ppermute(going_up, 'dp', [(i, i + 2) for i in range(0, size - 2 * dis...  59.1 us
    pallas_call x1, Pallas kernels, attend_back_call(): pl.pallas_call(functools.partial(attend_back_kernel, rows, block), grid=(...  57.3 us
    dynamic_update_slice x38, local copies, waits for them, and re-layouts, place(): lax.dynamic_update_slice(buffer, block.reshape((1,) * len(index) + block....  49.4 us
  transfers between devices with their start and end apart: 101, of which 33 were waited for; matrix products, arithmetic and copies ran while one was open for 22% of the time, Pallas kernels for 15%

profile of v1, /device:TPU:0, one launch (start us, length us, event | category | flops | bytes accessed | tf_op | source)
XLA Modules:
  0.0 1167.9 jit_solution(16577586940390493068)
XLA Ops:
  88.4 12.4 %collective-permute-done.36 = bf16[512,256]{1,0:T(8,128)(2,1)S(1)} collective-permute-done((bf16[512,256]{1,0:T(8,128)(2,1)S(1)}, bf16[512,256]{1,0:T(8,128)(2,1)S(1)}, u32[]{:S(2)}, u32[]{:S(2)}) %collective-permute-start.36) | collective-permute-done | bytes 262176 | tf_op jit(solution)/shard_map/ppermute | solution.py:35
  127.3 16.4 %collective-permute-done.16 = bf16[512,1024]{1,0:T(8,128)(2,1)S(1)} collective-permute-done((bf16[512,1024]{1,0:T(8,128)(2,1)}, bf16[512,1024]{1,0:T(8,128)(2,1)S(1)}, u32[]{:S(2)}, u32[]{:S(2)}) %collective-permute-start.16) | collective-permute-done | bytes 1048608 | tf_op jit(solution)/shard_map/ppermute | solution.py:35
  182.9 34.3 %collective-permute-done.1 = bf16[512,2048]{1,0:T(8,128)(2,1)S(1)} collective-permute-done((bf16[512,2048]{1,0:T(8,128)(2,1)}, bf16[512,2048]{1,0:T(8,128)(2,1)S(1)}, u32[]{:S(2)}, u32[]{:S(2)}) %collective-permute-start.1) | collective-permute-done | bytes 2097184 | tf_op jit(solution)/shard_map/ppermute | solution.py:25
  217.9 41.2 %collective-permute-done.44 = bf16[512,2048]{1,0:T(8,128)(2,1)S(1)} collective-permute-done((bf16[512,2048]{1,0:T(8,128)(2,1)}, bf16[512,2048]{1,0:T(8,128)(2,1)S(1)}, u32[]{:S(2)}, u32[]{:S(2)}) %collective-permute-start.44) | collective-permute-done | bytes 2097184 | tf_op jit(solution)/shard_map/ppermute | solution.py:25
  291.4 16.9 %collective-permute-done.48 = bf16[256,2048]{1,0:T(8,128)(2,1)S(1)} collective-permute-done((bf16[256,2048]{1,0:T(8,128)(2,1)S(1)}, bf16[256,2048]{1,0:T(8,128)(2,1)S(1)}, u32[]{:S(2)}, u32[]{:S(2)}) %collective-permute-start.48) | collective-permute-done | bytes 1048608 | tf_op jit(solution)/shard_map/ppermute | solution.py:25
  314.1 16.2 %collective-permute-done.20 = bf16[512,1024]{1,0:T(8,128)(2,1)S(1)} collective-permute-done((bf16[512,1024]{1,0:T(8,128)(2,1)S(1)}, bf16[512,1024]{1,0:T(8,128)(2,1)S(1)}, u32[]{:S(2)}, u32[]{:S(2)}) %collective-permute-start.20) | collective-permute-done | bytes 1048608 | tf_op jit(solution)/shard_map/ppermute | solution.py:35
  334.8 23.5 %collective-permute-done.14 = bf16[512,1024]{1,0:T(8,128)(2,1)S(1)} collective-permute-done((bf16[512,1024]{1,0:T(8,128)(2,1)S(1)}, bf16[512,1024]{1,0:T(8,128)(2,1)S(1)}, u32[]{:S(2)}, u32[]{:S(2)}) %collective-permute-start.14) | collective-permute-done | bytes 1048608 | tf_op jit(solution)/shard_map/ppermute | solution.py:35
  358.8 16.1 %collective-permute-done.21 = bf16[512,1024]{1,0:T(8,128)(2,1)S(1)} collective-permute-done((bf16[512,1024]{1,0:T(8,128)(2,1)S(1)}, bf16[512,1024]{1,0:T(8,128)(2,1)S(1)}, u32[]{:S(2)}, u32[]{:S(2)}) %collective-permute-start.21) | collective-permute-done | bytes 1048608 | tf_op jit(solution)/shard_map/ppermute | solution.py:35
  391.4 20.3 %shard_map.220.qkv_ref = bf16[4096,768]{1,0:T(8,128)(2,1)} custom-call(bf16[4096,2048]{1,0:T(8,128)(2,1)} %bitcast.9.h_ref, bf16[2048,768]{1,0:T(8,128)(2,1)} %bitcast.226, f32[1,768]{1,0:T(1,128)} %reshape.375.b_ref, f32[4096,128]{1,0:T(8,128)} %concatenate.23.cos_ref, f32[4096,128]{1,0:T(8,128)} %concatenate.24.sin_ref), custom_call_target="tpu_custom_call" | custom-call | flops 12884901888 | bytes 16777216 | tf_op jit(solution)/shard_map/pallas_call | solution.py:104
  411.7 33.2 %shard_map.221 = (f32[4096,256]{1,0:T(8,128)}, f32[4096,256]{1,0:T(8,128)}) custom-call(bf16[4096,768]{1,0:T(8,128)(2,1)} %shard_map.220.qkv_ref, bf16[4096,128]{1,0:T(8,128)(2,1)} %get-tuple-element.110.aq_ref, bf16[4096,128]{1,0:T(8,128)(2,1)} %get-tuple-element.109.ak_ref), custom_call_target="tpu_custom_call" | custom-call | flops 17179869184 | bytes 33554432 | tf_op jit(solution)/shard_map/pallas_call | solution.py:170
  461.0 57.3 %shard_map.230.refs_2_ = bf16[4096,768]{1,0:T(8,128)(2,1)} custom-call(bf16[4096,768]{1,0:T(8,128)(2,1)} %shard_map.220.qkv_ref, bf16[4096,128]{1,0:T(8,128)(2,1)} %get-tuple-element.110.aq_ref, bf16[4096,128]{1,0:T(8,128)(2,1)} %get-tuple-element.109.ak_ref, f32[4096,256]{1,0:T(8,128)} %get-tuple-element.14.o_ref, f32[4096,256]{1,0:T(8,128)} %get-tuple-element.15.lse_ref, ...), custom_call_target="tpu_custom_call" | custom-call | flops 42949672960 | bytes 33554432 | tf_op jit(solution)/shard_map/pallas_call | solution.py:248
  543.7 25.7 %fusion.7 = (bf16[4096,1024]{1,0:T(8,128)(2,1)S(1)}, f32[4096,1024]{1,0:T(8,128)}) fusion(f32[1024]{0:T(1024)S(1)} %bitcast.285, bf16[4096,2048]{1,0:T(8,128)(2,1)} %bitcast.9.h_ref, bf16[2048,1024]{1,0:T(8,128)(2,1)S(1)} %bitcast.217), kind=kOutput, calls=%fused_computation.10 | convolution fusion | flops 17221812224 | bytes 46141440 | tf_op jit(solution)/shard_map/dot_general | solution.py:405
  569.4 10.8 fusion.89
  602.9 34.3 %convert_reduce_fusion = (f32[1024]{0:T(1024)S(1)}, bf16[4096,1024]{1,0:T(8,128)(2,1)}) fusion(f32[4096,1024]{1,0:T(8,128)} %get-tuple-element.117, f32[1024]{0:T(1024)S(1)} %bitcast.286, bf16[4096,2048]{1,0:T(8,128)(2,1)} %bitcast.73, bf16[2048,1024]{1,0:T(8,128)(2,1)S(1)} %bitcast.214), kind=kOutput, calls=%fused_computation.18 | convolution fusion | flops 17272143872 | bytes 46145536 | tf_op jit(solution)/shard_map/dot_general | solution.py:424
  654.4 12.9 %shard_map.235 = bf16[2048,1024]{1,0:T(8,128)(2,1)} custom-call(s32[4]{0:T(128)} %add_add_fusion.1.index_ref, bf16[4096,1024]{1,0:T(8,128)(2,1)} %get-tuple-element.119.refs_0_, bf16[2048,1024]{1,0:T(8,128)(2,1)} %bitcast.218, bf16[4096,768]{1,0:T(8,128)(2,1)} %shard_map.230.refs_2_, bf16[2048,768]{1,0:T(8,128)(2,1)} %bitcast.227), custom_call_target="tpu_custom_call" | custom-call | flops 7516192768 | bytes 8388608 | tf_op jit(solution)/shard_map/pallas_call | solution.py:287
  672.0 12.8 %shard_map.231 = bf16[2048,1024]{1,0:T(8,128)(2,1)} custom-call(s32[4]{0:T(128)} %add_add_fusion.index_ref, bf16[4096,1024]{1,0:T(8,128)(2,1)} %get-tuple-element.119.refs_0_, bf16[2048,1024]{1,0:T(8,128)(2,1)} %bitcast.219, bf16[4096,768]{1,0:T(8,128)(2,1)} %shard_map.230.refs_2_, bf16[2048,768]{1,0:T(8,128)(2,1)} %bitcast.228), custom_call_target="tpu_custom_call" | custom-call | flops 7516192768 | bytes 8388608 | tf_op jit(solution)/shard_map/pallas_call | solution.py:287
  688.5 14.5 %collective-permute-done.91 = f32[1,1024]{1,0:T(1,128)S(1)} collective-permute-done((f32[1,1024]{1,0:T(1,128)S(1)}, f32[1,1024]{1,0:T(1,128)S(1)}, u32[]{:S(2)}, u32[]{:S(2)}) %collective-permute-start.91) | collective-permute-done | bytes 4128 | tf_op jit(solution)/shard_map/ppermute | solution.py:25
  711.1 10.7 shard_map.226
  730.2 23.1 %collective-permute-done.73 = bf16[512,256]{1,0:T(8,128)(2,1)S(1)} collective-permute-done((bf16[512,256]{1,0:T(8,128)(2,1)S(1)}, bf16[512,256]{1,0:T(8,128)(2,1)S(1)}, u32[]{:S(2)}, u32[]{:S(2)}) %collective-permute-start.73) | collective-permute-done | bytes 262176 | tf_op jit(solution)/shard_map/ppermute | solution.py:66
  876.1 16.0 %collective-permute-done.96 = bf16[512,1024]{1,0:T(8,128)(2,1)} collective-permute-done((bf16[512,1024]{1,0:T(8,128)(2,1)}, bf16[512,1024]{1,0:T(8,128)(2,1)}, u32[]{:S(2)}, u32[]{:S(2)}) %collective-permute-start.96) | collective-permute-done | bytes 1048608 | tf_op jit(solution)/shard_map/ppermute | solution.py:66
  910.4 10.9 collective-permute-done.89
  932.0 12.5 %collective-permute-done.86 = bf16[512,1024]{1,0:T(8,128)(2,1)S(1)} collective-permute-done((bf16[512,1024]{1,0:T(8,128)(2,1)}, bf16[512,1024]{1,0:T(8,128)(2,1)S(1)}, u32[]{:S(2)}, u32[]{:S(2)}) %collective-permute-start.86) | collective-permute-done | bytes 1048608 | tf_op jit(solution)/shard_map/ppermute | solution.py:66
  1043.3 14.2 %collective-permute-done.41 = bf16[1024,1024]{1,0:T(8,128)(2,1)S(1)} collective-permute-done((bf16[1024,1024]{1,0:T(8,128)(2,1)}, bf16[1024,1024]{1,0:T(8,128)(2,1)S(1)}, u32[]{:S(2)}, u32[]{:S(2)}) %collective-permute-start.41) | collective-permute-done | bytes 2097184 | tf_op jit(solution)/shard_map/ppermute | solution.py:25
  1082.1 14.7 %collective-permute-done.56.refs_6_ = bf16[512,1024]{1,0:T(8,128)(2,1)S(1)} collective-permute-done((bf16[512,1024]{1,0:T(8,128)(2,1)}, bf16[512,1024]{1,0:T(8,128)(2,1)S(1)}, u32[]{:S(2)}, u32[]{:S(2)}) %collective-permute-start.56) | collective-permute-done | bytes 1048608 | tf_op jit(solution)/shard_map/ppermute | solution.py:25
  (569 shorter events, 664.4 us)
Async XLA Ops:
  3.3 66.8 %collective-permute-start.8 = (bf16[256,1024]{1,0:T(8,128)(2,1)}, bf16[256,1024]{1,0:T(8,128)(2,1)}, u32[]{:S(2)}, u32[]{:S(2)}) collective-permute-start(bf16[256,1024]{1,0:T(8,128)(2,1)} %bitcast.260), channel_id=1, source_target_pairs={{0,4},{4,0},{8,12},{12,8},{16,20},{20,16},{24,28},{28,24},{1,5},{5... | collective-permute-start | bytes 1572872 | tf_op jit(solution)/shard_map/ppermute | solution.py:25
  70.2 103.5 %collective-permute-start = (bf16[512,2048]{1,0:T(8,128)(2,1)}, bf16[512,2048]{1,0:T(8,128)(2,1)}, u32[]{:S(2)}, u32[]{:S(2)}) collective-permute-start(bf16[512,2048]{1,0:T(8,128)(2,1)} %get-tuple-element.73), channel_id=1, source_target_pairs={{0,1},{1,0},{2,3},{3,2},{4,5},{5,4},{6,7},{7,6},{8,9},{9,8},{10,11... | collective-permute-start | bytes 6291464 | tf_op jit(solution)/shard_map/ppermute | solution.py:25
  113.1 66.0 %collective-permute-start.43 = (bf16[512,2048]{1,0:T(8,128)(2,1)}, bf16[512,2048]{1,0:T(8,128)(2,1)}, u32[]{:S(2)}, u32[]{:S(2)}) collective-permute-start(bf16[512,2048]{1,0:T(8,128)(2,1)} %get-tuple-element.71), channel_id=1, source_target_pairs={{0,1},{1,0},{2,3},{3,2},{4,5},{5,4},{6,7},{7,6},{8,9},{9,8},{10,11... | collective-permute-start | bytes 6291464 | tf_op jit(solution)/shard_map/ppermute | solution.py:25
  169.9 89.2 %collective-permute-start.44 = (bf16[512,2048]{1,0:T(8,128)(2,1)}, bf16[512,2048]{1,0:T(8,128)(2,1)S(1)}, u32[]{:S(2)}, u32[]{:S(2)}) collective-permute-start(bf16[512,2048]{1,0:T(8,128)(2,1)} %get-tuple-element.71), channel_id=1, source_target_pairs={{0,2},{1,3},{2,0},{3,1},{4,6},{5,7},{6,4},{7,5},{8,10},{9,11},{10,... | collective-permute-start | bytes 6291464 | tf_op jit(solution)/shard_map/ppermute | solution.py:25
  173.2 88.4 %collective-permute-start.3 = (bf16[512,2048]{1,0:T(8,128)(2,1)}, bf16[512,2048]{1,0:T(8,128)(2,1)S(1)}, u32[]{:S(2)}, u32[]{:S(2)}) collective-permute-start(bf16[512,2048]{1,0:T(8,128)(2,1)} %get-tuple-element.73), channel_id=1, source_target_pairs={{0,4},{4,0},{8,12},{12,8},{16,20},{20,16},{24,28},{28,24},{1,5},{5... | collective-permute-start | bytes 6291464 | tf_op jit(solution)/shard_map/ppermute | solution.py:25
  173.7 90.4 %collective-permute-start.46 = (bf16[512,2048]{1,0:T(8,128)(2,1)}, bf16[512,2048]{1,0:T(8,128)(2,1)S(1)}, u32[]{:S(2)}, u32[]{:S(2)}) collective-permute-start(bf16[512,2048]{1,0:T(8,128)(2,1)} %get-tuple-element.71), channel_id=1, source_target_pairs={{0,4},{4,0},{8,12},{12,8},{16,20},{20,16},{24,28},{28,24},{1,5},{5... | collective-permute-start | bytes 6291464 | tf_op jit(solution)/shard_map/ppermute | solution.py:25
  179.0 85.4 %collective-permute-start.26 = (bf16[512,768]{1,0:T(8,128)(2,1)}, bf16[512,768]{1,0:T(8,128)(2,1)S(1)}, u32[]{:S(2)}, u32[]{:S(2)}) collective-permute-start(bf16[512,768]{1,0:T(8,128)(2,1)} %collective-permute-done.25), channel_id=1, source_target_pairs={{16,24},{20,28},{17,25},{21,29},{18,26},{22,30},{19,27},{23,31}} | collective-permute-start | bytes 2359304 | tf_op jit(solution)/shard_map/ppermute | solution.py:30
  310.6 64.7 %collective-permute-start.2 = (bf16[512,2048]{1,0:T(8,128)(2,1)S(1)}, bf16[512,2048]{1,0:T(8,128)(2,1)S(1)}, u32[]{:S(2)}, u32[]{:S(2)}) collective-permute-start(bf16[512,2048]{1,0:T(8,128)(2,1)S(1)} %collective-permute-done.1), channel_id=1, source_target_pairs={{0,1},{1,0},{2,3},{3,2},{4,5},{5,4},{6,7},{7,6},{8,9},{9,8},{10,11... | collective-permute-start | bytes 6291464 | tf_op jit(solution)/shard_map/ppermute | solution.py:25
  314.1 65.2 %collective-permute-start.4 = (bf16[512,2048]{1,0:T(8,128)(2,1)S(1)}, bf16[512,2048]{1,0:T(8,128)(2,1)S(1)}, u32[]{:S(2)}, u32[]{:S(2)}) collective-permute-start(bf16[512,2048]{1,0:T(8,128)(2,1)S(1)} %collective-permute-done.3), channel_id=1, source_target_pairs={{0,1},{1,0},{2,3},{3,2},{4,5},{5,4},{6,7},{7,6},{8,9},{9,8},{10,11... | collective-permute-start | bytes 6291464 | tf_op jit(solution)/shard_map/ppermute | solution.py:25
  375.3 72.1 %collective-permute-start.50 = (bf16[512,2048]{1,0:T(8,128)(2,1)}, bf16[512,2048]{1,0:T(8,128)(2,1)}, u32[]{:S(2)}, u32[]{:S(2)}) collective-permute-start(bf16[512,2048]{1,0:T(8,128)(2,1)} %constant_dynamic-update-slice_fusion.12), channel_id=1, source_target_pairs={{0,1},{1,0},{2,3},{3,2},{4,5},{5,4},{6,7},{7,6},{8,9},{9,8},{10,11... | collective-permute-start | bytes 6291464 | tf_op jit(solution)/shard_map/ppermute | solution.py:25
  684.7 73.1 %collective-permute-start.62 = (bf16[512,768]{1,0:T(8,128)(2,1)}, bf16[512,768]{1,0:T(8,128)(2,1)}, u32[]{:S(2)}, u32[]{:S(2)}) collective-permute-start(bf16[512,768]{1,0:T(8,128)(2,1)} %fusion.98), channel_id=1, source_target_pairs={{0,8},{4,12},{1,9},{5,13},{2,10},{6,14},{3,11},{7,15}} | collective-permute-start | bytes 2359304 | tf_op jit(solution)/shard_map/ppermute | solution.py:66
  686.9 72.5 %collective-permute-start.65 = (bf16[512,768]{1,0:T(8,128)(2,1)}, bf16[512,768]{1,0:T(8,128)(2,1)}, u32[]{:S(2)}, u32[]{:S(2)}) collective-permute-start(bf16[512,768]{1,0:T(8,128)(2,1)} %fusion.92), channel_id=1, source_target_pairs={{24,16},{28,20},{25,17},{29,21},{26,18},{30,22},{27,19},{31,23}} | collective-permute-start | bytes 2359304 | tf_op jit(solution)/shard_map/ppermute | solution.py:69
  721.8 66.3 %collective-permute-start.94 = (bf16[512,1024]{1,0:T(8,128)(2,1)}, bf16[512,1024]{1,0:T(8,128)(2,1)S(1)}, u32[]{:S(2)}, u32[]{:S(2)}) collective-permute-start(bf16[512,1024]{1,0:T(8,128)(2,1)} %fusion.89), channel_id=1, source_target_pairs={{0,8},{4,12},{1,9},{5,13},{2,10},{6,14},{3,11},{7,15}} | collective-permute-start | bytes 3145736 | tf_op jit(solution)/shard_map/ppermute | solution.py:66
  753.3 60.5 %collective-permute-start.84 = (bf16[512,1024]{1,0:T(8,128)(2,1)}, bf16[512,1024]{1,0:T(8,128)(2,1)S(1)}, u32[]{:S(2)}, u32[]{:S(2)}) collective-permute-start(bf16[512,1024]{1,0:T(8,128)(2,1)} %fusion.80), channel_id=1, source_target_pairs={{0,8},{4,12},{1,9},{5,13},{2,10},{6,14},{3,11},{7,15}} | collective-permute-start | bytes 3145736 | tf_op jit(solution)/shard_map/ppermute | solution.py:66
  861.2 90.1 %collective-permute-start.54 = (bf16[2048,1024]{1,0:T(8,128)(2,1)}, bf16[2048,1024]{1,0:T(8,128)(2,1)}, u32[]{:S(2)}, u32[]{:S(2)}) collective-permute-start(bf16[2048,1024]{1,0:T(8,128)(2,1)} %shard_map.235), channel_id=1, source_target_pairs={{0,1},{1,0},{2,3},{3,2},{4,5},{5,4},{6,7},{7,6},{8,9},{9,8},{10,11... | collective-permute-start | bytes 12582920 | tf_op jit(solution)/shard_map/ppermute | solution.py:25
  875.5 92.9 %collective-permute-start.51 = (bf16[2048,1024]{1,0:T(8,128)(2,1)}, bf16[2048,1024]{1,0:T(8,128)(2,1)}, u32[]{:S(2)}, u32[]{:S(2)}) collective-permute-start(bf16[2048,1024]{1,0:T(8,128)(2,1)} %shard_map.231), channel_id=1, source_target_pairs={{0,1},{1,0},{2,3},{3,2},{4,5},{5,4},{6,7},{7,6},{8,9},{9,8},{10,11... | collective-permute-start | bytes 12582920 | tf_op jit(solution)/shard_map/ppermute | solution.py:25
  875.5 108.7 %collective-permute-start.40 = (bf16[2048,1024]{1,0:T(8,128)(2,1)}, bf16[2048,1024]{1,0:T(8,128)(2,1)}, u32[]{:S(2)}, u32[]{:S(2)}) collective-permute-start(bf16[2048,1024]{1,0:T(8,128)(2,1)} %shard_map.226), channel_id=1, source_target_pairs={{0,1},{1,0},{2,3},{3,2},{4,5},{5,4},{6,7},{7,6},{8,9},{9,8},{10,11... | collective-permute-start | bytes 12582920 | tf_op jit(solution)/shard_map/ppermute | solution.py:25
  876.0 120.5 %collective-permute-start.37 = (bf16[2048,1024]{1,0:T(8,128)(2,1)}, bf16[2048,1024]{1,0:T(8,128)(2,1)}, u32[]{:S(2)}, u32[]{:S(2)}) collective-permute-start(bf16[2048,1024]{1,0:T(8,128)(2,1)} %shard_map.222), channel_id=1, source_target_pairs={{0,1},{1,0},{2,3},{3,2},{4,5},{5,4},{6,7},{7,6},{8,9},{9,8},{10,11... | collective-permute-start | bytes 12582920 | tf_op jit(solution)/shard_map/ppermute | solution.py:25
  965.9 182.6 %collective-permute-start.90 = (bf16[256,1024]{1,0:T(8,128)(2,1)}, bf16[256,1024]{1,0:T(8,128)(2,1)}, u32[]{:S(2)}, u32[]{:S(2)}) collective-permute-start(bf16[256,1024]{1,0:T(8,128)(2,1)} %fusion.121), channel_id=1, source_target_pairs={{0,4},{4,0},{8,12},{12,8},{16,20},{20,16},{24,28},{28,24},{1,5},{5... | collective-permute-start | bytes 1572872 | tf_op jit(solution)/shard_map/ppermute | solution.py:25
  994.5 63.0 %collective-permute-start.41 = (bf16[1024,1024]{1,0:T(8,128)(2,1)}, bf16[1024,1024]{1,0:T(8,128)(2,1)S(1)}, u32[]{:S(2)}, u32[]{:S(2)}) collective-permute-start(bf16[1024,1024]{1,0:T(8,128)(2,1)} %shard_map.227), channel_id=1, source_target_pairs={{0,2},{1,3},{2,0},{3,1},{4,6},{5,7},{6,4},{7,5},{8,10},{9,11},{10,... | collective-permute-start | bytes 6291464 | tf_op jit(solution)/shard_map/ppermute | solution.py:25
  1007.0 67.3 %collective-permute-start.38 = (bf16[1024,1024]{1,0:T(8,128)(2,1)}, bf16[1024,1024]{1,0:T(8,128)(2,1)S(1)}, u32[]{:S(2)}, u32[]{:S(2)}) collective-permute-start(bf16[1024,1024]{1,0:T(8,128)(2,1)} %shard_map.223), channel_id=1, source_target_pairs={{0,4},{4,0},{8,12},{12,8},{16,20},{20,16},{24,28},{28,24},{1,5},{5... | collective-permute-start | bytes 6291464 | tf_op jit(solution)/shard_map/ppermute | solution.py:25
  1026.3 70.5 %collective-permute-start.56 = (bf16[512,1024]{1,0:T(8,128)(2,1)}, bf16[512,1024]{1,0:T(8,128)(2,1)S(1)}, u32[]{:S(2)}, u32[]{:S(2)}) collective-permute-start(bf16[512,1024]{1,0:T(8,128)(2,1)} %shard_map.237), channel_id=1, source_target_pairs={{0,4},{4,0},{8,12},{12,8},{16,20},{20,16},{24,28},{28,24},{1,5},{5... | collective-permute-start | bytes 3145736 | tf_op jit(solution)/shard_map/ppermute | solution.py:25
  1038.9 66.4 %collective-permute-start.53 = (bf16[512,1024]{1,0:T(8,128)(2,1)}, bf16[512,1024]{1,0:T(8,128)(2,1)S(1)}, u32[]{:S(2)}, u32[]{:S(2)}) collective-permute-start(bf16[512,1024]{1,0:T(8,128)(2,1)} %shard_map.233), channel_id=1, source_target_pairs={{0,2},{1,3},{2,0},{3,1},{4,6},{5,7},{6,4},{7,5},{8,10},{9,11},{10,... | collective-permute-start | bytes 3145736 | tf_op jit(solution)/shard_map/ppermute | solution.py:25
  1057.5 95.7 %collective-permute-start.100 = (bf16[256,1024]{1,0:T(8,128)(2,1)S(1)}, bf16[256,1024]{1,0:T(8,128)(2,1)}, u32[]{:S(2)}, u32[]{:S(2)}) collective-permute-start(bf16[256,1024]{1,0:T(8,128)(2,1)S(1)} %fusion.122), channel_id=1, source_target_pairs={{0,4},{4,0},{8,12},{12,8},{16,20},{20,16},{24,28},{28,24},{1,5},{5... | collective-permute-start | bytes 1572872 | tf_op jit(solution)/shard_map/ppermute | solution.py:25
  (155 other events, 3815.8 us)

commit v2 on v1

v2 whole, which is shorter than its diff:
```python
import functools
import math

import jax
import jax.numpy as jnp
from jax import lax
from jax.experimental import pallas as pl
from jax.experimental.pallas import tpu as pltpu
from jax.sharding import PartitionSpec as P

HEAD = 64
ROT = 32
EPS = 1e-05
NEG = -1e30
LANES = 128
BF = jnp.bfloat16
F32 = jnp.float32
NT = (((1,), (1,)), ((), ()))
TN = (((0,), (0,)), ((), ()))
VMEM = 56 * 2**20
COST = pl.CostEstimate(flops=0, bytes_accessed=0, transcendentals=0)


def swap(x, axis, bit):
    size = lax.axis_size(axis)
    return lax.ppermute(x, axis, [(i, i ^ bit) for i in range(size)])


def line(x, pairs):
    return lax.ppermute(x, "dp", [(2 * i + s, 2 * j + s) for i, j in pairs for s in (0, 1)])


def after(x, *earlier):
    return lax.optimization_barrier((x,) + earlier)[0]


def pick(x, index):
    return lax.dynamic_index_in_dim(x, index, 0, keepdims=False)


def place(buffer, block, *index):
    return lax.dynamic_update_slice(
        buffer, block.reshape((1,) * len(index) + block.shape), tuple(index) + (0,) * block.ndim
    )


def add(*terms):
    return functools.reduce(lambda a, b: a + b, [x.astype(F32) for x in terms])


def first_terms(parts, places):
    if places != 4:
        return ()
    return (
        line(parts[3], [(0, 1)]),
        line(parts[1], [(3, 2)]),
        line(parts[1], [(0, 1), (1, 2), (2, 3)]),
        line(parts[3], [(1, 0), (2, 1), (3, 2)]),
    )


def join_terms(parts, begun, places, *earlier):
    if places != 4:
        return ()
    joined = add(parts[2], after(begun[0], *earlier), begun[1]).astype(BF)
    return joined, line(joined, [(i, (i + 2) % 4) for i in range(4)])


def last_terms(parts, begun, joined, places, *earlier):
    own = after(parts[0], *earlier) if earlier else parts[0]
    if places == 4:
        return add(own, begun[2], begun[3], joined[1])
    going_up, going_down = parts[places - 1], parts[1]
    for distance in range(places - 1, 0, -1):
        got_up = line(going_up, [(i, i + 1) for i in range(places - distance)])
        got_down = line(going_down, [(i, i - 1) for i in range(distance, places)])
        if distance > 1:
            going_up = add(parts[distance - 1], got_up).astype(BF)
            going_down = add(parts[places - distance + 1], got_down).astype(BF)
    return add(own, got_up, got_down)


def everywhere(x, axes):
    for axis in axes:
        bits = lax.axis_size(axis).bit_length() - 1
        done = 0
        while done < bits:
            now = min(3, bits - done)
            terms = [x] + [swap(x, axis, k << done) for k in range(1, 1 << now)]
            while len(terms) > 1:
                terms = [a + b for a, b in zip(terms[::2], terms[1::2])]
            x = terms[0]
            done += now
    return x


def lanes_of(shape):
    return lax.broadcasted_iota(jnp.int32, shape, 1)


def turn(x, cosine, sine):
    lane = lanes_of(x.shape) % HEAD
    other = jnp.where(lane < ROT // 2, pltpu.roll(x, LANES - ROT // 2, 1), pltpu.roll(x, ROT // 2, 1))
    return x * cosine + other * sine


def qkv_rows(acc, extras, outs):
    bias, cosine, sine = (ref[...] for ref in extras)
    acc = acc + bias
    out_ref = outs[0]
    for at in range(0, acc.shape[1], 3 * LANES):
        q = turn(acc[:, at : at + LANES], cosine, sine).astype(BF)
        out_ref[:, at : at + LANES] = (q.astype(F32) * HEAD**-0.5).astype(BF)
        k = turn(acc[:, at + LANES : at + 2 * LANES], cosine, sine)
        out_ref[:, at + LANES : at + 2 * LANES] = k.astype(BF)
        out_ref[:, at + 2 * LANES : at + 3 * LANES] = acc[:, at + 2 * LANES : at + 3 * LANES].astype(BF)


def plain_rows(acc, extras, outs):
    outs[0][...] = acc.astype(BF)


def gelu_rows(acc, extras, outs):
    z = acc + extras[0][...]
    c = math.sqrt(2.0 / math.pi)
    square = z * z
    gate = 0.5 + 0.5 * jnp.tanh(z * (c + (c * 0.044715) * square))
    value = z * gate
    outs[0][...] = value.astype(BF)
    outs[1][...] = (gate + (value - value * gate) * (2.0 * c + (6.0 * 0.044715 * c) * square)).astype(BF)


def slope_rows(acc, extras, outs):
    outs[0][...] = (acc * extras[0][...].astype(F32)).astype(BF)


class Links:
    def __init__(self, send, recv):
        self.send, self.recv, self.count, self.pending = send, recv, 0, []

    def copy(self, src, dst, device, sends=None, gets=None):
        n = self.count
        self.count += 1
        made = pltpu.make_async_remote_copy(
            src_ref=src,
            dst_ref=dst,
            send_sem=self.send.at[n],
            recv_sem=self.recv.at[n],
            device_id=device,
            device_id_type=pl.DeviceIdType.MESH,
        )
        return Sent(self, made, sends, gets)

    def finish(self):
        for sent in self.pending:
            sent.when(sent.sends, sent.made.wait_send)


class Sent:
    def __init__(self, links, made, sends, gets):
        self.links, self.made, self.sends, self.gets = links, made, sends, gets

    def when(self, condition, action):
        if condition is None:
            action()
        else:
            pl.when(condition)(action)

    def start(self):
        self.when(self.sends, self.made.start)
        self.links.pending.append(self)
        return self

    def get(self):
        self.when(self.gets, self.made.wait_recv)


def greet(devices):
    barrier = pltpu.get_barrier_semaphore()
    for device in devices:
        pl.semaphore_signal(barrier, inc=1, device_id=device, device_id_type=pl.DeviceIdType.MESH)
    pl.semaphore_wait(barrier, len(devices))


class Spot:
    def __init__(self, ndp, nt):
        self.dp, self.t = lax.axis_index("dp"), lax.axis_index("tensor")
        self.half, self.at = self.dp % 2, self.dp // 2
        self.chip, self.core = self.t // 2, self.t % 2
        self.places, self.nt = ndp // 2, nt
        self.mate = (self.dp + 1 - 2 * self.half, self.t)
        self.across = (self.dp, self.t + 2 - 4 * self.chip)
        self.twin = (self.dp, self.t + 1 - 2 * self.core)

    def along(self, place):
        return (2 * place + self.half, self.t)

    def partners(self):
        line = [self.along((self.at + j) % self.places) for j in range(1, self.places)]
        return [self.mate, self.across, self.twin] + line

    def block(self, mates, acrosses, twins):
        g = self.half if not mates else 1 - self.half
        x = self.chip if not acrosses else 1 - self.chip
        c = self.core if not twins else 1 - self.core
        return g * self.nt + 2 * x + c


class GatherRows:
    def __init__(self, links, spot, own, whole, sem):
        self.links, self.spot, self.whole, self.own = links, spot, whole, own
        self.size = own.shape[0]
        self.mid = self.size // 4
        self.local = pltpu.make_async_copy(own, self.rows(spot.block(0, 0, 0)), sem)

    def rows(self, block, first=0, count=None):
        at = pl.multiple_of(block * self.size, self.size) + first
        return self.whole.at[pl.ds(at, count or self.size)]

    def forward(self, block, device, first=0, count=None):
        place = self.rows(block, first, count)
        return self.links.copy(place, place, device).start()

    def first(self):
        spot = self.spot
        self.local.start()
        place = self.rows(spot.block(0, 0, 0))
        self.x = self.links.copy(self.own, place, spot.across).start()
        self.y = self.links.copy(self.own, place, spot.mate).start()
        self.parts = [self.links.copy(self.own, place, spot.twin).start()]

    def second(self):
        spot, rest = self.spot, self.size - self.mid
        self.x.get()
        self.low = self.forward(spot.block(0, 1, 0), spot.mate, 0, self.mid)
        self.parts.append(self.forward(spot.block(0, 1, 0), spot.twin))
        self.y.get()
        self.high = self.forward(spot.block(1, 0, 0), spot.across, self.mid, rest)
        self.parts.append(self.forward(spot.block(1, 0, 0), spot.twin))

    def third(self):
        spot, rest = self.spot, self.size - self.mid
        self.low.get()
        self.parts.append(self.forward(spot.block(1, 1, 0), spot.twin, 0, self.mid))
        self.high.get()
        self.parts.append(self.forward(spot.block(1, 1, 0), spot.twin, self.mid, rest))

    def finish(self):
        self.local.wait()
        for part in self.parts:
            part.get()


class GatherWeight:
    def __init__(self, links, spot, halves, whole, sem):
        self.links, self.spot, self.halves, self.whole = links, spot, halves, whole
        self.shard = halves.shape[1]
        at = pl.multiple_of((2 * spot.at + spot.half) * self.shard, self.shard)
        self.place = whole.at[pl.ds(at, self.shard)]
        self.local = pltpu.make_async_copy(halves.at[spot.half], self.place, sem)

    def pair(self, place):
        return self.whole.at[pl.ds(pl.multiple_of(place * 2 * self.shard, 2 * self.shard), 2 * self.shard)]

    def forward(self, place, to, sends=None, gets=None):
        return self.links.copy(self.pair(place), self.pair(place), self.spot.along(to), sends, gets).start()

    def first(self):
        self.local.start()
        self.y = self.links.copy(self.halves.at[1 - self.spot.half], self.place, self.spot.mate).start()

    def second(self):
        at, places = self.spot.at, self.spot.places
        self.local.wait()
        self.y.get()
        if places == 4:
            self.two = self.forward(at, (at + 2) % 4)
            self.parts = [
                self.forward(at, (at + 1) % 4, at < 3, at > 0),
                self.forward(at, (at + 3) % 4, at > 0, at < 3),
            ]
        else:
            self.parts = [self.forward(at, (at + j) % places) for j in range(1, places)]

    def third(self):
        at = self.spot.at
        if self.spot.places == 4:
            self.two.get()
            inner = (at == 1) | (at == 2)
            self.parts.append(self.forward((at + 2) % 4, 3 * (at // 2), inner, ~inner))

    def finish(self):
        for part in self.parts:
            part.get()


def qkv_body(h_ref, w_ref, b_ref, cos_ref, sin_ref, out_ref):
    acc = jnp.dot(h_ref[...], w_ref[...], preferred_element_type=F32) + b_ref[...]
    cosine, sine = cos_ref[...], sin_ref[...]
    for at in range(0, acc.shape[1], 3 * LANES):
        q = turn(acc[:, at : at + LANES], cosine, sine).astype(BF)
        out_ref[:, at : at + LANES] = (q.astype(F32) * HEAD**-0.5).astype(BF)
        k = turn(acc[:, at + LANES : at + 2 * LANES], cosine, sine)
        out_ref[:, at + LANES : at + 2 * LANES] = k.astype(BF)
        out_ref[:, at + 2 * LANES : at + 3 * LANES] = acc[:, at + 2 * LANES : at + 3 * LANES].astype(BF)


def gelu_body(h_ref, w_ref, b_ref, act_ref, slope_ref):
    z = jnp.dot(h_ref[...], w_ref[...], preferred_element_type=F32) + b_ref[...]
    c = math.sqrt(2.0 / math.pi)
    square = z * z
    gate = 0.5 + 0.5 * jnp.tanh(z * (c + (c * 0.044715) * square))
    value = z * gate
    act_ref[...] = value.astype(BF)
    slope_ref[...] = (gate + (value - value * gate) * (2.0 * c + (6.0 * 0.044715 * c) * square)).astype(BF)


def plain_body(h_ref, w_ref, out_ref):
    out_ref[...] = jnp.dot(h_ref[...], w_ref[...], preferred_element_type=F32).astype(BF)


def slope_body(h_ref, w_ref, slope_ref, out_ref):
    acc = jnp.dot(h_ref[...], w_ref[...], preferred_element_type=F32)
    out_ref[...] = (acc * slope_ref[...].astype(F32)).astype(BF)


def by_rows(body, ins, outs, block, first=0, count=None):
    total = outs[0].shape[0]
    count = count or total // block

    def spec(ref):
        width = ref.shape[1]
        if ref.shape[0] == total:
            return pl.BlockSpec((block, width), lambda i: (first + i, 0))
        return pl.BlockSpec(ref.shape, lambda i: (0, 0))

    pltpu.emit_pipeline(
        body, grid=(count,), in_specs=[spec(r) for r in ins], out_specs=[spec(r) for r in outs]
    )(*ins, *outs)


def by_heads(body, wide_ins, ins, aug_ins, outs, rows, g):
    pairs = wide_ins[0].shape[1] // (3 * LANES)

    def spec(ref, kind):
        if kind == 2:
            return pl.BlockSpec((rows, LANES), lambda j: (g, 0))
        width = 3 * LANES if ref.shape[1] == pairs * 3 * LANES else LANES
        return pl.BlockSpec((rows, width), lambda j: (g, j))

    specs = [spec(r, 0) for r in wide_ins] + [spec(r, 2) for r in aug_ins] + [spec(r, 0) for r in ins]
    pltpu.emit_pipeline(
        body, grid=(pairs,), in_specs=specs, out_specs=[spec(r, 0) for r in outs]
    )(*wide_ins, *aug_ins, *ins, *outs)


def front_kernel(ndp, nt, *refs):
    refs = list(refs)
    take = lambda n: [refs.pop(0) for _ in range(n)]
    h_own, gb_own, wq2, w12, wd2, w22, bias_q, bias_1, cosine, sine, aq, ak = take(12)
    h, gb, wq, w1, wd, w2, qkv, o_float, o, lse, act, slope, go, da = take(14)
    dk_s, dv_s, dqt_s, local_sem, send, recv = take(6)
    spot = Spot(ndp, nt)
    links = Links(send, recv)
    group = h.shape[0] // 2
    own = h_own.shape[0]
    greet(spot.partners())

    rows_h = GatherRows(links, spot, h_own, h, local_sem.at[0])
    rows_gb = GatherRows(links, spot, gb_own, gb, local_sem.at[1])
    gather_q = GatherWeight(links, spot, wq2, wq, local_sem.at[2])
    gather_1 = GatherWeight(links, spot, w12, w1, local_sem.at[3])
    gather_d = GatherWeight(links, spot, wd2, wd, local_sem.at[4])
    gather_2 = GatherWeight(links, spot, w22, w2, local_sem.at[5])

    gather_q.first()
    rows_h.first()
    gather_1.first()
    gather_q.second()
    rows_h.second()
    gather_q.third()
    gather_1.second()
    rows_h.third()
    gather_q.finish()
    rows_gb.first()
    gather_d.first()
    gather_2.first()
    rows_h.finish()
    by_rows(qkv_body, [h, wq, bias_q, cosine, sine], [qkv], own)
    attend = functools.partial(attend_kernel, group, 512)
    by_heads(attend, [qkv], [], [aq, ak], [o_float, o, lse], group, 0)
    gather_1.third()
    gather_d.second()
    by_heads(attend, [qkv], [], [aq, ak], [o_float, o, lse], group, 1)
    rows_gb.second()
    gather_2.second()
    gather_1.finish()
    steps = 2 * group // own
    by_rows(gelu_body, [h, w1, bias_1], [act, slope], own, 0, steps // 2)
    rows_gb.third()
    gather_d.third()
    by_rows(gelu_body, [h, w1, bias_1], [act, slope], own, steps // 2, steps // 2)
    rows_gb.finish()
    gather_d.finish()
    by_rows(plain_body, [gb, wd], [go], own)
    back = functools.partial(attend_back_kernel, group, 256)

    def attend_back(qkv_ref, aq_ref, ak_ref, cos_ref, sin_ref, o_ref, lse_ref, go_ref, out_ref):
        back(qkv_ref, aq_ref, ak_ref, o_ref, lse_ref, go_ref, cos_ref, sin_ref, out_ref, dk_s, dv_s, dqt_s)

    by_heads(attend_back, [qkv], [o_float, lse, go], [aq, ak, cosine, sine], [da], group, 0)
    gather_2.third()
    by_heads(attend_back, [qkv], [o_float, lse, go], [aq, ak, cosine, sine], [da], group, 1)
    gather_2.finish()
    links.finish()


def front_call(ndp, nt, h_own, gb_own, weights, biases, tables):
    own, width = h_own.shape
    rows = 2 * nt * own
    q3, f, q = weights[0].shape[2], weights[1].shape[2], weights[2].shape[2]
    shape = lambda a, b, dtype=BF: jax.ShapeDtypeStruct((a, b), dtype)
    out_shape = [shape(rows, width), shape(rows, width)]
    out_shape += [shape(width, n) for n in (q3, f, q, f)]
    out_shape += [shape(rows, q3), shape(rows, q, F32), shape(rows, q), shape(rows, q, F32)]
    out_shape += [shape(rows, f), shape(rows, f), shape(rows, q), shape(rows, q3)]
    anywhere = pl.BlockSpec(memory_space=pl.ANY)
    group = nt * own
    transfers = 2 * 10 + 4 * (1 + max(4, ndp // 2))
    return pl.pallas_call(
        functools.partial(front_kernel, ndp, nt),
        in_specs=[anywhere] * 12,
        out_specs=[anywhere] * 14,
        out_shape=out_shape,
        scratch_shapes=[
            pltpu.VMEM((group, LANES), F32),
            pltpu.VMEM((group, LANES), F32),
            pltpu.VMEM((LANES, group), F32),
            pltpu.SemaphoreType.DMA((6,)),
            pltpu.SemaphoreType.DMA((transfers,)),
            pltpu.SemaphoreType.DMA((transfers,)),
        ],
        compiler_params=pltpu.CompilerParams(collective_id=0, has_side_effects=True, vmem_limit_bytes=VMEM),
    )(h_own, gb_own, *weights, *biases, *tables)


def outer_kernel(places, steps, n_right, order_ref, left_ref, *refs):
    rights, outs, acc = refs[:n_right], refs[n_right : n_right + places], refs[n_right + places]
    j, r = pl.program_id(0), pl.program_id(1)
    block = left_ref.shape[0]
    here = pl.ds(pl.multiple_of(r * block, block), block)
    first = 0
    for right_ref in rights:
        columns = slice(first, first + right_ref.shape[1])
        first += right_ref.shape[1]
        term = lax.dot_general(left_ref[...], right_ref[here], TN, preferred_element_type=F32)
        for n in range(places):
            @pl.when((j == n) & (r == steps - 1))
            def _():
                outs[n][:, columns] = (term if steps == 1 else acc[:, columns] + term).astype(outs[n].dtype)

        if steps > 1:
            @pl.when(r == 0)
            def _():
                acc[:, columns] = term

            @pl.when((r > 0) & (r < steps - 1))
            def _():
                acc[:, columns] += term


def outer_call(left, rights, at, places, block=2048):
    rows, width = left.shape
    columns = sum(right.shape[1] for right in rights)
    size = width // places
    order = (at + jnp.arange(places, dtype=jnp.int32)) % places
    steps = rows // block
    return pl.pallas_call(
        functools.partial(outer_kernel, places, steps, len(rights)),
        grid_spec=pltpu.PrefetchScalarGridSpec(
            num_scalar_prefetch=1,
            grid=(places, steps),
            in_specs=[pl.BlockSpec((block, size), lambda j, r, order: (r, order[j]))]
            + [pl.BlockSpec((rows, right.shape[1]), lambda j, r, order: (0, 0)) for right in rights],
            out_specs=[pl.BlockSpec((size, columns), lambda j, r, order: (0, 0))] * places,
            scratch_shapes=[pltpu.VMEM((size, columns), F32)],
        ),
        out_shape=[jax.ShapeDtypeStruct((size, columns), BF if j else F32) for j in range(places)],
        compiler_params=pltpu.CompilerParams(vmem_limit_bytes=VMEM),
        cost_estimate=COST,
    )(order, left, *rights)


def attend_kernel(rows, block, qkv_ref, aq_ref, ak_ref, *refs):
    o_ref, bf_ref, lse_ref = refs[-3:]
    lane = lanes_of((rows, LANES))
    lane_q = lanes_of((block, LANES))
    one = jnp.where(lane % HEAD < 3, 1.0, 0.0).astype(BF)
    first = lane < HEAD
    keys = [jnp.where(half, qkv_ref[:, LANES : 2 * LANES], ak_ref[...]) for half in (first, ~first)]
    values = [jnp.where(half, qkv_ref[:, 2 * LANES :], one) for half in (first, ~first)]
    causal = lanes_of((block, block)) <= lax.broadcasted_iota(jnp.int32, (block, block), 0)
    for b in range(rows // block):
        here = pl.ds(b * block, block)
        lo, hi = b * block, (b + 1) * block
        outs, sums = [], []
        for side in (0, 1):
            half = (lane_q < HEAD) if side == 0 else (lane_q >= HEAD)
            q = jnp.where(half, qkv_ref[here, :LANES], aq_ref[here])
            s_near = lax.dot_general(q, keys[side][lo:hi], NT, preferred_element_type=F32)
            s_near = jnp.where(causal, s_near, NEG)
            top = jnp.max(s_near, axis=1, keepdims=True)
            if b:
                s_far = lax.dot_general(q, keys[side][:lo], NT, preferred_element_type=F32)
                top = jnp.maximum(top, jnp.max(s_far, axis=1, keepdims=True))
            o = jnp.dot(jnp.exp(s_near - top).astype(BF), values[side][lo:hi], preferred_element_type=F32)
            if b:
                o = o + jnp.dot(
                    jnp.exp(s_far - top).astype(BF), values[side][:lo], preferred_element_type=F32
                )
            at = HEAD if side == 0 else 0
            total = o[:, at : at + 1]
            outs.append(o / total)
            sums.append(top + jnp.log(total))
        out = jnp.where(lane_q < HEAD, outs[0], outs[1])
        o_ref[here] = out
        bf_ref[here] = out.astype(BF)
        lse_ref[here] = jnp.where(lane_q < HEAD, sums[0], sums[1])


def split3(x):
    a = x.astype(BF).astype(F32)
    b = (x - a).astype(BF).astype(F32)
    return a, b, x - a - b


def attend_back_kernel(
    rows, block, qkv_ref, aq_ref, ak_ref, o_ref, lse_ref, go_ref, cos_ref, sin_ref, *refs
):
    out_ref, dk_s, dv_s, dqt_s = refs
    lane = lanes_of((rows, LANES))
    lane_k = lanes_of((block, LANES))
    one = jnp.where(lane % HEAD < 3, 1.0, 0.0).astype(BF)
    causal = lax.broadcasted_iota(jnp.int32, (block, block), 0) <= lanes_of((block, block))
    prod = o_ref[...] * go_ref[...].astype(F32)
    dq_first = None
    for side in (0, 1):
        half = (lane < HEAD) if side == 0 else (lane >= HEAD)
        delta = -jnp.sum(jnp.where(half, prod, 0.0), axis=1, keepdims=True)
        at = 0 if side == 0 else HEAD
        lse = -lse_ref[:, at : at + 1]
        q = jnp.where(half, qkv_ref[:, :LANES], aq_ref[...]).astype(F32)
        g = jnp.where(half, go_ref[...].astype(F32), 0.0)
        base = HEAD - at
        for i, (a, d) in enumerate(zip(split3(lse), split3(delta))):
            q = jnp.where(lane == base + 8 + i, a, q)
            g = jnp.where(lane == base + i, d, g)
        q, g = q.astype(BF), g.astype(BF)
        k = jnp.where(half, qkv_ref[:, LANES : 2 * LANES], ak_ref[...])
        v = jnp.where(half, qkv_ref[:, 2 * LANES :], one)
        kt = k.T
        for b in range(rows // block):
            lo, hi = b * block, (b + 1) * block
            here = pl.ds(lo, block)
            st = lax.dot_general(k[lo:hi], q[lo:], NT, preferred_element_type=F32)
            dpt = lax.dot_general(v[lo:hi], g[lo:], NT, preferred_element_type=F32)
            p = jnp.exp(st)
            near = jnp.where(causal, p[:, :block], 0.0)
            p = jnp.concatenate([near, p[:, block:]], axis=1) if hi < rows else near
            ds = (p * dpt).astype(BF)
            dv = jnp.dot(p.astype(BF), g[lo:], preferred_element_type=F32)
            dk = jnp.dot(ds, q[lo:], preferred_element_type=F32)
            dq = jnp.dot(kt[:, lo:hi], ds, preferred_element_type=F32)
            if side == 0:
                dk_s[here] = dk
                dv_s[here] = dv
            else:
                dk = jnp.where(lane_k < HEAD, dk_s[here], dk)
                dv = jnp.where(lane_k < HEAD, dv_s[here], dv)
                out_ref[here, LANES : 2 * LANES] = turn(dk, cos_ref[here], -sin_ref[here]).astype(BF)
                out_ref[here, 2 * LANES :] = dv.astype(BF)
            if b == 0:
                dqt_s[...] = dq
            else:
                dqt_s[:, lo:] += dq
        d = dqt_s[...].T * HEAD**-0.5
        if side == 0:
            dq_first = d
        else:
            d = jnp.where(lane < HEAD, dq_first, d)
            out_ref[:, :LANES] = turn(d, cos_ref[...], -sin_ref[...]).astype(BF)


def slope_call(rows, w, slope, block):
    total, depth = rows.shape
    columns = w.shape[1]
    return pl.pallas_call(
        slope_body,
        grid=(total // block,),
        in_specs=[
            pl.BlockSpec((block, depth), lambda i: (i, 0)),
            pl.BlockSpec((depth, columns), lambda i: (0, 0)),
            pl.BlockSpec((block, columns), lambda i: (i, 0)),
        ],
        out_specs=pl.BlockSpec((block, columns), lambda i: (i, 0)),
        out_shape=jax.ShapeDtypeStruct((total, columns), BF),
        compiler_params=pltpu.CompilerParams(vmem_limit_bytes=VMEM),
        cost_estimate=COST,
    )(rows, w, slope)


def rows_kernel(count, terms, added, dtype, index_ref, *refs):
    ins, outs = refs[:-2], refs[-2:]
    i = pl.program_id(0)
    acc = lax.dot_general(ins[0][...], ins[1][...], NT, preferred_element_type=F32)
    for n in range(1, terms):
        acc = acc + lax.dot_general(ins[2 * n][...], ins[2 * n + 1][...], NT, preferred_element_type=F32)
    for part in (0, 1):
        @pl.when(i // count == part)
        def _():
            total = acc
            first = 2 * terms + part * added
            for ref in ins[first : first + added]:
                total = total + ref[...].astype(F32)
            outs[part][...] = total.astype(dtype)


def rows_call(index, factors, added, block, dtype):
    count = len(index[0])
    columns = factors[0][1].shape[0] // 2
    in_specs, args = [], []
    for a, b in factors:
        depth = a.shape[1]
        in_specs.append(pl.BlockSpec((block, depth), lambda i, index: (index[i], 0)))
        in_specs.append(pl.BlockSpec((columns, depth), lambda i, index: (i // count, 0)))
        args += [a, b]
    places = (lambda i: jnp.minimum(i, count - 1), lambda i: jnp.maximum(i - count, 0))
    for part in (0, 1):
        for a, first in added[part]:
            spec = pl.BlockSpec(
                (block, columns), lambda i, index, first=first, part=part: (first + places[part](i), 0)
            )
            in_specs.append(spec)
            args.append(a)
    return pl.pallas_call(
        functools.partial(rows_kernel, count, len(factors), len(added[0]), dtype),
        grid_spec=pltpu.PrefetchScalarGridSpec(
            num_scalar_prefetch=1,
            grid=(2 * count,),
            in_specs=in_specs,
            out_specs=[
                pl.BlockSpec((block, columns), lambda i, index: (places[0](i), 0)),
                pl.BlockSpec((block, columns), lambda i, index: (places[1](i), 0)),
            ],
        ),
        out_shape=[jax.ShapeDtypeStruct((count * block, columns), dtype)] * 2,
        compiler_params=pltpu.CompilerParams(vmem_limit_bytes=VMEM),
        cost_estimate=COST,
    )(jnp.stack(index[0] + index[1]).astype(jnp.int32), *args)


def local(
    layer_input,
    seq_lens,
    ln_gain,
    ln_bias,
    w_qkv,
    b_qkv,
    w_dense,
    b_dense,
    w_fc1,
    b_fc1,
    w_fc2,
    b_fc2,
    cotangent,
):
    own, width = layer_input.shape
    ndp, nt = lax.axis_size("dp"), lax.axis_size("tensor")
    dp, t = lax.axis_index("dp"), lax.axis_index("tensor")
    half, at, places = dp % 2, dp // 2, ndp // 2
    chip, core = t // 2, t % 2
    group = own * nt
    shard = w_qkv.shape[0]
    q_width = w_qkv.shape[2] // 2
    f_width = w_fc1.shape[1] // 2
    pairs = q_width // LANES
    other = 1 - half

    wq = w_qkv.reshape(shard, 3, 2, pairs, LANES).transpose(2, 0, 3, 1, 4).reshape(2, shard, 3 * q_width)
    wd = w_dense.T.reshape(shard, 2, q_width).transpose(1, 0, 2)
    w1 = w_fc1.reshape(shard, 2, f_width).transpose(1, 0, 2)
    w2 = w_fc2.T.reshape(shard, 2, f_width).transpose(1, 0, 2)

    xf = layer_input.astype(F32)
    mean = jnp.mean(xf, axis=1, keepdims=True)
    centred = xf - mean
    rstd = lax.rsqrt(jnp.mean(centred * centred, axis=1, keepdims=True) + EPS)
    x_hat = centred * rstd
    h_own = (x_hat * ln_gain + ln_bias).astype(BF)
    used = jnp.sum(seq_lens[0])
    valid = (t * own + jnp.arange(own, dtype=jnp.int32) < used).astype(F32)[:, None]
    gy = cotangent.astype(F32) * valid
    gb_own = gy.astype(BF)

    lens_of_mate = swap(seq_lens, "dp", 1)

    lens = jnp.zeros((2, seq_lens.shape[1]), jnp.int32)
    lens = place(place(lens, seq_lens[0], half), lens_of_mate[0], other)
    ends = jnp.cumsum(lens, axis=1)
    rows = jnp.arange(group, dtype=jnp.int32)
    segment = jnp.sum((rows[None, :, None] >= ends[:, None, :]).astype(jnp.int32), axis=2)
    begins = jnp.concatenate([ends - lens, ends[:, -1:]], axis=1)
    labels = jnp.arange(begins.shape[1], dtype=jnp.int32)
    mine = segment[:, :, None] == labels
    position = rows[None] - jnp.sum(jnp.where(mine, begins[:, None, :], 0), axis=2)
    steps = jnp.arange(ROT // 2, dtype=F32)
    inverse = jnp.exp(-math.log(10000.0) * 2.0 * steps / ROT)
    angle = inverse[:, None] * position.reshape(1, 2 * group).astype(F32)
    cos16, sin16 = jnp.cos(angle).T, jnp.sin(angle).T
    still = jnp.zeros((2 * group, HEAD - ROT), F32)
    cosine = jnp.concatenate([cos16, cos16, still + 1.0] * 2, axis=1)
    sine = jnp.concatenate([-sin16, sin16, still] * 2, axis=1)
    lane = jnp.arange(LANES, dtype=jnp.int32) % HEAD
    same = segment.reshape(2 * group, 1) == lane[None, :]
    count = begins.shape[1]
    aq = jnp.where(same & (lane < count), NEG, 0.0).astype(BF)
    ak = jnp.where(~same & (lane < count) | (lane >= 8) & (lane < 11), 1.0, 0.0).astype(BF)

    bias_q = pick(b_qkv.reshape(3, 2, pairs, LANES).transpose(1, 2, 0, 3), half).reshape(1, 3 * q_width)
    bias_1 = pick(b_fc1.reshape(2, f_width), half)[None]

    def weight_out(total, *earlier):
        total = total.reshape(2, shard, total.shape[1])
        theirs = swap(pick(total, other).astype(BF), "dp", 1)
        return pick(total, half), theirs

    def both(mine, theirs):
        theirs = theirs.astype(F32)
        return jnp.stack([jnp.where(half == 0, mine, theirs), jnp.where(half == 0, theirs, mine)])

    name = lambda g, x, c: g * nt + 2 * x + c
    p0, p1, x0, x1 = half, other, chip, 1 - chip
    targets = ([(p1, x1), (p1, x0), (p0, x1), (p0, x0)], [(p1, x1), (p0, x1), (p1, x0), (p0, x0)])
    axes = ((("dp", 1), ("tensor", 2)), (("tensor", 2), ("dp", 1)))

    def scatter(stage, factors, got, *earlier):
        if earlier:
            factors = [(after(factors[0][0], *earlier), factors[0][1])] + factors[1:]
        first, last = ((0, 4), (0, 2), (2, 3), (3, 4))[stage]
        c = 1 - core if stage == 0 else core
        index = [[name(g, x, c) for g, x in target[first:last]] for target in targets]
        offsets = ((), (0,), (2, 0), (3, 1, 0))[stage]
        added = [[(got[n][part], offsets[n]) for n in range(stage)] for part in (0, 1)]
        outs = rows_call(index, factors, added, own, F32 if stage == 3 else BF)
        if stage == 3:
            return outs
        if stage == 0:
            return [swap(x, "tensor", 1) for x in outs]
        return [swap(x, *axes[part][stage - 1]) for part, x in enumerate(outs)]

    h, gb, wq_all, w1_all, wd_all, w2_all, qkv, o_float, o, lse, act, slope, go, da = front_call(
        ndp, nt, h_own, gb_own, [wq, w1, wd, w2], [bias_q, bias_1], [cosine, sine, aq, ak]
    )
    g2 = outer_call(gb, [act, o], at, places)
    g2_begun = first_terms(g2, places)
    gz = slope_call(after(gb, g2[0]), w2_all, slope, own)
    g2_joined = join_terms(g2, g2_begun, places, gz)
    branch_by, grad_by = [(act, w2_all), (o, wd_all)], [(gz, w1_all)]
    branch = [scatter(0, branch_by, [], gz)]
    g1 = outer_call(after(h, gz, branch_by[0][0]), [gz], at, places)
    g1_begun = first_terms(g1, places)
    g2_out = weight_out(last_terms(g2, g2_begun, g2_joined, places, g1[0]))
    branch.append(scatter(1, branch_by, branch, g1[0], g2_out[0]))
    grad_by.append((da, wq_all))
    grad = [scatter(0, grad_by, [], g2_out[0])]
    g1_joined = join_terms(g1, g1_begun, places, grad[0][0])
    branch.append(scatter(2, branch_by, branch, grad[0][0]))
    gq = outer_call(after(h, branch[2][0]), [da], at, places)
    gq_begun = first_terms(gq, places)
    grad.append(scatter(1, grad_by, grad, gq[0]))
    g1_out = weight_out(last_terms(g1, g1_begun, g1_joined, places, gq[0]))
    gq_joined = join_terms(gq, gq_begun, places, g1_out[0])
    branch = jnp.concatenate(scatter(3, branch_by, branch, gq[0]), axis=1)
    output = (xf + branch + b_dense + b_fc2).astype(BF)
    grad.append(scatter(2, grad_by, grad, output))
    gq_out = weight_out(last_terms(gq, gq_begun, gq_joined, places))
    dn = jnp.concatenate(scatter(3, grad_by, grad), axis=1)

    scaled = dn * ln_gain
    m1 = jnp.mean(scaled, axis=1, keepdims=True)
    m2 = jnp.mean(scaled * x_hat, axis=1, keepdims=True)
    grad_x = rstd * (scaled - m1 - x_hat * m2) + gy

    def spread(x):
        return place(jnp.zeros((2,) + x.shape, F32), x, half).reshape(-1)

    late = everywhere(jnp.stack([jnp.sum(dn * x_hat, axis=0), jnp.sum(dn, axis=0)]), ("tensor", "dp"))
    early = everywhere(jnp.sum(gy, axis=0, keepdims=True), ("tensor", "dp"))[0]
    g_b1 = spread(jnp.sum(gz, axis=0, dtype=F32))
    g_bq = spread(jnp.sum(da, axis=0, dtype=F32))
    g_biases = everywhere(jnp.concatenate([g_b1, g_bq])[None], ("dp",))[0]
    g_b1 = g_biases[: 2 * f_width]
    g_bq = g_biases[2 * f_width :].reshape(2, pairs, 3, LANES).transpose(2, 0, 1, 3).reshape(3, 2 * q_width)

    g_2 = both(*g2_out)
    g_w2, g_wd = g_2[:, :, :f_width], g_2[:, :, f_width:]
    g_w1, g_wq = both(*g1_out), both(*gq_out)
    out_wq = g_wq.reshape(2, shard, pairs, 3, LANES).transpose(1, 3, 0, 2, 4).reshape(shard, 3, 2 * q_width)
    out_wd = g_wd.transpose(0, 2, 1).reshape(2 * q_width, shard)
    out_w1 = g_w1.transpose(1, 0, 2).reshape(shard, 2 * f_width)
    out_w2 = g_w2.transpose(0, 2, 1).reshape(2 * f_width, shard)
    return (
        output,
        grad_x,
        late[0],
        late[1],
        out_wq,
        g_bq,
        out_wd,
        early,
        out_w1,
        g_b1,
        out_w2,
        early,
    )


def solution(mesh):
    rows = P(("dp", "tensor"), None)
    in_specs = (
        rows,
        P("dp", None),
        P(),
        P(),
        P("dp", None, "tensor"),
        P(None, "tensor"),
        P("tensor", "dp"),
        P(),
        P("dp", "tensor"),
        P("tensor"),
        P("tensor", "dp"),
        P(),
        rows,
    )
    out_specs = (
        rows,
        rows,
        P(),
        P(),
        P("dp", None, "tensor"),
        P(None, "tensor"),
        P("tensor", "dp"),
        P(),
        P("dp", "tensor"),
        P("tensor"),
        P("tensor", "dp"),
        P(),
    )
    return jax.shard_map(local, mesh=mesh, in_specs=in_specs, out_specs=out_specs, check_vma=False)
```

time: 1180 us -> 924 us (0.78)
  Pallas kernels: 240 us -> 540 us
  waiting for transfers between devices: 358 us -> 164 us
  matrix products: 182 us -> 0 us
  local copies, waits for them, and re-layouts: 159 us -> 59.3 us
  starting transfers between devices: 154 us -> 81.7 us
    pallas_call x19 -> x13, Pallas kernels: 240 us -> 540 us  [the longest x1 311 us: front_call(): pl.pallas_call(functools.partial(front_kernel, ndp, nt), in_specs=[anywhe...]
    dot_general x19 -> x0, matrix products: 182 us -> none  [the longest x16 113 us: reduce_weight(): lax.dot_general(columns, right, TN, preferred_element_type=F32)]
    ppermute x48 -> x15, waiting for transfers between devices: 192 us -> 48.1 us  [line(): lax.ppermute(x, 'dp', [(2 * i + s, 2 * j + s) for i, j in pairs for s in...]
    ppermute x48 -> x15, starting transfers between devices: 108 us -> 29.1 us  [line(): lax.ppermute(x, 'dp', [(2 * i + s, 2 * j + s) for i, j in pairs for s in...]
    ppermute x53 -> x43, waiting for transfers between devices: 167 us -> 116 us  [swap(): return lax.ppermute(x, axis, [(i, i ^ bit) for i in range(size)])]
    dynamic_update_slice x38 -> x4, local copies, waits for them, and re-layouts: 49.4 us -> 0.97 us  [place(): lax.dynamic_update_slice(buffer, block.reshape((1,) * len(index) + block....]
    slice x16 -> x2, local copies, waits for them, and re-layouts: 34 us -> 0.62 us  [the longest x1 0.6 us: local(): g_b1 = g_biases[:2 * f_width]]
    another operation x18 -> x2, local copies, waits for them, and re-layouts: 24.3 us -> 0.6 us  [the longest x1 0.6 us: rows_call(): jnp.stack(index[0] + index[1]).astype(jnp.int32)]
  transfers between devices with their start and end apart: 101 -> 58, of which waited for: 33 -> 12; matrix products, arithmetic and copies ran while one was open for 22% -> 8% of each run, Pallas kernels for 15% -> 19%
where the time goes in v2:
time: 924 us; the launch traced here: 918 us
  Pallas kernels  540 us (58%)
  waiting for transfers between devices  164 us (18%)
  starting transfers between devices  81.7 us (9%)
  other arithmetic  71.4 us (8%)
  local copies, waits for them, and re-layouts  59.3 us (6%)
    pallas_call x1, Pallas kernels, front_call(): pl.pallas_call(functools.partial(front_kernel, ndp, nt), in_specs=[anywhe...  311 us
    ppermute x43, waiting for transfers between devices, swap(): return lax.ppermute(x, axis, [(i, i ^ bit) for i in range(size)])  116 us
    pallas_call x8, Pallas kernels, rows_call(): pl.pallas_call(functools.partial(rows_kernel, count, len(factors), len(ad...  113 us
    pallas_call x3, Pallas kernels, outer_call(): pl.pallas_call(functools.partial(outer_kernel, places, steps, len(rights)...  93.4 us
    ppermute x43, starting transfers between devices, swap(): return lax.ppermute(x, axis, [(i, i ^ bit) for i in range(size)])  52.6 us
    ppermute x15, waiting for transfers between devices, line(): lax.ppermute(x, 'dp', [(2 * i + s, 2 * j + s) for i, j in pairs for s in...  48.1 us
    ppermute x15, starting transfers between devices, line(): lax.ppermute(x, 'dp', [(2 * i + s, 2 * j + s) for i, j in pairs for s in...  29.1 us
    pallas_call x1, Pallas kernels, slope_call(): pl.pallas_call(slope_body, grid=(total // block,), in_specs=[pl.BlockSpec...  23.1 us
  transfers between devices with their start and end apart: 58, of which 12 were waited for; matrix products, arithmetic and copies ran while one was open for 8% of the time, Pallas kernels for 19%

profile of v2, /device:TPU:0, one launch (start us, length us, event | category | flops | bytes accessed | tf_op | source)
XLA Modules:
  0.0 918.1 jit_solution(8578149810318247737)
XLA Ops:
  26.8 9.8 %multiply_sine_fusion = (f32[4096,16]{1,0:T(8,128)}, f32[4096,16]{1,0:T(8,128)}, f32[4096,16]{1,0:T(8,128)}) fusion(f32[16]{0:T(128)S(1)} %multiply_exponential_fusion, f32[4096]{0:T(1024)S(1)} %bitcast.115), kind=kLoop, calls=%fused_computation.26 | loop fusion | flops 131072 | bytes 802880 | tf_op jit(solution)/shard_map/sin | solution.py:719
  38.1 10.4 %concatenate.20.refs_8_ = f32[4096,128]{1,0:T(8,128)} concatenate(f32[4096,16]{1,0:T(8,128)} %get-tuple-element.170, f32[4096,16]{1,0:T(8,128)} %get-tuple-element.170, f32[4096,32]{1,0:T(8,128)} %add.353, f32[4096,16]{1,0:T(8,128)} %get-tuple-element.170, f32[4096,16]{1,0:T(8,128)} %get-tuple-element.170, f32[4096,32]{1,0:T(8,128)} %add.353), dimensions={1} | concatenate | bytes 4194304 | tf_op jit(solution)/shard_map/concatenate | solution.py:721
  50.0 10.3 %concatenate.21.refs_9_ = f32[4096,128]{1,0:T(8,128)} concatenate(f32[4096,16]{1,0:T(8,128)} %get-tuple-element.169, f32[4096,16]{1,0:T(8,128)} %get-tuple-element.168, f32[4096,32]{1,0:T(8,128)} %broadcast_in_dim.36, f32[4096,16]{1,0:T(8,128)} %get-tuple-element.169, f32[4096,16]{1,0:T(8,128)} %get-tuple-element.168, f32[4096,32]{1,0:T(8,128)} %broadcast_in_dim.36), dimensions={1} | concatenate | bytes 4194304 | tf_op jit(solution)/shard_map/concatenate | solution.py:722
  63.1 310.7 %shard_map.220 = (bf16[4096,2048]{1,0:T(8,128)(2,1)}, bf16[4096,2048]{1,0:T(8,128)(2,1)}, bf16[2048,768]{1,0:T(8,128)(2,1)}, bf16[2048,1024]{1,0:T(8,128)(2,1)},...) custom-call(bf16[512,2048]{1,0:T(8,128)(2,1)} %get-tuple-element.175, ...), custom_call_target="tpu_custom_call" | custom-call | tf_op jit(solution)/shard_map/pallas_call | solution.py:430
  373.9 43.4 %shard_map.221 = (f32[512,1280]{1,0:T(8,128)}, bf16[512,1280]{1,0:T(8,128)(2,1)}, bf16[512,1280]{1,0:T(8,128)(2,1)}, bf16[512,1280]{1,0:T(8,128)(2,1)}) custom-call(s32[4]{0:T(128)} %and_select_fusion.order_ref, bf16[4096,2048]{1,0:T(8,128)(2,1)} %get-tuple-element.70.left_ref.h_ref, bf16[4096,1024]{1,0:T(8,128)(2,1)} %get-tuple-element.96.refs_0_, ...), custom_call_target="tpu_custom_call" | custom-call | tf_op jit(solution)/shard_map/pallas_call | solution.py:478
  424.3 23.1 %shard_map.222.refs_0_ = bf16[4096,1024]{1,0:T(8,128)(2,1)} custom-call(bf16[4096,2048]{1,0:T(8,128)(2,1)} %get-tuple-element.70.left_ref.h_ref, bf16[2048,1024]{1,0:T(8,128)(2,1)} %get-tuple-element.71.w_ref.refs_1_, bf16[4096,1024]{1,0:T(8,128)(2,1)} %get-tuple-element.72.slope_ref), custom_call_target="tpu_custom_call" | custom-call | tf_op jit(solution)/shard_map/pallas_call | solution.py:597
  455.5 27.8 %shard_map.223 = (f32[512,1024]{1,0:T(8,128)}, bf16[512,1024]{1,0:T(8,128)(2,1)}, bf16[512,1024]{1,0:T(8,128)(2,1)}, bf16[512,1024]{1,0:T(8,128)(2,1)}) custom-call(s32[4]{0:T(128)} %and_select_fusion.order_ref, bf16[4096,2048]{1,0:T(8,128)(2,1)} %get-tuple-element.94.left_ref, bf16[4096,1024]{1,0:T(8,128)(2,1)} %shard_map.222.refs_0_), custom_call_target="tpu_custom_call" | custom-call | tf_op jit(solution)/shard_map/pallas_call | solution.py:478
  483.3 27.7 %collective-permute-done.5 = bf16[512,1280]{1,0:T(8,128)(2,1)} collective-permute-done((bf16[512,1280]{1,0:T(8,128)(2,1)}, bf16[512,1280]{1,0:T(8,128)(2,1)}, u32[]{:S(2)}, u32[]{:S(2)}) %collective-permute-start.5) | collective-permute-done | bytes 1310752 | tf_op jit(solution)/shard_map/ppermute | solution.py:30
  515.9 18.5 %shard_map.225 = (bf16[2048,1024]{1,0:T(8,128)(2,1)}, bf16[2048,1024]{1,0:T(8,128)(2,1)}) custom-call(s32[8]{0:T(128)} %stack.109.index_ref, bf16[4096,1024]{1,0:T(8,128)(2,1)} %get-tuple-element.96.refs_0_, bf16[2048,1024]{1,0:T(8,128)(2,1)} %get-tuple-element.71.w_ref.refs_1_, bf16[4096,256]{1,0:T(8,128)(2,1)} %get-tuple-element.68.refs_1_.refs_2_, ...), custom_call_target="tpu_custom_call" | custom-call | tf_op jit(solution)/shard_map/pallas_call | solution.py:645
  537.8 23.3 %shard_map.224 = (bf16[2048,1024]{1,0:T(8,128)(2,1)}, bf16[2048,1024]{1,0:T(8,128)(2,1)}) custom-call(s32[8]{0:T(128)} %stack.109.index_ref, bf16[4096,1024]{1,0:T(8,128)(2,1)} %shard_map.222.refs_0_, bf16[2048,1024]{1,0:T(8,128)(2,1)} %get-tuple-element.81.refs_1_, bf16[4096,768]{1,0:T(8,128)(2,1)} %get-tuple-element.82.refs_2_.refs_0_, ...), custom_call_target="tpu_custom_call" | custom-call | tf_op jit(solution)/shard_map/pallas_call | solution.py:645
  561.8 12.5 %shard_map.226 = (bf16[1024,1024]{1,0:T(8,128)(2,1)}, bf16[1024,1024]{1,0:T(8,128)(2,1)}) custom-call(s32[4]{0:T(128)} %pad_add_fusion.3.index_ref, bf16[4096,1024]{1,0:T(8,128)(2,1)} %get-tuple-element.96.refs_0_, bf16[2048,1024]{1,0:T(8,128)(2,1)} %get-tuple-element.71.w_ref.refs_1_, bf16[4096,256]{1,0:T(8,128)(2,1)} %get-tuple-element.68.refs_1_.refs_2_, ...), custom_call_target="tpu_custom_call" | custom-call | tf_op jit(solution)/shard_map/pallas_call | solution.py:645
  581.2 41.3 %collective-permute-done.10.refs_7_.refs_8_ = bf16[1024,1024]{1,0:T(8,128)(2,1)} collective-permute-done((bf16[1024,1024]{1,0:T(8,128)(2,1)}, bf16[1024,1024]{1,0:T(8,128)(2,1)}, u32[]{:S(2)}, u32[]{:S(2)}) %collective-permute-start.10) | collective-permute-done | bytes 2097184 | tf_op jit(solution)/shard_map/ppermute | solution.py:26
  626.2 9.6 %shard_map.227 = (bf16[512,1024]{1,0:T(8,128)(2,1)}, bf16[512,1024]{1,0:T(8,128)(2,1)}) custom-call(s32[2]{0:T(128)} %pad_add_fusion.2.index_ref, bf16[4096,1024]{1,0:T(8,128)(2,1)} %get-tuple-element.96.refs_0_, bf16[2048,1024]{1,0:T(8,128)(2,1)} %get-tuple-element.71.w_ref.refs_1_, bf16[4096,256]{1,0:T(8,128)(2,1)} %get-tuple-element.68.refs_1_.refs_2_, ...), custom_call_target="tpu_custom_call" | custom-call | tf_op jit(solution)/shard_map/pallas_call | solution.py:645
  650.7 10.2 %collective-permute-done.11.refs_6_ = bf16[512,1024]{1,0:T(8,128)(2,1)} collective-permute-done((bf16[512,1024]{1,0:T(8,128)(2,1)}, bf16[512,1024]{1,0:T(8,128)(2,1)}, u32[]{:S(2)}, u32[]{:S(2)}) %collective-permute-start.11) | collective-permute-done | bytes 1048608 | tf_op jit(solution)/shard_map/ppermute | solution.py:26
  662.1 22.2 %shard_map.228 = (f32[512,768]{1,0:T(8,128)}, bf16[512,768]{1,0:T(8,128)(2,1)}, bf16[512,768]{1,0:T(8,128)(2,1)}, bf16[512,768]{1,0:T(8,128)(2,1)}) custom-call(s32[4]{0:T(128)} %and_select_fusion.order_ref, bf16[4096,2048]{1,0:T(8,128)(2,1)} %get-tuple-element.94.left_ref, bf16[4096,768]{1,0:T(8,128)(2,1)} %get-tuple-element.82.refs_2_.refs_0_), custom_call_target="tpu_custom_call" | custom-call | tf_op jit(solution)/shard_map/pallas_call | solution.py:478
  687.0 10.1 %collective-permute-done.35 = bf16[512,1024]{1,0:T(8,128)(2,1)} collective-permute-done((bf16[512,1024]{1,0:T(8,128)(2,1)}, bf16[512,1024]{1,0:T(8,128)(2,1)}, u32[]{:S(2)}, u32[]{:S(2)}) %collective-permute-start.35) | collective-permute-done | bytes 1048608 | tf_op jit(solution)/shard_map/ppermute | solution.py:30
  710.7 15.1 %shard_map.230 = (bf16[1024,1024]{1,0:T(8,128)(2,1)}, bf16[1024,1024]{1,0:T(8,128)(2,1)}) custom-call(s32[4]{0:T(128)} %pad_add_fusion.3.index_ref, bf16[4096,1024]{1,0:T(8,128)(2,1)} %shard_map.222.refs_0_, bf16[2048,1024]{1,0:T(8,128)(2,1)} %get-tuple-element.81.refs_1_, bf16[4096,768]{1,0:T(8,128)(2,1)} %get-tuple-element.82.refs_2_.refs_0_, ...), custom_call_target="tpu_custom_call" | custom-call | tf_op jit(solution)/shard_map/pallas_call | solution.py:645
  735.4 8.4 collective-permute-done.30
  743.7 5.2 collective-permute-start.28
  751.6 41.3 %collective-permute-done.12.refs_9_ = bf16[512,1024]{1,0:T(8,128)(2,1)} collective-permute-done((bf16[512,1024]{1,0:T(8,128)(2,1)}, bf16[512,1024]{1,0:T(8,128)(2,1)}, u32[]{:S(2)}, u32[]{:S(2)}) %collective-permute-start.12) | collective-permute-done | bytes 1048608 | tf_op jit(solution)/shard_map/ppermute | solution.py:26
  801.2 10.8 %shard_map.229 = (f32[512,1024]{1,0:T(8,128)}, f32[512,1024]{1,0:T(8,128)}) custom-call(s32[2]{0:T(128)} %pad_add_fusion.1.index_ref, bf16[4096,1024]{1,0:T(8,128)(2,1)} %get-tuple-element.96.refs_0_, bf16[2048,1024]{1,0:T(8,128)(2,1)} %get-tuple-element.71.w_ref.refs_1_, bf16[4096,256]{1,0:T(8,128)(2,1)} %get-tuple-element.68.refs_1_.refs_2_, ...), custom_call_target="tpu_custom_call" | custom-call | tf_op jit(solution)/shard_map/pallas_call | solution.py:645
  816.5 10.9 %shard_map.231 = (bf16[512,1024]{1,0:T(8,128)(2,1)}, bf16[512,1024]{1,0:T(8,128)(2,1)}) custom-call(s32[2]{0:T(128)} %pad_add_fusion.2.index_ref, bf16[4096,1024]{1,0:T(8,128)(2,1)} %shard_map.222.refs_0_, bf16[2048,1024]{1,0:T(8,128)(2,1)} %get-tuple-element.81.refs_1_, bf16[4096,768]{1,0:T(8,128)(2,1)} %get-tuple-element.82.refs_2_.refs_0_, ...), custom_call_target="tpu_custom_call" | custom-call | tf_op jit(solution)/shard_map/pallas_call | solution.py:645
  838.9 18.3 %collective-permute-done.38 = bf16[256,768]{0,1:T(8,128)(2,1)S(1)} collective-permute-done((bf16[256,768]{0,1:T(8,128)(2,1)}, bf16[256,768]{0,1:T(8,128)(2,1)S(1)}, u32[]{:S(2)}, u32[]{:S(2)}) %collective-permute-start.38) | collective-permute-done | bytes 393248 | tf_op jit(solution)/shard_map/ppermute | solution.py:26
  858.5 12.2 %shard_map.232 = (f32[512,1024]{1,0:T(8,128)}, f32[512,1024]{1,0:T(8,128)}) custom-call(s32[2]{0:T(128)} %pad_add_fusion.1.index_ref, bf16[4096,1024]{1,0:T(8,128)(2,1)} %shard_map.222.refs_0_, bf16[2048,1024]{1,0:T(8,128)(2,1)} %get-tuple-element.81.refs_1_, bf16[4096,768]{1,0:T(8,128)(2,1)} %get-tuple-element.82.refs_2_.refs_0_, ...), custom_call_target="tpu_custom_call" | custom-call | tf_op jit(solution)/shard_map/pallas_call | solution.py:645
  (269 shorter events, 183.6 us)
Async XLA Ops:
  417.2 32.0 %collective-permute-start.3 = (bf16[512,1280]{1,0:T(8,128)(2,1)}, bf16[512,1280]{1,0:T(8,128)(2,1)S(1)}, u32[]{:S(2)}, u32[]{:S(2)}) collective-permute-start(bf16[512,1280]{1,0:T(8,128)(2,1)} %get-tuple-element.77), channel_id=1, source_target_pairs={{0,8},{4,12},{1,9},{5,13},{2,10},{6,14},{3,11},{7,15}} | collective-permute-start | bytes 3932168 | tf_op jit(solution)/shard_map/ppermute | solution.py:30
  419.8 29.5 %collective-permute-start.4 = (bf16[512,1280]{1,0:T(8,128)(2,1)}, bf16[512,1280]{1,0:T(8,128)(2,1)}, u32[]{:S(2)}, u32[]{:S(2)}) collective-permute-start(bf16[512,1280]{1,0:T(8,128)(2,1)} %get-tuple-element.76), channel_id=1, source_target_pairs={{24,16},{28,20},{25,17},{29,21},{26,18},{30,22},{27,19},{31,23}} | collective-permute-start | bytes 3932168 | tf_op jit(solution)/shard_map/ppermute | solution.py:30
  421.6 61.7 %collective-permute-start.1 = (bf16[512,1280]{1,0:T(8,128)(2,1)}, bf16[512,1280]{1,0:T(8,128)(2,1)S(1)}, u32[]{:S(2)}, u32[]{:S(2)}) collective-permute-start(bf16[512,1280]{1,0:T(8,128)(2,1)} %get-tuple-element.76), channel_id=1, source_target_pairs={{0,8},{4,12},{8,16},{12,20},{16,24},{20,28},{1,9},{5,13},{9,17},{1... | collective-permute-start | bytes 3932168 | tf_op jit(solution)/shard_map/ppermute | solution.py:30
  423.0 60.3 %collective-permute-start.2 = (bf16[512,1280]{1,0:T(8,128)(2,1)}, bf16[512,1280]{1,0:T(8,128)(2,1)S(1)}, u32[]{:S(2)}, u32[]{:S(2)}) collective-permute-start(bf16[512,1280]{1,0:T(8,128)(2,1)} %get-tuple-element.77), channel_id=1, source_target_pairs={{8,0},{12,4},{16,8},{20,12},{24,16},{28,20},{9,1},{13,5},{17,9},{2... | collective-permute-start | bytes 3932168 | tf_op jit(solution)/shard_map/ppermute | solution.py:30
  452.2 58.7 %collective-permute-start.5 = (bf16[512,1280]{1,0:T(8,128)(2,1)}, bf16[512,1280]{1,0:T(8,128)(2,1)}, u32[]{:S(2)}, u32[]{:S(2)}) collective-permute-start(bf16[512,1280]{1,0:T(8,128)(2,1)} %add_convert_fusion), channel_id=1, source_target_pairs={{0,16},{4,20},{8,24},{12,28},{16,0},{20,4},{24,8},{28,12},{1,17},{... | collective-permute-start | bytes 3932168 | tf_op jit(solution)/shard_map/ppermute | solution.py:30
  534.5 27.3 %collective-permute-start.7 = (bf16[2048,1024]{1,0:T(8,128)(2,1)}, bf16[2048,1024]{1,0:T(8,128)(2,1)}, u32[]{:S(2)}, u32[]{:S(2)}) collective-permute-start(bf16[2048,1024]{1,0:T(8,128)(2,1)} %get-tuple-element.88), channel_id=1, source_target_pairs={{0,1},{1,0},{2,3},{3,2},{4,5},{5,4},{6,7},{7,6},{8,9},{9,8},{10,11... | collective-permute-start | bytes 12582920 | tf_op jit(solution)/shard_map/ppermute | solution.py:26
  534.5 27.3 %collective-permute-start.8 = (bf16[2048,1024]{1,0:T(8,128)(2,1)}, bf16[2048,1024]{1,0:T(8,128)(2,1)}, u32[]{:S(2)}, u32[]{:S(2)}) collective-permute-start(bf16[2048,1024]{1,0:T(8,128)(2,1)} %get-tuple-element.90), channel_id=1, source_target_pairs={{0,1},{1,0},{2,3},{3,2},{4,5},{5,4},{6,7},{7,6},{8,9},{9,8},{10,11... | collective-permute-start | bytes 12582920 | tf_op jit(solution)/shard_map/ppermute | solution.py:26
  574.2 48.3 %collective-permute-start.10 = (bf16[1024,1024]{1,0:T(8,128)(2,1)}, bf16[1024,1024]{1,0:T(8,128)(2,1)}, u32[]{:S(2)}, u32[]{:S(2)}) collective-permute-start(bf16[1024,1024]{1,0:T(8,128)(2,1)} %get-tuple-element.92), channel_id=1, source_target_pairs={{0,2},{1,3},{2,0},{3,1},{4,6},{5,7},{6,4},{7,5},{8,10},{9,11},{10,... | collective-permute-start | bytes 6291464 | tf_op jit(solution)/shard_map/ppermute | solution.py:26
  574.8 50.1 %collective-permute-start.9 = (bf16[1024,1024]{1,0:T(8,128)(2,1)}, bf16[1024,1024]{1,0:T(8,128)(2,1)}, u32[]{:S(2)}, u32[]{:S(2)}) collective-permute-start(bf16[1024,1024]{1,0:T(8,128)(2,1)} %get-tuple-element.91), channel_id=1, source_target_pairs={{0,4},{4,0},{8,12},{12,8},{16,20},{20,16},{24,28},{28,24},{1,5},{5... | collective-permute-start | bytes 6291464 | tf_op jit(solution)/shard_map/ppermute | solution.py:26
  576.0 134.7 %collective-permute-start.13 = (bf16[2048,1024]{1,0:T(8,128)(2,1)}, bf16[2048,1024]{1,0:T(8,128)(2,1)}, u32[]{:S(2)}, u32[]{:S(2)}) collective-permute-start(bf16[2048,1024]{1,0:T(8,128)(2,1)} %get-tuple-element.101), channel_id=1, source_target_pairs={{0,1},{1,0},{2,3},{3,2},{4,5},{5,4},{6,7},{7,6},{8,9},{9,8},{10,11... | collective-permute-start | bytes 12582920 | tf_op jit(solution)/shard_map/ppermute | solution.py:26
  576.0 59.8 %collective-permute-start.33 = (bf16[512,1024]{1,0:T(8,128)(2,1)}, bf16[512,1024]{1,0:T(8,128)(2,1)}, u32[]{:S(2)}, u32[]{:S(2)}) collective-permute-start(bf16[512,1024]{1,0:T(8,128)(2,1)} %get-tuple-element.114), channel_id=1, source_target_pairs={{0,8},{4,12},{1,9},{5,13},{2,10},{6,14},{3,11},{7,15}} | collective-permute-start | bytes 3145736 | tf_op jit(solution)/shard_map/ppermute | solution.py:30
  578.2 58.1 %collective-permute-start.34 = (bf16[512,1024]{1,0:T(8,128)(2,1)}, bf16[512,1024]{1,0:T(8,128)(2,1)}, u32[]{:S(2)}, u32[]{:S(2)}) collective-permute-start(bf16[512,1024]{1,0:T(8,128)(2,1)} %get-tuple-element.113), channel_id=1, source_target_pairs={{24,16},{28,20},{25,17},{29,21},{26,18},{30,22},{27,19},{31,23}} | collective-permute-start | bytes 3145736 | tf_op jit(solution)/shard_map/ppermute | solution.py:30
  622.6 61.8 %collective-permute-start.31 = (bf16[512,1024]{1,0:T(8,128)(2,1)}, bf16[512,1024]{1,0:T(8,128)(2,1)}, u32[]{:S(2)}, u32[]{:S(2)}) collective-permute-start(bf16[512,1024]{1,0:T(8,128)(2,1)} %get-tuple-element.113), channel_id=1, source_target_pairs={{0,8},{4,12},{8,16},{12,20},{16,24},{20,28},{1,9},{5,13},{9,17},{1... | collective-permute-start | bytes 3145736 | tf_op jit(solution)/shard_map/ppermute | solution.py:30
  624.9 61.8 %collective-permute-start.32 = (bf16[512,1024]{1,0:T(8,128)(2,1)}, bf16[512,1024]{1,0:T(8,128)(2,1)}, u32[]{:S(2)}, u32[]{:S(2)}) collective-permute-start(bf16[512,1024]{1,0:T(8,128)(2,1)} %get-tuple-element.114), channel_id=1, source_target_pairs={{8,0},{12,4},{16,8},{20,12},{24,16},{28,20},{9,1},{13,5},{17,9},{2... | collective-permute-start | bytes 3145736 | tf_op jit(solution)/shard_map/ppermute | solution.py:30
  639.5 57.6 %collective-permute-start.35 = (bf16[512,1024]{1,0:T(8,128)(2,1)}, bf16[512,1024]{1,0:T(8,128)(2,1)}, u32[]{:S(2)}, u32[]{:S(2)}) collective-permute-start(bf16[512,1024]{1,0:T(8,128)(2,1)} %add_convert_fusion.1), channel_id=1, source_target_pairs={{0,16},{4,20},{8,24},{12,28},{16,0},{20,4},{24,8},{28,12},{1,17},{... | collective-permute-start | bytes 3145736 | tf_op jit(solution)/shard_map/ppermute | solution.py:30
  660.9 38.9 %collective-permute-start.39 = (f32[1,3584]{1,0:T(1,128)S(1)}, f32[1,3584]{1,0:T(1,128)S(1)}, u32[]{:S(2)}, u32[]{:S(2)}) collective-permute-start(f32[1,3584]{1,0:T(1,128)S(1)} %broadcast_in_dim.69), channel_id=1, source_target_pairs={{0,4},{4,0},{8,12},{12,8},{16,20},{20,16},{24,28},{28,24},{1,5},{5... | collective-permute-start | bytes 43016 | tf_op jit(solution)/shard_map/ppermute | solution.py:26
  725.8 90.7 %collective-permute-start.14 = (bf16[1024,1024]{1,0:T(8,128)(2,1)}, bf16[1024,1024]{1,0:T(8,128)(2,1)}, u32[]{:S(2)}, u32[]{:S(2)}) collective-permute-start(bf16[1024,1024]{1,0:T(8,128)(2,1)} %get-tuple-element.102), channel_id=1, source_target_pairs={{0,4},{4,0},{8,12},{12,8},{16,20},{20,16},{24,28},{28,24},{1,5},{5... | collective-permute-start | bytes 6291464 | tf_op jit(solution)/shard_map/ppermute | solution.py:26
  726.6 89.9 %collective-permute-start.15 = (bf16[1024,1024]{1,0:T(8,128)(2,1)}, bf16[1024,1024]{1,0:T(8,128)(2,1)}, u32[]{:S(2)}, u32[]{:S(2)}) collective-permute-start(bf16[1024,1024]{1,0:T(8,128)(2,1)} %get-tuple-element.104), channel_id=1, source_target_pairs={{0,2},{1,3},{2,0},{3,1},{4,6},{5,7},{6,4},{7,5},{8,10},{9,11},{10,... | collective-permute-start | bytes 6291464 | tf_op jit(solution)/shard_map/ppermute | solution.py:26
  727.7 65.1 %collective-permute-start.12 = (bf16[512,1024]{1,0:T(8,128)(2,1)}, bf16[512,1024]{1,0:T(8,128)(2,1)}, u32[]{:S(2)}, u32[]{:S(2)}) collective-permute-start(bf16[512,1024]{1,0:T(8,128)(2,1)} %get-tuple-element.97), channel_id=1, source_target_pairs={{0,4},{4,0},{8,12},{12,8},{16,20},{20,16},{24,28},{28,24},{1,5},{5... | collective-permute-start | bytes 3145736 | tf_op jit(solution)/shard_map/ppermute | solution.py:26
  743.7 85.0 %collective-permute-start.28 = (bf16[512,768]{1,0:T(8,128)(2,1)}, bf16[512,768]{1,0:T(8,128)(2,1)}, u32[]{:S(2)}, u32[]{:S(2)}) collective-permute-start(bf16[512,768]{1,0:T(8,128)(2,1)} %get-tuple-element.109), channel_id=1, source_target_pairs={{0,8},{4,12},{8,16},{12,20},{16,24},{20,28},{1,9},{5,13},{9,17},{1... | collective-permute-start | bytes 2359304 | tf_op jit(solution)/shard_map/ppermute | solution.py:30
  748.9 79.8 %collective-permute-start.29 = (bf16[512,768]{1,0:T(8,128)(2,1)}, bf16[512,768]{1,0:T(8,128)(2,1)}, u32[]{:S(2)}, u32[]{:S(2)}) collective-permute-start(bf16[512,768]{1,0:T(8,128)(2,1)} %get-tuple-element.110), channel_id=1, source_target_pairs={{8,0},{12,4},{16,8},{20,12},{24,16},{28,20},{9,1},{13,5},{17,9},{2... | collective-permute-start | bytes 2359304 | tf_op jit(solution)/shard_map/ppermute | solution.py:30
  792.9 35.8 %collective-permute-start.37 = (bf16[512,768]{1,0:T(8,128)(2,1)}, bf16[512,768]{1,0:T(8,128)(2,1)}, u32[]{:S(2)}, u32[]{:S(2)}) collective-permute-start(bf16[512,768]{1,0:T(8,128)(2,1)} %add_convert_fusion.2), channel_id=1, source_target_pairs={{0,16},{4,20},{8,24},{12,28},{16,0},{20,4},{24,8},{28,12},{1,17},{... | collective-permute-start | bytes 2359304 | tf_op jit(solution)/shard_map/ppermute | solution.py:30
  827.4 31.1 %collective-permute-start.16 = (bf16[512,1024]{1,0:T(8,128)(2,1)}, bf16[512,1024]{1,0:T(8,128)(2,1)}, u32[]{:S(2)}, u32[]{:S(2)}) collective-permute-start(bf16[512,1024]{1,0:T(8,128)(2,1)} %get-tuple-element.105), channel_id=1, source_target_pairs={{0,2},{1,3},{2,0},{3,1},{4,6},{5,7},{6,4},{7,5},{8,10},{9,11},{10,... | collective-permute-start | bytes 3145736 | tf_op jit(solution)/shard_map/ppermute | solution.py:26
  827.9 30.6 %collective-permute-start.17 = (bf16[512,1024]{1,0:T(8,128)(2,1)}, bf16[512,1024]{1,0:T(8,128)(2,1)}, u32[]{:S(2)}, u32[]{:S(2)}) collective-permute-start(bf16[512,1024]{1,0:T(8,128)(2,1)} %get-tuple-element.106), channel_id=1, source_target_pairs={{0,4},{4,0},{8,12},{12,8},{16,20},{20,16},{24,28},{28,24},{1,5},{5... | collective-permute-start | bytes 3145736 | tf_op jit(solution)/shard_map/ppermute | solution.py:26
  (66 other events, 810.9 us)

commit v3 on v2

--- a/solution.py
+++ b/solution.py
@@ -26,14 +26,6 @@
     return lax.ppermute(x, axis, [(i, i ^ bit) for i in range(size)])
 
 
-def line(x, pairs):
-    return lax.ppermute(x, "dp", [(2 * i + s, 2 * j + s) for i, j in pairs for s in (0, 1)])
-
-
-def after(x, *earlier):
-    return lax.optimization_barrier((x,) + earlier)[0]
-
-
 def pick(x, index):
     return lax.dynamic_index_in_dim(x, index, 0, keepdims=False)
 
@@ -42,56 +34,6 @@
     return lax.dynamic_update_slice(
         buffer, block.reshape((1,) * len(index) + block.shape), tuple(index) + (0,) * block.ndim
     )
-
-
-def add(*terms):
-    return functools.reduce(lambda a, b: a + b, [x.astype(F32) for x in terms])
-
-
-def first_terms(parts, places):
-    if places != 4:
-        return ()
-    return (
-        line(parts[3], [(0, 1)]),
-        line(parts[1], [(3, 2)]),
-        line(parts[1], [(0, 1), (1, 2), (2, 3)]),
-        line(parts[3], [(1, 0), (2, 1), (3, 2)]),
-    )
-
-
-def join_terms(parts, begun, places, *earlier):
-    if places != 4:
-        return ()
-    joined = add(parts[2], after(begun[0], *earlier), begun[1]).astype(BF)
-    return joined, line(joined, [(i, (i + 2) % 4) for i in range(4)])
-
-
-def last_terms(parts, begun, joined, places, *earlier):
-    own = after(parts[0], *earlier) if earlier else parts[0]
-    if places == 4:
-        return add(own, begun[2], begun[3], joined[1])
-    going_up, going_down = parts[places - 1], parts[1]
-    for distance in range(places - 1, 0, -1):
-        got_up = line(going_up, [(i, i + 1) for i in range(places - distance)])
-        got_down = line(going_down, [(i, i - 1) for i in range(distance, places)])
-        if distance > 1:
-            going_up = add(parts[distance - 1], got_up).astype(BF)
-            going_down = add(parts[places - distance + 1], got_down).astype(BF)
-    return add(own, got_up, got_down)
-
-
-def everywhere(x, axes):
-    for axis in axes:
-        bits = lax.axis_size(axis).bit_length() - 1
-        done = 0
-        while done < bits:
-            now = min(3, bits - done)
-            terms = [x] + [swap(x, axis, k << done) for k in range(1, 1 << now)]
-            while len(terms) > 1:
-                terms = [a + b for a, b in zip(terms[::2], terms[1::2])]
-            x = terms[0]
-            done += now
-    return x
 
 
 def lanes_of(shape):
@@ -173,6 +115,10 @@
 
     def get(self):
         self.when(self.gets, self.made.wait_recv)
+
+    def drain(self):
+        self.links.pending.remove(self)
+        self.when(self.sends, self.made.wait_send)
 
 
 def greet(devices):
@@ -442,53 +388,6 @@
         ],
         compiler_params=pltpu.CompilerParams(collective_id=0, has_side_effects=True, vmem_limit_bytes=VMEM),
     )(h_own, gb_own, *weights, *biases, *tables)
-
-
-def outer_kernel(places, steps, n_right, order_ref, left_ref, *refs):
-    rights, outs, acc = refs[:n_right], refs[n_right : n_right + places], refs[n_right + places]
-    j, r = pl.program_id(0), pl.program_id(1)
-    block = left_ref.shape[0]
-    here = pl.ds(pl.multiple_of(r * block, block), block)
-    first = 0
-    for right_ref in rights:
-        columns = slice(first, first + right_ref.shape[1])
-        first += right_ref.shape[1]
-        term = lax.dot_general(left_ref[...], right_ref[here], TN, preferred_element_type=F32)
-        for n in range(places):
-            @pl.when((j == n) & (r == steps - 1))
-            def _():
-                outs[n][:, columns] = (term if steps == 1 else acc[:, columns] + term).astype(outs[n].dtype)
-
-        if steps > 1:
-            @pl.when(r == 0)
-            def _():
-                acc[:, columns] = term
-
-            @pl.when((r > 0) & (r < steps - 1))
-            def _():
-                acc[:, columns] += term
-
-
-def outer_call(left, rights, at, places, block=2048):
-    rows, width = left.shape
-    columns = sum(right.shape[1] for right in rights)
-    size = width // places
-    order = (at + jnp.arange(places, dtype=jnp.int32)) % places
-    steps = rows // block
-    return pl.pallas_call(
-        functools.partial(outer_kernel, places, steps, len(rights)),
-        grid_spec=pltpu.PrefetchScalarGridSpec(
-            num_scalar_prefetch=1,
-            grid=(places, steps),
-            in_specs=[pl.BlockSpec((block, size), lambda j, r, order: (r, order[j]))]
-            + [pl.BlockSpec((rows, right.shape[1]), lambda j, r, order: (0, 0)) for right in rights],
-            out_specs=[pl.BlockSpec((size, columns), lambda j, r, order: (0, 0))] * places,
-            scratch_shapes=[pltpu.VMEM((size, columns), F32)],
-        ),
-        out_shape=[jax.ShapeDtypeStruct((size, columns), BF if j else F32) for j in range(places)],
-        compiler_params=pltpu.CompilerParams(vmem_limit_bytes=VMEM),
-        cost_estimate=COST,
-    )(order, left, *rights)
 
 
 def attend_kernel(rows, block, qkv_ref, aq_ref, ak_ref, *refs):
@@ -591,72 +490,400 @@
             out_ref[:, :LANES] = turn(d, cos_ref[...], -sin_ref[...]).astype(BF)
 
 
-def slope_call(rows, w, slope, block):
-    total, depth = rows.shape
-    columns = w.shape[1]
+def outer_products(left, rights, parts, acc, spot, block, sums=None):
+    places = spot.places
+    rows, size = left.shape[0], left.shape[1] // places
+    steps = rows // block
+    columns = parts.shape[2]
+
+    def body(step, left_ref, *refs):
+        right_refs, out = refs[:-1], refs[-1]
+        r, j = step.index
+        first = 0
+        for right_ref in right_refs:
+            there = slice(first, first + right_ref.shape[1])
+            first += right_ref.shape[1]
+            term = lax.dot_general(left_ref[...], right_ref[...], TN, preferred_element_type=F32)
+
+            @pl.when(r == 0)
+            def _():
+                acc[j, :, there] = term
+
+            @pl.when((r > 0) & (r < steps - 1))
+            def _():
+                acc[j, :, there] += term
+
+            @pl.when(r == steps - 1)
+            def _():
+                out[:, there] = (acc[j, :, there] + term).astype(BF)
+
+            if sums is not None:
+                @pl.when(j == 0)
+                def _():
+                    sums[...] += jnp.sum(right_ref[...].astype(F32), axis=0, keepdims=True)
+
+    pltpu.emit_pipeline(
+        body,
+        grid=(steps, places),
+        in_specs=[pl.BlockSpec((block, size), lambda r, j: (r, lax.rem(spot.at + j, places)))]
+        + [pl.BlockSpec((block, x.shape[1]), lambda r, j: (r, 0)) for x in rights],
+        out_specs=[pl.BlockSpec((None, size, columns), lambda r, j: (jnp.where(r == steps - 1, j, 0), 0, 0))],
+        _explicit_indices=True,
+    )(left, *rights, parts)
+
+
+class ReduceWeight:
+    def __init__(self, links, spot, parts, slots, end, joined, mine, given, theirs):
+        self.links, self.spot = links, spot
+        self.parts, self.slots, self.end, self.joined = parts, slots, end, joined
+        self.mine, self.given, self.theirs = mine, given, theirs
+        self.shard = mine.shape[0]
+
+    def send(self, src, dst, to, sends=None, gets=None):
+        return self.links.copy(src, dst, self.spot.along(to), sends, gets).start()
+
+    def first(self):
+        at = self.spot.at
+        if self.spot.places == 4:
+            self.edges = [
+                self.send(self.parts.at[3], self.end, 1, at == 0, at == 1),
+                self.send(self.parts.at[1], self.end, 2, at == 3, at == 2),
+            ]
+
+    def second(self):
+        at, places, parts, slots = self.spot.at, self.spot.places, self.parts, self.slots
+        if places == 4:
+            inner = (at == 1) | (at == 2)
+            self.got = [
+                self.send(parts.at[1], slots.at[0], (at + 1) % 4, at < 3, at > 0),
+                self.send(parts.at[3], slots.at[1], (at + 3) % 4, at > 0, at < 3),
+                self.send(parts.at[2], slots.at[2], (at + 2) % 4, ~inner, inner),
+            ]
+        else:
+            self.got = [self.send(parts.at[j], slots.at[j - 1], (at + j) % places) for j in range(1, places)]
+
+    def third(self):
+        if self.spot.places != 4:
+            return
+        at = self.spot.at
+        inner = (at == 1) | (at == 2)
+        for edge in self.edges:
+            edge.get()
+        size, columns = self.parts.shape[1:]
+
+        def body(a, b, out):
+            out[...] = (a[...].astype(F32) + b[...].astype(F32)).astype(BF)
+
+        @pl.when(inner)
+        def _():
+            spec = pl.BlockSpec((self.shard, columns), lambda i: (i, 0))
+            pltpu.emit_pipeline(
+                body,
+                grid=(size // self.shard,),
+                in_specs=[pl.BlockSpec((None, self.shard, columns), lambda i: (2, i, 0)), spec],
+                out_specs=[spec],
+            )(self.parts, self.end, self.joined)
+
+        self.got.append(self.send(self.joined, self.slots.at[2], (at + 2) % 4, inner, ~inner))
+
+    def fourth(self):
+        spot = self.spot
+        at, places = spot.at, spot.places
+        for sent in self.got:
+            sent.get()
+        columns = self.parts.shape[2]
+
+        def body(own, *refs):
+            out = refs[-1]
+            total = own[...].astype(F32)
+            for k, ref in enumerate(refs[:-1]):
+                term = ref[...].astype(F32)
+                if places == 4 and k < 2:
+                    term = term * jnp.where(at > 0 if k == 0 else at < 3, 1.0, 0.0)
+                total = total + term
+            out[...] = total.astype(out.dtype)
+
+        def slot(k, part):
+            if places == 4 and k < 2:
+                k = jnp.where(at > 0, 0, 2) if k == 0 else jnp.where(at < 3, 1, 2)
+            return pl.BlockSpec((None, self.shard, columns), lambda i: (k, part, 0))
+
+        for part, out in ((1 - spot.half, self.given), (spot.half, self.mine)):
+            own = pl.BlockSpec((None, self.shard, columns), lambda i, part=part: (0, part, 0))
+            pltpu.emit_pipeline(
+                body,
+                grid=(1,),
+                in_specs=[own] + [slot(k, part) for k in range(places - 1)],
+                out_specs=[pl.BlockSpec((self.shard, columns), lambda i: (0, 0))],
+            )(self.parts, *[self.slots] * (places - 1), out)
+            if out is self.given:
+                self.mate = self.links.copy(self.given, self.theirs, spot.mate).start()
+
+    def finish(self):
+        self.mate.get()
+
+
+class ReduceRows:
+    def __init__(self, links, spot, factors, buffers, own):
+        self.links, self.spot, self.factors, self.own = links, spot, factors, own
+        self.given, self.got = buffers[:3], buffers[3:]
+        self.columns = factors[0][1].shape[0] // 2
+        self.sent = [[None, None] for _ in range(3)]
+
+    def block(self, part, n, twins):
+        spot = self.spot
+        g_own, x_own = (n // 2, n % 2) if part == 0 else (n % 2, n // 2)
+        other, x1 = 1 - spot.half, 1 - spot.chip
+        g = other + g_own * (spot.half - other)
+        x = x1 + x_own * (spot.chip - x1)
+        c = 1 - spot.core if twins else spot.core
+        return g * spot.nt + 2 * x + c
+
+    def added(self, stage):
+        return [((), (0,), (2, 0), (3, 1, 0))[stage][k] for k in range(stage)]
+
+    def run(self, stage, part, cut):
+        first, last = ((0, 4), (0, 2), (2, 3))[stage]
+        own, columns = self.own, self.columns
+        rows = own // cut
+        n_factors = len(self.factors)
+        for earlier in range(stage):
+            self.wait(earlier, part, stage)
+
+        def body(*refs):
+            ins, out = refs[:-1], refs[-1]
+            total = None
+            for k in range(n_factors):
+                term = lax.dot_general(ins[2 * k][...], ins[2 * k + 1][...], NT, preferred_element_type=F32)
+                total = term if total is None else total + term
+            for ref in ins[2 * n_factors :]:
+                total = total + ref[...].astype(F32)
+            out[...] = total.astype(BF)
+
+        in_specs, args = [], []
+        for a, b in self.factors:
+            depth = a.shape[1]
+            in_specs.append(
+                pl.BlockSpec(
+                    (rows, depth), lambda i: (self.block(part, first + i // cut, stage == 0) * cut + i % cut, 0)
+                )
+            )
+            in_specs.append(pl.BlockSpec((columns, depth), lambda i: (part, 0)))
+            args += [a, b]
+        for k, offset in enumerate(self.added(stage)):
+            in_specs.append(
+                pl.BlockSpec((None, rows, columns), lambda i, offset=offset: (part, offset * cut + i, 0))
+            )
+            args.append(self.got[k])
+        pltpu.emit_pipeline(
+            body,
+            grid=((last - first) * cut,),
+            in_specs=in_specs,
+            out_specs=[pl.BlockSpec((None, rows, columns), lambda i: (part, i, 0))],
+        )(*args, self.given[stage])
+        axes = (self.spot.mate, self.spot.across) if part == 0 else (self.spot.across, self.spot.mate)
+        device = self.spot.twin if stage == 0 else axes[stage - 1]
+        pieces = ((0, 2), (2, 1), (3, 1)) if stage == 0 else ((0, 1), (1, 1)) if stage == 1 else ((0, 1),)
+        sent = []
+        for at, count in pieces:
+            there = pl.ds(at * own, count * own)
+            sent.append(
+                self.links.copy(self.given[stage].at[part, there], self.got[stage].at[part, there], device).start()
+            )
+        self.sent[stage][part] = sent
+
+    def wait(self, earlier, part, stage):
+        self.sent[earlier][part][stage - earlier - 1].get()
+
+    def last(self, epilogue, ins, outs, cut):
+        own, columns = self.own, self.columns
+        rows = own // cut
+        n_factors = len(self.factors)
+        for part in (0, 1):
+            for earlier in range(3):
+                self.wait(earlier, part, 3)
+
+        def body(*refs):
+            mine, rest = refs[: 2 * n_factors], refs[2 * n_factors :]
+            total = None
+            for k in range(n_factors):
+                term = lax.dot_general(mine[2 * k][...], mine[2 * k + 1][...], NT, preferred_element_type=F32)
+                total = term if total is None else total + term
+            extra = []
+            for part in (0, 1):
+                terms = [ref[...].astype(F32) for ref in rest[3 * part : 3 * part + 3]]
+                extra.append(terms[0] + terms[1] + terms[2])
+            total = total + jnp.concatenate(extra, axis=1)
+            epilogue(total, rest[6 : 6 + len(ins)], rest[6 + len(ins) :])
+
+        in_specs, args = [], []
+        for a, b in self.factors:
+            depth = a.shape[1]
+            in_specs.append(pl.BlockSpec((rows, depth), lambda i: (self.block(0, 3, False) * cut + i, 0)))
+            in_specs.append(pl.BlockSpec((2 * columns, depth), lambda i: (0, 0)))
+            args += [a, b]
+        for part in (0, 1):
+            for k, offset in enumerate(self.added(3)):
+                in_specs.append(
+                    pl.BlockSpec(
+                        (None, rows, columns), lambda i, part=part, offset=offset: (part, offset * cut + i, 0)
+                    )
+                )
+                args.append(self.got[k])
+
+        def spec(ref):
+            if ref.shape[0] == 1:
+                return pl.BlockSpec(ref.shape, lambda i: (0, 0))
+            return pl.BlockSpec((rows, ref.shape[1]), lambda i: (i, 0))
+
+        pltpu.emit_pipeline(
+            body, grid=(cut,), in_specs=in_specs + [spec(r) for r in ins], out_specs=[spec(r) for r in outs]
+        )(*args, *ins, *outs)
+
+
+def output_rows(total, ins, outs):
+    x_ref, bias_ref = ins
+    outs[0][...] = (x_ref[...].astype(F32) + total + bias_ref[...]).astype(BF)
+
+
+def norm_rows(sums, total, ins, outs):
+    x_ref, g_ref, gain_ref = ins
+    x = x_ref[...].astype(F32)
+    gy = g_ref[...].astype(F32)
+    centred = x - jnp.mean(x, axis=1, keepdims=True)
+    rstd = lax.rsqrt(jnp.mean(centred * centred, axis=1, keepdims=True) + EPS)
+    x_hat = centred * rstd
+    scaled = total * gain_ref[...]
+    m1 = jnp.mean(scaled, axis=1, keepdims=True)
+    m2 = jnp.mean(scaled * x_hat, axis=1, keepdims=True)
+    outs[0][...] = rstd * (scaled - m1 - x_hat * m2) + gy
+    sums[0:1, :] += jnp.sum(total * x_hat, axis=0, keepdims=True)
+    sums[1:2, :] += jnp.sum(total, axis=0, keepdims=True)
+    sums[2:3, :] += jnp.sum(gy, axis=0, keepdims=True)
+
+
+SUMMED = 8
+
+
+def back_kernel(ndp, nt, *refs):
+    refs = list(refs)
+    take = lambda n: [refs.pop(0) for _ in range(n)]
+    h, gb, act, slope, o, da, wq, wd, w1, w2, x_own, g_own, gain, bias = take(14)
+    output, grad_x, small, gz = take(4)
+    weights = [take(7) for _ in range(3)]
+    row_buffers = [take(6) for _ in range(2)]
+    acc, sums, biases, line_got, pair_got, send, recv = take(7)
+    spot = Spot(ndp, nt)
+    links = Links(send, recv)
+    own = x_own.shape[0]
+    greet(spot.partners())
+    sums[...] = jnp.zeros(sums.shape, F32)
+    biases[...] = jnp.zeros(biases.shape, F32)
+
+    q_columns, f_columns = da.shape[1], act.shape[1]
+    reduce_2, reduce_q, reduce_1 = [
+        ReduceWeight(links, spot, parts, slots, end, joined, mine, given, theirs)
+        for mine, theirs, given, parts, slots, end, joined in weights
+    ]
+    branch = ReduceRows(links, spot, [(act, w2), (o, wd)], row_buffers[0], own)
+    grad = ReduceRows(links, spot, [(gz, w1), (da, wq)], row_buffers[1], own)
+
+    def outer(left, rights, target, columns, total=None):
+        outer_products(left, rights, target.parts, acc.at[:, :, pl.ds(0, columns)], spot, left.shape[0] // 2, total)
+
+    outer(h, [da], reduce_q, q_columns, biases.at[1:2, pl.ds(0, q_columns)])
+    reduce_q.first()
+    branch.run(0, 0, 1)
+    branch.run(0, 1, 1)
+    reduce_q.second()
+    branch.run(1, 0, 1)
+    branch.run(1, 1, 1)
+    reduce_q.third()
+    outer(gb, [act, o], reduce_2, f_columns + o.shape[1])
+    reduce_2.first()
+    by_rows(slope_body, [gb, w2, slope], [gz], own)
+    reduce_2.second()
+    grad.run(0, 0, 1)
+    grad.run(0, 1, 1)
+    branch.run(2, 0, 2)
+    branch.run(2, 1, 2)
+    reduce_2.third()
+    grad.run(1, 0, 1)
+    grad.run(1, 1, 1)
+    outer(h, [gz], reduce_1, f_columns, biases.at[0:1, pl.ds(0, f_columns)])
+    reduce_1.first()
+    reduce_q.fourth()
+    reduce_1.second()
+    branch.last(output_rows, [x_own, bias], [output], 2)
+    grad.run(2, 0, 2)
+    grad.run(2, 1, 2)
+    reduce_1.third()
+    reduce_2.fourth()
+    reduce_q.finish()
+    grad.last(functools.partial(norm_rows, sums), [x_own, g_own, gain], [grad_x], 2)
+    reduce_1.fourth()
+
+    sums[SUMMED // 2 : SUMMED // 2 + 2, :] = biases[...]
+    places = spot.places
+    line_got[0] = sums[...]
+    got = [links.copy(sums, line_got.at[j], spot.along((spot.at + j) % places)).start() for j in range(1, places)]
+    for sent in got:
+        sent.get()
+    for sent in got:
+        sent.drain()
+    total = line_got[spot.at]
+    for place in range(1, places):
+        total = total + line_got[(spot.at + places - place) % places]
+    sums[...] = total
+    row = lax.broadcasted_iota(jnp.int32, sums.shape, 0)
+    for k, device in enumerate((spot.mate, spot.across, spot.twin)):
+        sent = links.copy(sums, pair_got.at[k], device).start()
+        sent.get()
+        sent.drain()
+        theirs = pair_got[k]
+        if k == 0:
+            small[1] = theirs
+        sums[...] = sums[...] + jnp.where(row < SUMMED // 2, theirs, 0.0)
+    small[0] = sums[...]
+    reduce_2.finish()
+    reduce_1.finish()
+    links.finish()
+
+
+def back_call(ndp, nt, h, gb, act, slope, o, da, wq, wd, w1, w2, x_own, g_own, gain, bias):
+    own, width = x_own.shape
+    rows = h.shape[0]
+    places = ndp // 2
+    size, shard = width // places, width // ndp
+    q3, f, q = wq.shape[1], w1.shape[1], wd.shape[1]
+    shape = lambda *s: jax.ShapeDtypeStruct(s, BF)
+    full = lambda *s: jax.ShapeDtypeStruct(s, F32)
+    out_shape = [shape(own, width), full(own, width), full(2, SUMMED, width), shape(rows, f)]
+    for n in (f + q, q3, f):
+        out_shape += [full(shard, n), shape(shard, n), shape(shard, n)]
+        out_shape += [shape(places, size, n), shape(places - 1, size, n), shape(size, n), shape(size, n)]
+    for _ in range(2):
+        out_shape += [shape(2, k * own, width // 2) for k in (4, 2, 1)] * 2
+    anywhere = pl.BlockSpec(memory_space=pl.ANY)
+    out_specs = [anywhere] * len(out_shape)
+    out_specs[2] = pl.BlockSpec(memory_space=pltpu.VMEM)
+    transfers = 3 * (1 + max(6, places)) + 2 * 2 * 6 + places + 3
     return pl.pallas_call(
-        slope_body,
-        grid=(total // block,),
-        in_specs=[
-            pl.BlockSpec((block, depth), lambda i: (i, 0)),
-            pl.BlockSpec((depth, columns), lambda i: (0, 0)),
-            pl.BlockSpec((block, columns), lambda i: (i, 0)),
+        functools.partial(back_kernel, ndp, nt),
+        in_specs=[anywhere] * 14,
+        out_specs=out_specs,
+        out_shape=out_shape,
+        scratch_shapes=[
+            pltpu.VMEM((places, size, f + q), F32),
+            pltpu.VMEM((SUMMED, width), F32),
+            pltpu.VMEM((2, width), F32),
+            pltpu.VMEM((places, SUMMED, width), F32),
+            pltpu.VMEM((3, SUMMED, width), F32),
+            pltpu.SemaphoreType.DMA((transfers,)),
+            pltpu.SemaphoreType.DMA((transfers,)),
         ],
-        out_specs=pl.BlockSpec((block, columns), lambda i: (i, 0)),
-        out_shape=jax.ShapeDtypeStruct((total, columns), BF),
-        compiler_params=pltpu.CompilerParams(vmem_limit_bytes=VMEM),
-        cost_estimate=COST,
-    )(rows, w, slope)
-
-
-def rows_kernel(count, terms, added, dtype, index_ref, *refs):
-    ins, outs = refs[:-2], refs[-2:]
-    i = pl.program_id(0)
-    acc = lax.dot_general(ins[0][...], ins[1][...], NT, preferred_element_type=F32)
-    for n in range(1, terms):
-        acc = acc + lax.dot_general(ins[2 * n][...], ins[2 * n + 1][...], NT, preferred_element_type=F32)
-    for part in (0, 1):
-        @pl.when(i // count == part)
-        def _():
-            total = acc
-            first = 2 * terms + part * added
-            for ref in ins[first : first + added]:
-                total = total + ref[...].astype(F32)
-            outs[part][...] = total.astype(dtype)
-
-
-def rows_call(index, factors, added, block, dtype):
-    count = len(index[0])
-    columns = factors[0][1].shape[0] // 2
-    in_specs, args = [], []
-    for a, b in factors:
-        depth = a.shape[1]
-        in_specs.append(pl.BlockSpec((block, depth), lambda i, index: (index[i], 0)))
-        in_specs.append(pl.BlockSpec((columns, depth), lambda i, index: (i // count, 0)))
-        args += [a, b]
-    places = (lambda i: jnp.minimum(i, count - 1), lambda i: jnp.maximum(i - count, 0))
-    for part in (0, 1):
-        for a, first in added[part]:
-            spec = pl.BlockSpec(
-                (block, columns), lambda i, index, first=first, part=part: (first + places[part](i), 0)
-            )
-            in_specs.append(spec)
-            args.append(a)
-    return pl.pallas_call(
-        functools.partial(rows_kernel, count, len(factors), len(added[0]), dtype),
-        grid_spec=pltpu.PrefetchScalarGridSpec(
-            num_scalar_prefetch=1,
-            grid=(2 * count,),
-            in_specs=in_specs,
-            out_specs=[
-                pl.BlockSpec((block, columns), lambda i, index: (places[0](i), 0)),
-                pl.BlockSpec((block, columns), lambda i, index: (places[1](i), 0)),
-            ],
-        ),
-        out_shape=[jax.ShapeDtypeStruct((count * block, columns), dtype)] * 2,
-        compiler_params=pltpu.CompilerParams(vmem_limit_bytes=VMEM),
-        cost_estimate=COST,
-    )(jnp.stack(index[0] + index[1]).astype(jnp.int32), *args)
+        compiler_params=pltpu.CompilerParams(collective_id=1, has_side_effects=True, vmem_limit_bytes=VMEM),
+    )(h, gb, act, slope, o, da, wq, wd, w1, w2, x_own, g_own, gain, bias)
 
 
 def local(
@@ -729,82 +956,25 @@
     bias_q = pick(b_qkv.reshape(3, 2, pairs, LANES).transpose(1, 2, 0, 3), half).reshape(1, 3 * q_width)
     bias_1 = pick(b_fc1.reshape(2, f_width), half)[None]
 
-    def weight_out(total, *earlier):
-        total = total.reshape(2, shard, total.shape[1])
-        theirs = swap(pick(total, other).astype(BF), "dp", 1)
-        return pick(total, half), theirs
+    h, gb, wq_all, w1_all, wd_all, w2_all, qkv, o_float, o, lse, act, slope, go, da = front_call(
+        ndp, nt, h_own, gb_own, [wq, w1, wd, w2], [bias_q, bias_1], [cosine, sine, aq, ak]
+    )
+    made = back_call(
+        ndp, nt, h, gb, act, slope, o, da, wq_all, wd_all, w1_all, w2_all, layer_input, gb_own, ln_gain[None],
+        (b_dense + b_fc2)[None],
+    )
+    output, grad_x, small = made[:3]
 
     def both(mine, theirs):
         theirs = theirs.astype(F32)
         return jnp.stack([jnp.where(half == 0, mine, theirs), jnp.where(half == 0, theirs, mine)])
 
-    name = lambda g, x, c: g * nt + 2 * x + c
-    p0, p1, x0, x1 = half, other, chip, 1 - chip
-    targets = ([(p1, x1), (p1, x0), (p0, x1), (p0, x0)], [(p1, x1), (p0, x1), (p1, x0), (p0, x0)])
-    axes = ((("dp", 1), ("tensor", 2)), (("tensor", 2), ("dp", 1)))
-
-    def scatter(stage, factors, got, *earlier):
-        if earlier:
-            factors = [(after(factors[0][0], *earlier), factors[0][1])] + factors[1:]
-        first, last = ((0, 4), (0, 2), (2, 3), (3, 4))[stage]
-        c = 1 - core if stage == 0 else core
-        index = [[name(g, x, c) for g, x in target[first:last]] for target in targets]
-        offsets = ((), (0,), (2, 0), (3, 1, 0))[stage]
-        added = [[(got[n][part], offsets[n]) for n in range(stage)] for part in (0, 1)]
-        outs = rows_call(index, factors, added, own, F32 if stage == 3 else BF)
-        if stage == 3:
-            return outs
-        if stage == 0:
-            return [swap(x, "tensor", 1) for x in outs]
-        return [swap(x, *axes[part][stage - 1]) for part, x in enumerate(outs)]
-
-    h, gb, wq_all, w1_all, wd_all, w2_all, qkv, o_float, o, lse, act, slope, go, da = front_call(
-        ndp, nt, h_own, gb_own, [wq, w1, wd, w2], [bias_q, bias_1], [cosine, sine, aq, ak]
-    )
-    g2 = outer_call(gb, [act, o], at, places)
-    g2_begun = first_terms(g2, places)
-    gz = slope_call(after(gb, g2[0]), w2_all, slope, own)
-    g2_joined = join_terms(g2, g2_begun, places, gz)
-    branch_by, grad_by = [(act, w2_all), (o, wd_all)], [(gz, w1_all)]
-    branch = [scatter(0, branch_by, [], gz)]
-    g1 = outer_call(after(h, gz, branch_by[0][0]), [gz], at, places)
-    g1_begun = first_terms(g1, places)
-    g2_out = weight_out(last_terms(g2, g2_begun, g2_joined, places, g1[0]))
-    branch.append(scatter(1, branch_by, branch, g1[0], g2_out[0]))
-    grad_by.append((da, wq_all))
-    grad = [scatter(0, grad_by, [], g2_out[0])]
-    g1_joined = join_terms(g1, g1_begun, places, grad[0][0])
-    branch.append(scatter(2, branch_by, branch, grad[0][0]))
-    gq = outer_call(after(h, branch[2][0]), [da], at, places)
-    gq_begun = first_terms(gq, places)
-    grad.append(scatter(1, grad_by, grad, gq[0]))
-    g1_out = weight_out(last_terms(g1, g1_begun, g1_joined, places, gq[0]))
-    gq_joined = join_terms(gq, gq_begun, places, g1_out[0])
-    branch = jnp.concatenate(scatter(3, branch_by, branch, gq[0]), axis=1)
-    output = (xf + branch + b_dense + b_fc2).astype(BF)
-    grad.append(scatter(2, grad_by, grad, output))
-    gq_out = weight_out(last_terms(gq, gq_begun, gq_joined, places))
-    dn = jnp.concatenate(scatter(3, grad_by, grad), axis=1)
-
-    scaled = dn * ln_gain
-    m1 = jnp.mean(scaled, axis=1, keepdims=True)
-    m2 = jnp.mean(scaled * x_hat, axis=1, keepdims=True)
-    grad_x = rstd * (scaled - m1 - x_hat * m2) + gy
-
-    def spread(x):
-        return place(jnp.zeros((2,) + x.shape, F32), x, half).reshape(-1)
-
-    late = everywhere(jnp.stack([jnp.sum(dn * x_hat, axis=0), jnp.sum(dn, axis=0)]), ("tensor", "dp"))
-    early = everywhere(jnp.sum(gy, axis=0, keepdims=True), ("tensor", "dp"))[0]
-    g_b1 = spread(jnp.sum(gz, axis=0, dtype=F32))
-    g_bq = spread(jnp.sum(da, axis=0, dtype=F32))
-    g_biases = everywhere(jnp.concatenate([g_b1, g_bq])[None], ("dp",))[0]
-    g_b1 = g_biases[: 2 * f_width]
-    g_bq = g_biases[2 * f_width :].reshape(2, pairs, 3, LANES).transpose(2, 0, 1, 3).reshape(3, 2 * q_width)
-
-    g_2 = both(*g2_out)
+    g_2, g_wq, g_w1 = [both(made[k], made[k + 1]) for k in (4, 11, 18)]
     g_w2, g_wd = g_2[:, :, :f_width], g_2[:, :, f_width:]
-    g_w1, g_wq = both(*g1_out), both(*gq_out)
+    late, early = small[0, :2], small[0, 2]
+    g_biases = both(small[0, SUMMED // 2 : SUMMED // 2 + 2], small[1, SUMMED // 2 : SUMMED // 2 + 2])
+    g_b1 = g_biases[:, 0, :f_width].reshape(-1)
+    g_bq = g_biases[:, 1, : 3 * q_width].reshape(2, pairs, 3, LANES).transpose(2, 0, 1, 3).reshape(3, 2 * q_width)
     out_wq = g_wq.reshape(2, shard, pairs, 3, LANES).transpose(1, 3, 0, 2, 4).reshape(shard, 3, 2 * q_width)
     out_wd = g_wd.transpose(0, 2, 1).reshape(2 * q_width, shard)
     out_w1 = g_w1.transpose(1, 0, 2).reshape(shard, 2 * f_width)

time: 924 us -> 706 us (0.76)
  waiting for transfers between devices: 164 us -> 0.01 us
  starting transfers between devices: 81.7 us -> 3.03 us
  Pallas kernels: 540 us -> 608 us
  other arithmetic: 71.4 us -> 33.2 us
    ppermute x43 -> x1, waiting for transfers between devices: 116 us -> 0.01 us  [swap(): return lax.ppermute(x, axis, [(i, i ^ bit) for i in range(size)])]
    pallas_call x12 -> x1, Pallas kernels: 229 us -> 297 us  [back_call(): pl.pallas_call(functools.partial(back_kernel, ndp, nt), in_specs=[anywher...]
    ppermute x43 -> x1, starting transfers between devices: 52.6 us -> 3.03 us  [swap(): return lax.ppermute(x, axis, [(i, i ^ bit) for i in range(size)])]
    ppermute x15 -> x0, waiting for transfers between devices: 48.1 us -> none  [line(): lax.ppermute(x, 'dp', [(2 * i + s, 2 * j + s) for i, j in pairs for s in...]
    ppermute x15 -> x0, starting transfers between devices: 29.1 us -> none  [line(): lax.ppermute(x, 'dp', [(2 * i + s, 2 * j + s) for i, j in pairs for s in...]
    reduce_sum x4 -> x0, other arithmetic: 14.3 us -> none  [the longest x1 4.6 us: local(): g_b1 = spread(jnp.sum(gz, axis=0, dtype=F32))]
    convert_element_type x4 -> x0, other arithmetic: 11.7 us -> none  [the longest x3 7.31 us: join_terms(): joined = add(parts[2], after(begun[0], *earlier), begun[1]).astype(BF)]
  transfers between devices with their start and end apart: 58 -> 1, of which waited for: 12 -> 0; matrix products, arithmetic and copies ran while one was open for 8% -> 3% of each run, Pallas kernels for 19% -> 0%
where the time goes in v3:
time: 706 us; the launch traced here: 701 us
  Pallas kernels  608 us (86%)
  local copies, waits for them, and re-layouts  55.6 us (8%)
  other arithmetic  33.2 us (5%)
    pallas_call x1, Pallas kernels, front_call(): pl.pallas_call(functools.partial(front_kernel, ndp, nt), in_specs=[anywhe...  311 us
    pallas_call x1, Pallas kernels, back_call(): pl.pallas_call(functools.partial(back_kernel, ndp, nt), in_specs=[anywher...  297 us
    unnamed x39, local copies, waits for them, and re-layouts  15.5 us
  transfers between devices with their start and end apart: 1, of which 0 were waited for; matrix products, arithmetic and copies ran while one was open for 3% of the time, Pallas kernels for 0%

profile of v3, /device:TPU:0, one launch (start us, length us, event | category | flops | bytes accessed | tf_op | source)
XLA Modules:
  0.0 700.7 jit_solution(5488441763909246612)
XLA Ops:
  0.7 3.0 collective-permute-start
  5.1 2.0 convert_reduce_fusion
  16.3 2.3 copy.79
  19.9 4.7 fusion.5
  25.4 9.5 %multiply_sine_fusion = (f32[4096,16]{1,0:T(8,128)}, f32[4096,16]{1,0:T(8,128)}, f32[4096,16]{1,0:T(8,128)S(1)}) fusion(f32[16]{0:T(128)S(1)} %multiply_exponential_fusion, f32[4096]{0:T(1024)S(1)} %bitcast.70), kind=kLoop, calls=%fused_computation.9 | loop fusion | flops 131072 | bytes 802880 | tf_op jit(solution)/shard_map/sin | solution.py:946
  34.9 1.5 add.81
  36.4 7.5 %concatenate.11.refs_8_ = f32[4096,128]{1,0:T(8,128)} concatenate(f32[4096,16]{1,0:T(8,128)S(1)} %get-tuple-element.113, f32[4096,16]{1,0:T(8,128)S(1)} %get-tuple-element.113, f32[4096,32]{1,0:T(8,128)} %add.81, f32[4096,16]{1,0:T(8,128)S(1)} %get-tuple-element.113, f32[4096,16]{1,0:T(8,128)S(1)} %get-tuple-element.113, f32[4096,32]{1,0:T(8,128)} %add.81), dimensions={1} | concatenate | bytes 4194304 | tf_op jit(solution)/shard_map/concatenate | solution.py:948
  43.9 1.5 broadcast_in_dim.52
  46.3 8.8 %concatenate.12.refs_9_ = f32[4096,128]{1,0:T(8,128)} concatenate(f32[4096,16]{1,0:T(8,128)} %get-tuple-element.112, f32[4096,16]{1,0:T(8,128)S(1)} %copy-done.3, f32[4096,32]{1,0:T(8,128)} %broadcast_in_dim.52, f32[4096,16]{1,0:T(8,128)} %get-tuple-element.112, f32[4096,16]{1,0:T(8,128)S(1)} %copy-done.3, f32[4096,32]{1,0:T(8,128)} %broadcast_in_dim.52), dimensions={1} | concatenate | bytes 4194304 | tf_op jit(solution)/shard_map/concatenate | solution.py:949
  55.0 2.9 select_convert_fusion
  58.0 310.8 %shard_map.220 = (bf16[4096,2048]{1,0:T(8,128)(2,1)}, bf16[4096,2048]{1,0:T(8,128)(2,1)}, bf16[2048,768]{1,0:T(8,128)(2,1)}, bf16[2048,1024]{1,0:T(8,128)(2,1)},...) custom-call(bf16[512,2048]{1,0:T(8,128)(2,1)} %get-tuple-element.116, ...), custom_call_target="tpu_custom_call" | custom-call | tf_op jit(solution)/shard_map/pallas_call | solution.py:376
  368.8 296.8 %shard_map.221 = (bf16[512,2048]{1,0:T(8,128)(2,1)}, f32[512,2048]{1,0:T(8,128)}, f32[2,8,2048]{2,1,0:T(8,128)}, bf16[4096,1024]{1,0:T(8,128)(2,1)}, f32[256,128...) custom-call(bf16[4096,2048]{1,0:T(8,128)(2,1)} %get-tuple-element.31, ...), custom_call_target="tpu_custom_call" | custom-call | tf_op jit(solution)/shard_map/pallas_call | solution.py:871
  665.6 1.6 fusion.16
  668.7 1.7 fusion.9
  671.3 2.2 convert_select_fusion.5
  673.5 2.3 copy.84
  677.0 1.5 maximum_bitcast_fusion.1
  679.9 3.1 copy.90
  682.9 1.5 fusion.11
  685.9 2.9 copy.88
  688.8 2.9 copy.91
  691.6 1.8 copy.89
  695.1 3.3 copy.100
  698.4 2.0 copy.101
  (74 shorter events, 21.3 us)
Async XLA Ops:
  0.6 7.3 %copy-start = (f32[3,512]{1,0:T(4,128)S(1)}, f32[3,512]{1,0:T(4,128)}, u32[]{:S(2)}) copy-start(f32[3,512]{1,0:T(4,128)} %param.18) | copy-start | bytes 18436
  0.7 6.5 copy-start.2
  0.7 23.9 %collective-permute-start = (s32[1,4]{1,0:T(1,128)}, s32[1,4]{1,0:T(1,128)S(1)}, u32[]{:S(2)}, u32[]{:S(2)}) collective-permute-start(s32[1,4]{1,0:T(1,128)} %param.14), channel_id=1, source_target_pairs={{0,4},{4,0},{8,12},{12,8},{16,20},{20,16},{24,28},{28,24},{1,5},{5... | collective-permute-start | bytes 56 | tf_op jit(solution)/shard_map/ppermute | solution.py:26
  5.1 2.8 copy-start.14
  5.1 3.5 copy-start.12
  5.1 4.1 copy-start.7
  5.1 4.9 copy-start.5
  15.0 4.3 copy-start.10
  15.0 4.3 copy-start.11
  15.0 4.9 copy-start.9
  15.0 4.9 copy-start.13
  43.9 2.3 copy-start.3
  667.2 27.3 %copy-start.8 = (f32[1,1,2048]{2,1,0:T(1,128)}, f32[1,1,2048]{2,1,0:T(1,128)S(1)}, u32[]{:S(2)}) copy-start(f32[1,1,2048]{2,1,0:T(1,128)S(1)} %get-tuple-element.104) | copy-start | bytes 24580
  679.9 3.1 copy-start.6
  695.1 3.3 copy-start.4
  698.4 2.0 copy-start.1

commit v4 on v3

--- a/solution.py
+++ b/solution.py
@@ -19,11 +19,6 @@
 TN = (((0,), (0,)), ((), ()))
 VMEM = 56 * 2**20
 COST = pl.CostEstimate(flops=0, bytes_accessed=0, transcendentals=0)
-
-
-def swap(x, axis, bit):
-    size = lax.axis_size(axis)
-    return lax.ppermute(x, axis, [(i, i ^ bit) for i in range(size)])
 
 
 def pick(x, index):
@@ -153,91 +148,97 @@
 
 
 class GatherRows:
+    def __init__(self, links, spot, whole, size):
+        self.whole, self.size = whole, size
+        low = size // 4
+        near, across, mate, far = [spot.block(g, x, 0) for g, x in ((0, 0), (0, 1), (1, 0), (1, 1))]
+        made = lambda block, device, first=0, count=size: links.copy(
+            self.rows(block, first, count), self.rows(block, first, count), device
+        )
+        self.x, self.y = made(near, spot.across), made(near, spot.mate)
+        self.low = made(across, spot.mate, 0, low)
+        self.high = made(mate, spot.across, low, size - low)
+        self.near_twin, self.x_twin, self.y_twin = [made(n, spot.twin) for n in (near, across, mate)]
+        self.low_twin = made(far, spot.twin, 0, low)
+        self.high_twin = made(far, spot.twin, low, size - low)
+
+    def rows(self, block, first, count):
+        return self.whole.at[pl.ds(pl.multiple_of(block * self.size, self.size) + first, count)]
+
+    def first(self):
+        self.x.start()
+        self.y.start()
+        self.near_twin.start()
+
+    def second(self):
+        self.x.get()
+        self.low.start()
+        self.x_twin.start()
+        self.y.get()
+        self.high.start()
+        self.y_twin.start()
+
+    def third(self):
+        self.low.get()
+        self.low_twin.start()
+        self.high.get()
+        self.high_twin.start()
+
+    def finish_near(self):
+        self.near_twin.get()
+        self.x_twin.get()
+
+    def finish(self):
+        for part in (self.y_twin, self.low_twin, self.high_twin):
+            part.get()
+
+
+class GatherWeight:
     def __init__(self, links, spot, own, whole, sem):
-        self.links, self.spot, self.whole, self.own = links, spot, whole, own
-        self.size = own.shape[0]
-        self.mid = self.size // 4
-        self.local = pltpu.make_async_copy(own, self.rows(spot.block(0, 0, 0)), sem)
-
-    def rows(self, block, first=0, count=None):
-        at = pl.multiple_of(block * self.size, self.size) + first
-        return self.whole.at[pl.ds(at, count or self.size)]
-
-    def forward(self, block, device, first=0, count=None):
-        place = self.rows(block, first, count)
-        return self.links.copy(place, place, device).start()
-
-    def first(self):
-        spot = self.spot
-        self.local.start()
-        place = self.rows(spot.block(0, 0, 0))
-        self.x = self.links.copy(self.own, place, spot.across).start()
-        self.y = self.links.copy(self.own, place, spot.mate).start()
-        self.parts = [self.links.copy(self.own, place, spot.twin).start()]
-
-    def second(self):
-        spot, rest = self.spot, self.size - self.mid
-        self.x.get()
-        self.low = self.forward(spot.block(0, 1, 0), spot.mate, 0, self.mid)
-        self.parts.append(self.forward(spot.block(0, 1, 0), spot.twin))
-        self.y.get()
-        self.high = self.forward(spot.block(1, 0, 0), spot.across, self.mid, rest)
-        self.parts.append(self.forward(spot.block(1, 0, 0), spot.twin))
-
-    def third(self):
-        spot, rest = self.spot, self.size - self.mid
-        self.low.get()
-        self.parts.append(self.forward(spot.block(1, 1, 0), spot.twin, 0, self.mid))
-        self.high.get()
-        self.parts.append(self.forward(spot.block(1, 1, 0), spot.twin, self.mid, rest))
-
-    def finish(self):
-        self.local.wait()
-        for part in self.parts:
-            part.get()
-
-
-class GatherWeight:
-    def __init__(self, links, spot, halves, whole, sem):
-        self.links, self.spot, self.halves, self.whole = links, spot, halves, whole
-        self.shard = halves.shape[1]
-        at = pl.multiple_of((2 * spot.at + spot.half) * self.shard, self.shard)
-        self.place = whole.at[pl.ds(at, self.shard)]
-        self.local = pltpu.make_async_copy(halves.at[spot.half], self.place, sem)
+        self.spot, self.whole = spot, whole
+        self.shard, columns = own.shape[0], whole.shape[1]
+        at, places = spot.at, spot.places
+        half = lambda k: own.at[:, pl.ds(pl.multiple_of(k * columns, columns), columns)]
+        place = whole.at[pl.ds(pl.multiple_of((2 * at + spot.half) * self.shard, self.shard), self.shard)]
+        self.local = pltpu.make_async_copy(half(spot.half), place, sem)
+        self.y = links.copy(half(1 - spot.half), place, spot.mate)
+        made = lambda n, to, sends=None, gets=None: links.copy(
+            self.pair(n), self.pair(n), spot.along(to), sends, gets
+        )
+        if places == 4:
+            inner = (at == 1) | (at == 2)
+            self.two = made(at, (at + 2) % 4)
+            self.parts = [made(at, (at + 1) % 4, at < 3, at > 0), made(at, (at + 3) % 4, at > 0, at < 3)]
+            self.three = made((at + 2) % 4, 3 * (at // 2), inner, ~inner)
+        else:
+            self.parts = [made(at, (at + j) % places) for j in range(1, places)]
 
     def pair(self, place):
-        return self.whole.at[pl.ds(pl.multiple_of(place * 2 * self.shard, 2 * self.shard), 2 * self.shard)]
-
-    def forward(self, place, to, sends=None, gets=None):
-        return self.links.copy(self.pair(place), self.pair(place), self.spot.along(to), sends, gets).start()
+        rows = 2 * self.shard
+        return self.whole.at[pl.ds(pl.multiple_of(place * rows, rows), rows)]
 
     def first(self):
         self.local.start()
-        self.y = self.links.copy(self.halves.at[1 - self.spot.half], self.place, self.spot.mate).start()
+        self.y.start()
 
     def second(self):
-        at, places = self.spot.at, self.spot.places
         self.local.wait()
         self.y.get()
-        if places == 4:
-            self.two = self.forward(at, (at + 2) % 4)
-            self.parts = [
-                self.forward(at, (at + 1) % 4, at < 3, at > 0),
-                self.forward(at, (at + 3) % 4, at > 0, at < 3),
-            ]
-        else:
-            self.parts = [self.forward(at, (at + j) % places) for j in range(1, places)]
+        if self.spot.places == 4:
+            self.two.start()
+        for part in self.parts:
+            part.start()
 
     def third(self):
-        at = self.spot.at
         if self.spot.places == 4:
             self.two.get()
-            inner = (at == 1) | (at == 2)
-            self.parts.append(self.forward((at + 2) % 4, 3 * (at // 2), inner, ~inner))
+            self.three.start()
 
     def finish(self):
         for part in self.parts:
             part.get()
+        if self.spot.places == 4:
+            self.three.get()
 
 
 def qkv_body(h_ref, w_ref, b_ref, cos_ref, sin_ref, out_ref):
@@ -270,7 +271,7 @@
     out_ref[...] = (acc * slope_ref[...].astype(F32)).astype(BF)
 
 
-def by_rows(body, ins, outs, block, first=0, count=None):
+def by_rows(body, ins, outs, block, first=0, count=None, events=None):
     total = outs[0].shape[0]
     count = count or total // block
 
@@ -280,8 +281,17 @@
             return pl.BlockSpec((block, width), lambda i: (first + i, 0))
         return pl.BlockSpec(ref.shape, lambda i: (0, 0))
 
+    def stepped(step, *refs):
+        for k, event in (events or {}).items():
+            pl.when(step.index[0] == k)(event)
+        body(*refs)
+
     pltpu.emit_pipeline(
-        body, grid=(count,), in_specs=[spec(r) for r in ins], out_specs=[spec(r) for r in outs]
+        stepped,
+        grid=(count,),
+        in_specs=[spec(r) for r in ins],
+        out_specs=[spec(r) for r in outs],
+        _explicit_indices=True,
     )(*ins, *outs)
 
 
@@ -300,94 +310,60 @@
     )(*wide_ins, *aug_ins, *ins, *outs)
 
 
-def front_kernel(ndp, nt, *refs):
-    refs = list(refs)
-    take = lambda n: [refs.pop(0) for _ in range(n)]
-    h_own, gb_own, wq2, w12, wd2, w22, bias_q, bias_1, cosine, sine, aq, ak = take(12)
-    h, gb, wq, w1, wd, w2, qkv, o_float, o, lse, act, slope, go, da = take(14)
-    dk_s, dv_s, dqt_s, local_sem, send, recv = take(6)
-    spot = Spot(ndp, nt)
-    links = Links(send, recv)
-    group = h.shape[0] // 2
-    own = h_own.shape[0]
-    greet(spot.partners())
-
-    rows_h = GatherRows(links, spot, h_own, h, local_sem.at[0])
-    rows_gb = GatherRows(links, spot, gb_own, gb, local_sem.at[1])
-    gather_q = GatherWeight(links, spot, wq2, wq, local_sem.at[2])
-    gather_1 = GatherWeight(links, spot, w12, w1, local_sem.at[3])
-    gather_d = GatherWeight(links, spot, wd2, wd, local_sem.at[4])
-    gather_2 = GatherWeight(links, spot, w22, w2, local_sem.at[5])
-
-    gather_q.first()
-    rows_h.first()
-    gather_1.first()
-    gather_q.second()
-    rows_h.second()
-    gather_q.third()
-    gather_1.second()
-    rows_h.third()
-    gather_q.finish()
-    rows_gb.first()
-    gather_d.first()
-    gather_2.first()
-    rows_h.finish()
-    by_rows(qkv_body, [h, wq, bias_q, cosine, sine], [qkv], own)
-    attend = functools.partial(attend_kernel, group, 512)
-    by_heads(attend, [qkv], [], [aq, ak], [o_float, o, lse], group, 0)
-    gather_1.third()
-    gather_d.second()
-    by_heads(attend, [qkv], [], [aq, ak], [o_float, o, lse], group, 1)
-    rows_gb.second()
-    gather_2.second()
-    gather_1.finish()
-    steps = 2 * group // own
-    by_rows(gelu_body, [h, w1, bias_1], [act, slope], own, 0, steps // 2)
-    rows_gb.third()
-    gather_d.third()
-    by_rows(gelu_body, [h, w1, bias_1], [act, slope], own, steps // 2, steps // 2)
-    rows_gb.finish()
-    gather_d.finish()
-    by_rows(plain_body, [gb, wd], [go], own)
-    back = functools.partial(attend_back_kernel, group, 256)
-
-    def attend_back(qkv_ref, aq_ref, ak_ref, cos_ref, sin_ref, o_ref, lse_ref, go_ref, out_ref):
-        back(qkv_ref, aq_ref, ak_ref, o_ref, lse_ref, go_ref, cos_ref, sin_ref, out_ref, dk_s, dv_s, dqt_s)
-
-    by_heads(attend_back, [qkv], [o_float, lse, go], [aq, ak, cosine, sine], [da], group, 0)
-    gather_2.third()
-    by_heads(attend_back, [qkv], [o_float, lse, go], [aq, ak, cosine, sine], [da], group, 1)
-    gather_2.finish()
-    links.finish()
-
-
-def front_call(ndp, nt, h_own, gb_own, weights, biases, tables):
-    own, width = h_own.shape
-    rows = 2 * nt * own
-    q3, f, q = weights[0].shape[2], weights[1].shape[2], weights[2].shape[2]
-    shape = lambda a, b, dtype=BF: jax.ShapeDtypeStruct((a, b), dtype)
-    out_shape = [shape(rows, width), shape(rows, width)]
-    out_shape += [shape(width, n) for n in (q3, f, q, f)]
-    out_shape += [shape(rows, q3), shape(rows, q, F32), shape(rows, q), shape(rows, q, F32)]
-    out_shape += [shape(rows, f), shape(rows, f), shape(rows, q), shape(rows, q3)]
-    anywhere = pl.BlockSpec(memory_space=pl.ANY)
-    group = nt * own
-    transfers = 2 * 10 + 4 * (1 + max(4, ndp // 2))
-    return pl.pallas_call(
-        functools.partial(front_kernel, ndp, nt),
-        in_specs=[anywhere] * 12,
-        out_specs=[anywhere] * 14,
-        out_shape=out_shape,
-        scratch_shapes=[
-            pltpu.VMEM((group, LANES), F32),
-            pltpu.VMEM((group, LANES), F32),
-            pltpu.VMEM((LANES, group), F32),
-            pltpu.SemaphoreType.DMA((6,)),
-            pltpu.SemaphoreType.DMA((transfers,)),
-            pltpu.SemaphoreType.DMA((transfers,)),
-        ],
-        compiler_params=pltpu.CompilerParams(collective_id=0, has_side_effects=True, vmem_limit_bytes=VMEM),
-    )(h_own, gb_own, *weights, *biases, *tables)
+def norm_inputs(spot, x_own, g_own, gain, shift, lens, h, gb, cut):
+    own = x_own.shape[0]
+    rows = own // cut
+
+    def body(step, x_ref, g_ref, gain_ref, shift_ref, h_ref, gb_ref):
+        x = x_ref[...].astype(F32)
+        centred = x - jnp.mean(x, axis=1, keepdims=True)
+        rstd = lax.rsqrt(jnp.mean(centred * centred, axis=1, keepdims=True) + EPS)
+        h_ref[...] = (centred * rstd * gain_ref[...] + shift_ref[...]).astype(BF)
+        used = jnp.sum(lens[0:1, :], axis=1, keepdims=True)
+        row = lax.broadcasted_iota(jnp.int32, (rows, 1), 0) + (spot.t * own + step.index[0] * rows)
+        gb_ref[...] = jnp.where(row.astype(F32) < used, g_ref[...].astype(F32), 0.0).astype(BF)
+
+    wide = pl.BlockSpec((rows, x_own.shape[1]), lambda i: (i, 0))
+    one = pl.BlockSpec(gain.shape, lambda i: (0, 0))
+    there = pl.BlockSpec((rows, x_own.shape[1]), lambda i: (spot.block(0, 0, 0) * cut + i, 0))
+    pltpu.emit_pipeline(
+        body, grid=(cut,), in_specs=[wide, wide, one, one], out_specs=[there, there], _explicit_indices=True
+    )(x_own, g_own, gain, shift, h, gb)
+
+
+def make_tables(spot, lens, count, inverse, cosine, sine, aq, ak, block):
+    total = cosine.shape[0]
+    steps = total // 2 // block
+
+    def body(step, inverse_ref, cos_ref, sin_ref, aq_ref, ak_ref):
+        i = step.index[0]
+        length = jnp.where(i // steps == spot.half, lens[0][0:1, :], lens[1][0:1, :])
+        shape = (block, LANES)
+        row = (lax.broadcasted_iota(jnp.int32, shape, 0) + (i % steps) * block).astype(F32)
+        lane = lanes_of(shape) % HEAD
+        segment, position, end = jnp.zeros(shape, F32), row, 0.0
+        for j in range(count):
+            end = end + length[:, j : j + 1]
+            passed = row >= end
+            segment = segment + jnp.where(passed, 1.0, 0.0)
+            position = position - jnp.where(passed, length[:, j : j + 1], 0.0)
+        angle = position * inverse_ref[...]
+        sign = jnp.where(lane < ROT // 2, -1.0, 1.0)
+        cos_ref[...] = jnp.cos(angle)
+        sin_ref[...] = jnp.sin(angle) * sign
+        same = segment == lane.astype(F32)
+        aq_ref[...] = jnp.where(same & (lane <= count), NEG, 0.0).astype(BF)
+        other = (lane <= count) & ~same
+        ak_ref[...] = jnp.where(other | ((lane >= 8) & (lane < 11)), 1.0, 0.0).astype(BF)
+
+    spec = pl.BlockSpec((block, LANES), lambda i: (i, 0))
+    pltpu.emit_pipeline(
+        body,
+        grid=(2 * steps,),
+        in_specs=[pl.BlockSpec((1, LANES), lambda i: (0, 0))],
+        out_specs=[spec] * 4,
+        _explicit_indices=True,
+    )(inverse, cosine, sine, aq, ak)
 
 
 def attend_kernel(rows, block, qkv_ref, aq_ref, ak_ref, *refs):
@@ -765,62 +741,130 @@
 SUMMED = 8
 
 
-def back_kernel(ndp, nt, *refs):
+def layer_kernel(ndp, nt, count, *refs):
     refs = list(refs)
     take = lambda n: [refs.pop(0) for _ in range(n)]
-    h, gb, act, slope, o, da, wq, wd, w1, w2, x_own, g_own, gain, bias = take(14)
-    output, grad_x, small, gz = take(4)
+    x_own, g_own, gain, shift, lens_own, inverse, wq_own, w1_own, wd_own, w2_own, bias_q, bias_1, bias_out = take(13)
+    output, grad_x, small = take(3)
     weights = [take(7) for _ in range(3)]
     row_buffers = [take(6) for _ in range(2)]
-    acc, sums, biases, line_got, pair_got, send, recv = take(7)
+    h, gb, wq, w1, wd, w2, qkv, o_float, o, lse, act, slope, go, da, cosine, sine, aq, ak, gz = take(19)
+    dk_s, dv_s, dqt_s, lens, acc, sums, biases, line_got, pair_got, local_sem, send, recv = take(12)
     spot = Spot(ndp, nt)
     links = Links(send, recv)
+    group = h.shape[0] // 2
     own = x_own.shape[0]
+    half, other = spot.half, 1 - spot.half
     greet(spot.partners())
-    sums[...] = jnp.zeros(sums.shape, F32)
-    biases[...] = jnp.zeros(biases.shape, F32)
-
-    q_columns, f_columns = da.shape[1], act.shape[1]
+
+    lens_given = links.copy(lens_own, lens, spot.mate)
+    gather_q = GatherWeight(links, spot, wq_own, wq, local_sem.at[0])
+    gather_1 = GatherWeight(links, spot, w1_own, w1, local_sem.at[1])
+    gather_d = GatherWeight(links, spot, wd_own, wd, local_sem.at[2])
+    gather_2 = GatherWeight(links, spot, w2_own, w2, local_sem.at[3])
+    rows_h = GatherRows(links, spot, h, own)
+    rows_gb = GatherRows(links, spot, gb, own)
     reduce_2, reduce_q, reduce_1 = [
         ReduceWeight(links, spot, parts, slots, end, joined, mine, given, theirs)
         for mine, theirs, given, parts, slots, end, joined in weights
     ]
     branch = ReduceRows(links, spot, [(act, w2), (o, wd)], row_buffers[0], own)
     grad = ReduceRows(links, spot, [(gz, w1), (da, wq)], row_buffers[1], own)
+    tables = [cosine, sine, aq, ak]
+    blocks = group // own
+    q_columns, f_columns = da.shape[1], act.shape[1]
+    attend = functools.partial(attend_kernel, group, min(512, group))
+    back = functools.partial(attend_back_kernel, group, min(256, group))
+
+    def attend_back(qkv_ref, aq_ref, ak_ref, cos_ref, sin_ref, o_ref, lse_ref, go_ref, out_ref):
+        back(qkv_ref, aq_ref, ak_ref, o_ref, lse_ref, go_ref, cos_ref, sin_ref, out_ref, dk_s, dv_s, dqt_s)
+
+    def project(g):
+        by_rows(qkv_body, [h, wq, bias_q, cosine, sine], [qkv], own, g * blocks, blocks)
+
+    def attend_group(g):
+        by_heads(attend, [qkv], [], [aq, ak], [o_float, o, lse], group, g)
+
+    def output_grads(g):
+        by_rows(plain_body, [gb, wd], [go], own, g * blocks, blocks)
+
+    def attend_back_group(g):
+        by_heads(attend_back, [qkv], [o_float, lse, go], [aq, ak, cosine, sine], [da], group, g)
 
     def outer(left, rights, target, columns, total=None):
         outer_products(left, rights, target.parts, acc.at[:, :, pl.ds(0, columns)], spot, left.shape[0] // 2, total)
 
+    lens_given.start()
+    gather_q.first()
+    sums[...] = jnp.zeros(sums.shape, F32)
+    biases[...] = jnp.zeros(biases.shape, F32)
+    norm_inputs(spot, x_own, g_own, gain, shift, lens_own, h, gb, 2)
+    rows_h.first()
+    gather_q.second()
+    gather_d.first()
+    gather_1.first()
+    lens_given.get()
+    make_tables(spot, (lens_own, lens), count, inverse, cosine, sine, aq, ak, own)
+    gather_q.third()
+    rows_h.second()
+    gather_d.second()
+    gather_q.finish()
+    gather_1.second()
+    rows_h.finish_near()
+    project(half)
+    rows_h.third()
+    rows_gb.first()
+    gather_2.first()
+    attend_group(half)
+    gather_d.third()
+    rows_h.finish()
+    project(other)
+    attend_group(other)
+    rows_gb.second()
+    gather_d.finish()
+    rows_gb.finish_near()
+    output_grads(half)
+    gather_1.third()
+    gather_2.second()
+    attend_back_group(half)
+    rows_gb.third()
+    gather_1.finish()
+    by_rows(gelu_body, [h, w1, bias_1], [act, slope], own)
+    rows_gb.finish()
+    output_grads(other)
+    gather_2.third()
+    outer(gb, [act, o], reduce_2, f_columns + o.shape[1])
+    reduce_2.first()
+    gather_2.finish()
+    branch.run(0, 0, 1)
+    reduce_2.second()
+    branch.run(0, 1, 1)
+    attend_back_group(other)
+    reduce_2.third()
+    branch.run(1, 0, 1)
+    branch.run(1, 1, 1)
     outer(h, [da], reduce_q, q_columns, biases.at[1:2, pl.ds(0, q_columns)])
     reduce_q.first()
-    branch.run(0, 0, 1)
-    branch.run(0, 1, 1)
+    by_rows(slope_body, [gb, w2, slope], [gz], own)
     reduce_q.second()
-    branch.run(1, 0, 1)
-    branch.run(1, 1, 1)
-    reduce_q.third()
-    outer(gb, [act, o], reduce_2, f_columns + o.shape[1])
-    reduce_2.first()
-    by_rows(slope_body, [gb, w2, slope], [gz], own)
-    reduce_2.second()
     grad.run(0, 0, 1)
     grad.run(0, 1, 1)
+    reduce_q.third()
     branch.run(2, 0, 2)
     branch.run(2, 1, 2)
-    reduce_2.third()
     grad.run(1, 0, 1)
     grad.run(1, 1, 1)
     outer(h, [gz], reduce_1, f_columns, biases.at[0:1, pl.ds(0, f_columns)])
     reduce_1.first()
-    reduce_q.fourth()
+    reduce_2.fourth()
     reduce_1.second()
-    branch.last(output_rows, [x_own, bias], [output], 2)
+    branch.last(output_rows, [x_own, bias_out], [output], 2)
     grad.run(2, 0, 2)
     grad.run(2, 1, 2)
+    reduce_q.fourth()
     reduce_1.third()
-    reduce_2.fourth()
-    reduce_q.finish()
-    grad.last(functools.partial(norm_rows, sums), [x_own, g_own, gain], [grad_x], 2)
+    norm = functools.partial(norm_rows, sums)
+    grad.last(norm, [x_own, gb.at[pl.ds(pl.multiple_of(spot.block(0, 0, 0) * own, own), own)], gain], [grad_x], 2)
     reduce_1.fourth()
 
     sums[SUMMED // 2 : SUMMED // 2 + 2, :] = biases[...]
@@ -845,45 +889,58 @@
             small[1] = theirs
         sums[...] = sums[...] + jnp.where(row < SUMMED // 2, theirs, 0.0)
     small[0] = sums[...]
-    reduce_2.finish()
-    reduce_1.finish()
+    for reduced in (reduce_2, reduce_q, reduce_1):
+        reduced.finish()
     links.finish()
 
 
-def back_call(ndp, nt, h, gb, act, slope, o, da, wq, wd, w1, w2, x_own, g_own, gain, bias):
+def layer_call(ndp, nt, count, x_own, g_own, gain, shift, lens, inverse, weights, biases):
     own, width = x_own.shape
-    rows = h.shape[0]
+    group = nt * own
+    rows = 2 * group
     places = ndp // 2
     size, shard = width // places, width // ndp
-    q3, f, q = wq.shape[1], w1.shape[1], wd.shape[1]
+    q3, f, q = [weights[k].shape[1] // 2 for k in (0, 1, 2)]
     shape = lambda *s: jax.ShapeDtypeStruct(s, BF)
     full = lambda *s: jax.ShapeDtypeStruct(s, F32)
-    out_shape = [shape(own, width), full(own, width), full(2, SUMMED, width), shape(rows, f)]
+    out_shape = [shape(own, width), full(own, width), full(2, SUMMED, width)]
     for n in (f + q, q3, f):
         out_shape += [full(shard, n), shape(shard, n), shape(shard, n)]
         out_shape += [shape(places, size, n), shape(places - 1, size, n), shape(size, n), shape(size, n)]
     for _ in range(2):
         out_shape += [shape(2, k * own, width // 2) for k in (4, 2, 1)] * 2
+    out_shape += [shape(rows, width), shape(rows, width)]
+    out_shape += [shape(width, n) for n in (q3, f, q, f)]
+    out_shape += [shape(rows, q3), full(rows, q), shape(rows, q), full(rows, q)]
+    out_shape += [shape(rows, f), shape(rows, f), shape(rows, q), shape(rows, q3)]
+    out_shape += [full(rows, LANES), full(rows, LANES), shape(rows, LANES), shape(rows, LANES), shape(rows, f)]
     anywhere = pl.BlockSpec(memory_space=pl.ANY)
+    in_specs = [anywhere] * 13
+    in_specs[4] = pl.BlockSpec(memory_space=pltpu.VMEM)
     out_specs = [anywhere] * len(out_shape)
     out_specs[2] = pl.BlockSpec(memory_space=pltpu.VMEM)
-    transfers = 3 * (1 + max(6, places)) + 2 * 2 * 6 + places + 3
+    transfers = 1 + 2 * 9 + 4 * (1 + max(4, places)) + 3 * (1 + max(6, places)) + 2 * 2 * 6 + places + 3
     return pl.pallas_call(
-        functools.partial(back_kernel, ndp, nt),
-        in_specs=[anywhere] * 14,
+        functools.partial(layer_kernel, ndp, nt, count),
+        in_specs=in_specs,
         out_specs=out_specs,
         out_shape=out_shape,
         scratch_shapes=[
+            pltpu.VMEM((group, LANES), F32),
+            pltpu.VMEM((group, LANES), F32),
+            pltpu.VMEM((LANES, group), F32),
+            pltpu.VMEM(lens.shape, F32),
             pltpu.VMEM((places, size, f + q), F32),
             pltpu.VMEM((SUMMED, width), F32),
             pltpu.VMEM((2, width), F32),
             pltpu.VMEM((places, SUMMED, width), F32),
             pltpu.VMEM((3, SUMMED, width), F32),
+            pltpu.SemaphoreType.DMA((4,)),
             pltpu.SemaphoreType.DMA((transfers,)),
             pltpu.SemaphoreType.DMA((transfers,)),
         ],
-        compiler_params=pltpu.CompilerParams(collective_id=1, has_side_effects=True, vmem_limit_bytes=VMEM),
-    )(h, gb, act, slope, o, da, wq, wd, w1, w2, x_own, g_own, gain, bias)
+        compiler_params=pltpu.CompilerParams(collective_id=0, has_side_effects=True, vmem_limit_bytes=VMEM),
+    )(x_own, g_own, gain, shift, lens, inverse, *weights, *biases)
 
 
 def local(
@@ -913,55 +970,18 @@
     pairs = q_width // LANES
     other = 1 - half
 
-    wq = w_qkv.reshape(shard, 3, 2, pairs, LANES).transpose(2, 0, 3, 1, 4).reshape(2, shard, 3 * q_width)
-    wd = w_dense.T.reshape(shard, 2, q_width).transpose(1, 0, 2)
-    w1 = w_fc1.reshape(shard, 2, f_width).transpose(1, 0, 2)
-    w2 = w_fc2.T.reshape(shard, 2, f_width).transpose(1, 0, 2)
-
-    xf = layer_input.astype(F32)
-    mean = jnp.mean(xf, axis=1, keepdims=True)
-    centred = xf - mean
-    rstd = lax.rsqrt(jnp.mean(centred * centred, axis=1, keepdims=True) + EPS)
-    x_hat = centred * rstd
-    h_own = (x_hat * ln_gain + ln_bias).astype(BF)
-    used = jnp.sum(seq_lens[0])
-    valid = (t * own + jnp.arange(own, dtype=jnp.int32) < used).astype(F32)[:, None]
-    gy = cotangent.astype(F32) * valid
-    gb_own = gy.astype(BF)
-
-    lens_of_mate = swap(seq_lens, "dp", 1)
-
-    lens = jnp.zeros((2, seq_lens.shape[1]), jnp.int32)
-    lens = place(place(lens, seq_lens[0], half), lens_of_mate[0], other)
-    ends = jnp.cumsum(lens, axis=1)
-    rows = jnp.arange(group, dtype=jnp.int32)
-    segment = jnp.sum((rows[None, :, None] >= ends[:, None, :]).astype(jnp.int32), axis=2)
-    begins = jnp.concatenate([ends - lens, ends[:, -1:]], axis=1)
-    labels = jnp.arange(begins.shape[1], dtype=jnp.int32)
-    mine = segment[:, :, None] == labels
-    position = rows[None] - jnp.sum(jnp.where(mine, begins[:, None, :], 0), axis=2)
+    wq = w_qkv.reshape(shard, 3, 2, pairs, LANES).transpose(0, 2, 3, 1, 4).reshape(shard, 6 * q_width)
+    bias_q = pick(b_qkv.reshape(3, 2, pairs, LANES).transpose(1, 2, 0, 3), half).reshape(1, 3 * q_width)
+    bias_1 = pick(b_fc1.reshape(2, f_width), half)[None]
+    count = seq_lens.shape[1]
+    lens = jnp.zeros((8, LANES), F32).at[0, :count].set(seq_lens[0].astype(F32))
     steps = jnp.arange(ROT // 2, dtype=F32)
     inverse = jnp.exp(-math.log(10000.0) * 2.0 * steps / ROT)
-    angle = inverse[:, None] * position.reshape(1, 2 * group).astype(F32)
-    cos16, sin16 = jnp.cos(angle).T, jnp.sin(angle).T
-    still = jnp.zeros((2 * group, HEAD - ROT), F32)
-    cosine = jnp.concatenate([cos16, cos16, still + 1.0] * 2, axis=1)
-    sine = jnp.concatenate([-sin16, sin16, still] * 2, axis=1)
-    lane = jnp.arange(LANES, dtype=jnp.int32) % HEAD
-    same = segment.reshape(2 * group, 1) == lane[None, :]
-    count = begins.shape[1]
-    aq = jnp.where(same & (lane < count), NEG, 0.0).astype(BF)
-    ak = jnp.where(~same & (lane < count) | (lane >= 8) & (lane < 11), 1.0, 0.0).astype(BF)
-
-    bias_q = pick(b_qkv.reshape(3, 2, pairs, LANES).transpose(1, 2, 0, 3), half).reshape(1, 3 * q_width)
-    bias_1 = pick(b_fc1.reshape(2, f_width), half)[None]
-
-    h, gb, wq_all, w1_all, wd_all, w2_all, qkv, o_float, o, lse, act, slope, go, da = front_call(
-        ndp, nt, h_own, gb_own, [wq, w1, wd, w2], [bias_q, bias_1], [cosine, sine, aq, ak]
-    )
-    made = back_call(
-        ndp, nt, h, gb, act, slope, o, da, wq_all, wd_all, w1_all, w2_all, layer_input, gb_own, ln_gain[None],
-        (b_dense + b_fc2)[None],
+    inverse = jnp.concatenate([inverse, inverse, jnp.zeros((HEAD - ROT,), F32)] * 2)[None]
+
+    made = layer_call(
+        ndp, nt, count, layer_input, cotangent, ln_gain[None], ln_bias[None], lens, inverse,
+        [wq, w_fc1, w_dense.T, w_fc2.T], [bias_q, bias_1, (b_dense + b_fc2)[None]],
     )
     output, grad_x, small = made[:3]
 
@@ -969,7 +989,7 @@
         theirs = theirs.astype(F32)
         return jnp.stack([jnp.where(half == 0, mine, theirs), jnp.where(half == 0, theirs, mine)])
 
-    g_2, g_wq, g_w1 = [both(made[k], made[k + 1]) for k in (4, 11, 18)]
+    g_2, g_wq, g_w1 = [both(made[k], made[k + 1]) for k in (3, 10, 17)]
     g_w2, g_wd = g_2[:, :, :f_width], g_2[:, :, f_width:]
     late, early = small[0, :2], small[0, 2]
     g_biases = both(small[0, SUMMED // 2 : SUMMED // 2 + 2], small[1, SUMMED // 2 : SUMMED // 2 + 2])

time: 706 us -> 616 us (0.87)
  Pallas kernels: 608 us -> 576 us
  local copies, waits for them, and re-layouts: 55.6 us -> 27.7 us
  other arithmetic: 33.2 us -> 5.92 us
    pallas_call x2 -> x1, Pallas kernels: 608 us -> 576 us  [layer_call(): pl.pallas_call(functools.partial(layer_kernel, ndp, nt, count), in_specs=...]
    concatenate x3 -> x1, local copies, waits for them, and re-layouts: 16.4 us -> 0.6 us  [local(): jnp.concatenate([inverse, inverse, jnp.zeros((HEAD - ROT,), F32)] * 2)[None]]
    sin x1 -> x0, other arithmetic: 9.54 us -> none  [local(): cos16, sin16 = (jnp.cos(angle).T, jnp.sin(angle).T)]
    convert_element_type x3 -> x1, other arithmetic: 8.31 us -> 0.66 us  [local(): lens = jnp.zeros((8, LANES), F32).at[0, :count].set(seq_lens[0].astype(F32))]
    unnamed x39 -> x26, local copies, waits for them, and re-layouts: 15.5 us -> 16 us
  transfers between devices with their start and end apart: 1 -> 0, of which waited for: 0 -> 0; matrix products, arithmetic and copies ran while one was open for 3% -> 0% of each run, Pallas kernels for 0% -> 0%
where the time goes in v4:
time: 616 us; the launch traced here: 610 us
  Pallas kernels  576 us (94%)
  local copies, waits for them, and re-layouts  27.7 us (4%)
    pallas_call x1, Pallas kernels, layer_call(): pl.pallas_call(functools.partial(layer_kernel, ndp, nt, count), in_specs=...  576 us
    unnamed x26, local copies, waits for them, and re-layouts  16 us

profile of v4, /device:TPU:0, one launch (start us, length us, event | category | flops | bytes accessed | tf_op | source)
XLA Modules:
  0.0 610.5 jit_solution(5588888776357452949)
XLA Ops:
  0.7 0.7 copy-done
  1.3 0.7 convert_element_type.13
  2.0 0.6 concatenate.6
  3.8 1.3 add.19
  5.1 0.7 reshape.96
  5.8 0.6 constant_dynamic-slice_fusion.refs_11_
  6.4 1.8 copy.43
  8.2 1.5 copy.41
  9.8 1.2 copy.46.refs_6_
  10.9 1.4 copy.44
  12.4 575.8 %shard_map.220 = (bf16[512,2048]{1,0:T(8,128)(2,1)}, f32[512,2048]{1,0:T(8,128)}, f32[2,8,2048]{2,1,0:T(8,128)}, f32[256,1280]{1,0:T(8,128)}, bf16[256,1280]{1,0...) custom-call(bf16[512,2048]{1,0:T(8,128)(2,1)} %refs_0_.1, ...), custom_call_target="tpu_custom_call" | custom-call | tf_op jit(solution)/shard_map/pallas_call | solution.py:923
  588.1 1.6 fusion.5
  589.7 0.9 broadcast_select_fusion.1
  590.7 0.6 pad_maximum_fusion.1
  591.3 0.6 reshape_squeeze.6
  591.9 1.3 convert_select_fusion.5
  594.0 1.6 copy.53
  596.1 1.8 copy.51
  598.0 3.0 copy.54
  601.5 1.8 copy.52
  603.3 1.0 copy.50
  604.3 0.6 copy.58
  604.9 3.3 copy.59
  608.2 2.0 copy.60
  (33 shorter events, 3.0 us)
Async XLA Ops:
  0.6 0.7 copy-start
  8.2 2.7 copy-start.4
  589.7 14.6 %copy-start.8 = (f32[1,1,2048]{2,1,0:T(1,128)}, f32[1,1,2048]{2,1,0:T(1,128)S(1)}, u32[]{:S(2)}) copy-start(f32[1,1,2048]{2,1,0:T(1,128)S(1)} %get-tuple-element.72) | copy-start | bytes 24580
  594.0 1.6 copy-start.5
  594.0 1.6 copy-start.7
  598.0 3.0 copy-start.3
  598.0 3.0 copy-start.6
  604.9 3.3 copy-start.2
  608.2 2.0 copy-start.1

commit v5 on v4

--- a/solution.py
+++ b/solution.py
@@ -476,10 +476,11 @@
         right_refs, out = refs[:-1], refs[-1]
         r, j = step.index
         first = 0
+        turned = left_ref[...].T
         for right_ref in right_refs:
             there = slice(first, first + right_ref.shape[1])
             first += right_ref.shape[1]
-            term = lax.dot_general(left_ref[...], right_ref[...], TN, preferred_element_type=F32)
+            term = jnp.dot(turned, right_ref[...], preferred_element_type=F32)
 
             @pl.when(r == 0)
             def _():
@@ -509,11 +510,11 @@
 
 
 class ReduceWeight:
-    def __init__(self, links, spot, parts, slots, end, joined, mine, given, theirs):
+    def __init__(self, links, spot, parts, slots, end, joined, results, given, theirs):
         self.links, self.spot = links, spot
         self.parts, self.slots, self.end, self.joined = parts, slots, end, joined
-        self.mine, self.given, self.theirs = mine, given, theirs
-        self.shard = mine.shape[0]
+        self.results, self.given, self.theirs = results, given, theirs
+        self.shard = given.shape[0]
 
     def send(self, src, dst, to, sends=None, gets=None):
         return self.links.copy(src, dst, self.spot.along(to), sends, gets).start()
@@ -569,34 +570,61 @@
             sent.get()
         columns = self.parts.shape[2]
 
-        def body(own, *refs):
-            out = refs[-1]
+        def body(given, own, *refs):
             total = own[...].astype(F32)
-            for k, ref in enumerate(refs[:-1]):
+            for k, ref in enumerate(refs[: places - 1]):
                 term = ref[...].astype(F32)
                 if places == 4 and k < 2:
                     term = term * jnp.where(at > 0 if k == 0 else at < 3, 1.0, 0.0)
                 total = total + term
-            out[...] = total.astype(out.dtype)
+            if given:
+                refs[-1][...] = total.astype(BF)
+            else:
+                self.store(total, refs[places - 1 :])
 
         def slot(k, part):
             if places == 4 and k < 2:
                 k = jnp.where(at > 0, 0, 2) if k == 0 else jnp.where(at < 3, 1, 2)
             return pl.BlockSpec((None, self.shard, columns), lambda i: (k, part, 0))
 
-        for part, out in ((1 - spot.half, self.given), (spot.half, self.mine)):
+        for part in (1 - spot.half, spot.half):
             own = pl.BlockSpec((None, self.shard, columns), lambda i, part=part: (0, part, 0))
+            given = part is not spot.half
+            specs, outs = self.whole_given() if given else self.own_columns(spot.half)
             pltpu.emit_pipeline(
-                body,
+                functools.partial(body, given),
                 grid=(1,),
                 in_specs=[own] + [slot(k, part) for k in range(places - 1)],
-                out_specs=[pl.BlockSpec((self.shard, columns), lambda i: (0, 0))],
-            )(self.parts, *[self.slots] * (places - 1), out)
-            if out is self.given:
+                out_specs=specs,
+            )(self.parts, *[self.slots] * (places - 1), *outs)
+            if given:
                 self.mate = self.links.copy(self.given, self.theirs, spot.mate).start()
+
+    def whole_given(self):
+        return [pl.BlockSpec(self.given.shape, lambda i: (0, 0))], [self.given]
+
+    def own_columns(self, half):
+        specs = []
+        for ref, first, width, turned in self.results:
+            if turned:
+                specs.append(pl.BlockSpec((width, self.shard), lambda i: (half, 0)))
+            else:
+                specs.append(pl.BlockSpec((self.shard, width), lambda i: (0, half)))
+        return specs, [result[0] for result in self.results]
+
+    def store(self, total, outs):
+        for out, (_, first, width, turned) in zip(outs, self.results):
+            mine = total[:, first : first + width]
+            out[...] = mine.T if turned else mine
 
     def finish(self):
         self.mate.get()
+
+        def body(theirs, *outs):
+            self.store(theirs[...].astype(F32), outs)
+
+        specs, outs = self.own_columns(1 - self.spot.half)
+        pltpu.emit_pipeline(body, grid=(1,), in_specs=self.whole_given()[0], out_specs=specs)(self.theirs, *outs)
 
 
 class ReduceRows:
@@ -608,7 +636,8 @@
 
     def block(self, part, n, twins):
         spot = self.spot
-        g_own, x_own = (n // 2, n % 2) if part == 0 else (n % 2, n // 2)
+        g_own = (1 - part) * (n // 2) + part * (n % 2)
+        x_own = (1 - part) * (n % 2) + part * (n // 2)
         other, x1 = 1 - spot.half, 1 - spot.chip
         g = other + g_own * (spot.half - other)
         x = x1 + x_own * (spot.chip - x1)
@@ -618,13 +647,15 @@
     def added(self, stage):
         return [((), (0,), (2, 0), (3, 1, 0))[stage][k] for k in range(stage)]
 
-    def run(self, stage, part, cut):
+    def run(self, stage, cut):
         first, last = ((0, 4), (0, 2), (2, 3))[stage]
         own, columns = self.own, self.columns
         rows = own // cut
+        each = (last - first) * cut
         n_factors = len(self.factors)
-        for earlier in range(stage):
-            self.wait(earlier, part, stage)
+        for part in (0, 1):
+            for earlier in range(stage):
+                self.wait(earlier, part, stage)
 
         def body(*refs):
             ins, out = refs[:-1], refs[-1]
@@ -636,37 +667,38 @@
                 total = total + ref[...].astype(F32)
             out[...] = total.astype(BF)
 
+        def row_block(i):
+            part, k = i // each, i % each
+            return self.block(part, first + k // cut, stage == 0) * cut + k % cut
+
         in_specs, args = [], []
         for a, b in self.factors:
             depth = a.shape[1]
-            in_specs.append(
-                pl.BlockSpec(
-                    (rows, depth), lambda i: (self.block(part, first + i // cut, stage == 0) * cut + i % cut, 0)
-                )
-            )
-            in_specs.append(pl.BlockSpec((columns, depth), lambda i: (part, 0)))
+            in_specs.append(pl.BlockSpec((rows, depth), lambda i: (row_block(i), 0)))
+            in_specs.append(pl.BlockSpec((columns, depth), lambda i: (i // each, 0)))
             args += [a, b]
         for k, offset in enumerate(self.added(stage)):
             in_specs.append(
-                pl.BlockSpec((None, rows, columns), lambda i, offset=offset: (part, offset * cut + i, 0))
+                pl.BlockSpec(
+                    (None, rows, columns), lambda i, offset=offset: (i // each, offset * cut + i % each, 0)
+                )
             )
             args.append(self.got[k])
         pltpu.emit_pipeline(
             body,
-            grid=((last - first) * cut,),
+            grid=(2 * each,),
             in_specs=in_specs,
-            out_specs=[pl.BlockSpec((None, rows, columns), lambda i: (part, i, 0))],
+            out_specs=[pl.BlockSpec((None, rows, columns), lambda i: (i // each, i % each, 0))],
         )(*args, self.given[stage])
-        axes = (self.spot.mate, self.spot.across) if part == 0 else (self.spot.across, self.spot.mate)
-        device = self.spot.twin if stage == 0 else axes[stage - 1]
         pieces = ((0, 2), (2, 1), (3, 1)) if stage == 0 else ((0, 1), (1, 1)) if stage == 1 else ((0, 1),)
-        sent = []
+        self.sent[stage] = [[], []]
         for at, count in pieces:
-            there = pl.ds(at * own, count * own)
-            sent.append(
-                self.links.copy(self.given[stage].at[part, there], self.got[stage].at[part, there], device).start()
-            )
-        self.sent[stage][part] = sent
+            for part in (0, 1):
+                axes = (self.spot.mate, self.spot.across) if part == 0 else (self.spot.across, self.spot.mate)
+                device = self.spot.twin if stage == 0 else axes[stage - 1]
+                there = pl.ds(at * own, count * own)
+                copy = self.links.copy(self.given[stage].at[part, there], self.got[stage].at[part, there], device)
+                self.sent[stage][part].append(copy.start())
 
     def wait(self, earlier, part, stage):
         self.sent[earlier][part][stage - earlier - 1].get()
@@ -746,7 +778,8 @@
     take = lambda n: [refs.pop(0) for _ in range(n)]
     x_own, g_own, gain, shift, lens_own, inverse, wq_own, w1_own, wd_own, w2_own, bias_q, bias_1, bias_out = take(13)
     output, grad_x, small = take(3)
-    weights = [take(7) for _ in range(3)]
+    g_w2, g_wd, g_wq, g_w1 = take(4)
+    weights = [take(6) for _ in range(3)]
     row_buffers = [take(6) for _ in range(2)]
     h, gb, wq, w1, wd, w2, qkv, o_float, o, lse, act, slope, go, da, cosine, sine, aq, ak, gz = take(19)
     dk_s, dv_s, dqt_s, lens, acc, sums, biases, line_got, pair_got, local_sem, send, recv = take(12)
@@ -765,8 +798,15 @@
     rows_h = GatherRows(links, spot, h, own)
     rows_gb = GatherRows(links, spot, gb, own)
     reduce_2, reduce_q, reduce_1 = [
-        ReduceWeight(links, spot, parts, slots, end, joined, mine, given, theirs)
-        for mine, theirs, given, parts, slots, end, joined in weights
+        ReduceWeight(links, spot, parts, slots, end, joined, results, given, theirs)
+        for results, (theirs, given, parts, slots, end, joined) in zip(
+            (
+                [(g_w2, 0, w2.shape[1], True), (g_wd, w2.shape[1], wd.shape[1], True)],
+                [(g_wq, 0, wq.shape[1], False)],
+                [(g_w1, 0, w1.shape[1], False)],
+            ),
+            weights,
+        )
     ]
     branch = ReduceRows(links, spot, [(act, w2), (o, wd)], row_buffers[0], own)
     grad = ReduceRows(links, spot, [(gz, w1), (da, wq)], row_buffers[1], own)
@@ -807,13 +847,13 @@
     make_tables(spot, (lens_own, lens), count, inverse, cosine, sine, aq, ak, own)
     gather_q.third()
     rows_h.second()
+    rows_gb.first()
+    gather_q.finish()
     gather_d.second()
-    gather_q.finish()
     gather_1.second()
     rows_h.finish_near()
     project(half)
     rows_h.third()
-    rows_gb.first()
     gather_2.first()
     attend_group(half)
     gather_d.third()
@@ -836,41 +876,37 @@
     outer(gb, [act, o], reduce_2, f_columns + o.shape[1])
     reduce_2.first()
     gather_2.finish()
-    branch.run(0, 0, 1)
+    branch.run(0, 1)
     reduce_2.second()
-    branch.run(0, 1, 1)
     attend_back_group(other)
     reduce_2.third()
-    branch.run(1, 0, 1)
-    branch.run(1, 1, 1)
+    branch.run(1, 1)
     outer(h, [da], reduce_q, q_columns, biases.at[1:2, pl.ds(0, q_columns)])
     reduce_q.first()
     by_rows(slope_body, [gb, w2, slope], [gz], own)
     reduce_q.second()
-    grad.run(0, 0, 1)
-    grad.run(0, 1, 1)
+    grad.run(0, 1)
     reduce_q.third()
-    branch.run(2, 0, 2)
-    branch.run(2, 1, 2)
-    grad.run(1, 0, 1)
-    grad.run(1, 1, 1)
+    branch.run(2, 1)
+    grad.run(1, 1)
     outer(h, [gz], reduce_1, f_columns, biases.at[0:1, pl.ds(0, f_columns)])
     reduce_1.first()
     reduce_2.fourth()
     reduce_1.second()
     branch.last(output_rows, [x_own, bias_out], [output], 2)
-    grad.run(2, 0, 2)
-    grad.run(2, 1, 2)
+    grad.run(2, 1)
+    reduce_2.finish()
     reduce_q.fourth()
     reduce_1.third()
     norm = functools.partial(norm_rows, sums)
     grad.last(norm, [x_own, gb.at[pl.ds(pl.multiple_of(spot.block(0, 0, 0) * own, own), own)], gain], [grad_x], 2)
-    reduce_1.fourth()
 
     sums[SUMMED // 2 : SUMMED // 2 + 2, :] = biases[...]
     places = spot.places
     line_got[0] = sums[...]
     got = [links.copy(sums, line_got.at[j], spot.along((spot.at + j) % places)).start() for j in range(1, places)]
+    reduce_q.finish()
+    reduce_1.fourth()
     for sent in got:
         sent.get()
     for sent in got:
@@ -889,8 +925,7 @@
             small[1] = theirs
         sums[...] = sums[...] + jnp.where(row < SUMMED // 2, theirs, 0.0)
     small[0] = sums[...]
-    for reduced in (reduce_2, reduce_q, reduce_1):
-        reduced.finish()
+    reduce_1.finish()
     links.finish()
 
 
@@ -904,8 +939,9 @@
     shape = lambda *s: jax.ShapeDtypeStruct(s, BF)
     full = lambda *s: jax.ShapeDtypeStruct(s, F32)
     out_shape = [shape(own, width), full(own, width), full(2, SUMMED, width)]
+    out_shape += [full(2 * f, shard), full(2 * q, shard), full(shard, 2 * q3), full(shard, 2 * f)]
     for n in (f + q, q3, f):
-        out_shape += [full(shard, n), shape(shard, n), shape(shard, n)]
+        out_shape += [shape(shard, n), shape(shard, n)]
         out_shape += [shape(places, size, n), shape(places - 1, size, n), shape(size, n), shape(size, n)]
     for _ in range(2):
         out_shape += [shape(2, k * own, width // 2) for k in (4, 2, 1)] * 2
@@ -986,19 +1022,14 @@
     output, grad_x, small = made[:3]
 
     def both(mine, theirs):
-        theirs = theirs.astype(F32)
         return jnp.stack([jnp.where(half == 0, mine, theirs), jnp.where(half == 0, theirs, mine)])
 
-    g_2, g_wq, g_w1 = [both(made[k], made[k + 1]) for k in (3, 10, 17)]
-    g_w2, g_wd = g_2[:, :, :f_width], g_2[:, :, f_width:]
+    out_w2, out_wd, g_wq, g_w1 = made[3:7]
     late, early = small[0, :2], small[0, 2]
     g_biases = both(small[0, SUMMED // 2 : SUMMED // 2 + 2], small[1, SUMMED // 2 : SUMMED // 2 + 2])
     g_b1 = g_biases[:, 0, :f_width].reshape(-1)
     g_bq = g_biases[:, 1, : 3 * q_width].reshape(2, pairs, 3, LANES).transpose(2, 0, 1, 3).reshape(3, 2 * q_width)
-    out_wq = g_wq.reshape(2, shard, pairs, 3, LANES).transpose(1, 3, 0, 2, 4).reshape(shard, 3, 2 * q_width)
-    out_wd = g_wd.transpose(0, 2, 1).reshape(2 * q_width, shard)
-    out_w1 = g_w1.transpose(1, 0, 2).reshape(shard, 2 * f_width)
-    out_w2 = g_w2.transpose(0, 2, 1).reshape(2 * f_width, shard)
+    out_wq = g_wq.reshape(shard, 2, pairs, 3, LANES).transpose(0, 3, 1, 2, 4).reshape(shard, 3, 2 * q_width)
     return (
         output,
         grad_x,
@@ -1008,7 +1039,7 @@
         g_bq,
         out_wd,
         early,
-        out_w1,
+        g_w1,
         g_b1,
         out_w2,
         early,

time: 616 us -> 598 us (0.971)
  Pallas kernels: 576 us -> 562 us
    pallas_call x1, Pallas kernels: 576 us -> 562 us  [layer_call(): pl.pallas_call(functools.partial(layer_kernel, ndp, nt, count), in_specs=...]
where the time goes in v5:
time: 598 us; the launch traced here: 592 us
  Pallas kernels  562 us (94%)
  local copies, waits for them, and re-layouts  25.5 us (4%)
    pallas_call x1, Pallas kernels, layer_call(): pl.pallas_call(functools.partial(layer_kernel, ndp, nt, count), in_specs=...  562 us
    unnamed x26, local copies, waits for them, and re-layouts  17.1 us

profile of v5, /device:TPU:0, one launch (start us, length us, event | category | flops | bytes accessed | tf_op | source)
XLA Modules:
  0.0 592.3 jit_solution(12669728377904539385)
XLA Ops:
  0.7 0.7 copy-done
  1.3 0.7 convert_element_type.4
  2.0 0.6 concatenate.5
  2.6 0.6 scatter.4.refs_4_
  3.8 1.3 add.19
  5.1 0.7 reshape.85
  5.8 0.6 constant_dynamic-slice_fusion.refs_11_
  6.4 1.8 copy.38
  8.2 1.4 copy.36
  9.7 1.2 copy.41.refs_6_
  10.9 1.4 copy.39
  12.3 562.2 %shard_map.220 = (bf16[512,2048]{1,0:T(8,128)(2,1)}, f32[512,2048]{1,0:T(8,128)}, f32[2,8,2048]{2,1,0:T(8,128)}, f32[2048,256]{1,0:T(8,128)}, f32[512,256]{1,0:T...) custom-call(bf16[512,2048]{1,0:T(8,128)(2,1)} %refs_0_.1, ...), custom_call_target="tpu_custom_call" | custom-call | tf_op jit(solution)/shard_map/pallas_call | solution.py:959
  574.5 1.6 fusion
  576.1 0.9 broadcast_select_fusion.1
  577.0 0.6 pad_maximum_fusion
  577.6 0.6 reshape_squeeze.6
  578.2 1.9 copy.42
  580.2 1.6 copy.44
  581.9 0.6 copy.51
  582.5 3.5 copy.52
  585.9 2.1 copy.53
  588.1 0.8 copy.54
  589.4 1.3 copy.55
  590.7 1.3 copy.56
  (22 shorter events, 1.4 us)
Async XLA Ops:
  0.6 0.7 copy-start
  0.7 10.2 %copy-start.5 = (bf16[2048,256]{1,0:T(8,128)(2,1)S(1)}, bf16[2048,256]{1,0:T(8,128)(2,1)}, u32[]{:S(2)}) copy-start(bf16[2048,256]{1,0:T(8,128)(2,1)} %param.25) | copy-start | bytes 3145732
  576.1 5.8 copy-start.7
  581.8 4.1 copy-start.2
  585.9 2.1 copy-start.6
  585.9 3.5 copy-start.4
  588.1 2.7 copy-start.3
  589.4 2.6 copy-start.1

commit v6 on v5

--- a/solution.py
+++ b/solution.py
@@ -466,47 +466,45 @@
             out_ref[:, :LANES] = turn(d, cos_ref[...], -sin_ref[...]).astype(BF)
 
 
-def outer_products(left, rights, parts, acc, spot, block, sums=None):
+def outer_products(left, rights, parts, spot, sums=None):
     places = spot.places
     rows, size = left.shape[0], left.shape[1] // places
-    steps = rows // block
     columns = parts.shape[2]
 
     def body(step, left_ref, *refs):
         right_refs, out = refs[:-1], refs[-1]
-        r, j = step.index
+        turned = left_ref[...].T
         first = 0
-        turned = left_ref[...].T
         for right_ref in right_refs:
             there = slice(first, first + right_ref.shape[1])
             first += right_ref.shape[1]
-            term = jnp.dot(turned, right_ref[...], preferred_element_type=F32)
-
-            @pl.when(r == 0)
-            def _():
-                acc[j, :, there] = term
-
-            @pl.when((r > 0) & (r < steps - 1))
-            def _():
-                acc[j, :, there] += term
-
-            @pl.when(r == steps - 1)
-            def _():
-                out[:, there] = (acc[j, :, there] + term).astype(BF)
+            out[:, there] = jnp.dot(turned, right_ref[...], preferred_element_type=F32).astype(BF)
 
             if sums is not None:
-                @pl.when(j == 0)
+                @pl.when(step.index[0] == 0)
                 def _():
                     sums[...] += jnp.sum(right_ref[...].astype(F32), axis=0, keepdims=True)
 
     pltpu.emit_pipeline(
         body,
-        grid=(steps, places),
-        in_specs=[pl.BlockSpec((block, size), lambda r, j: (r, lax.rem(spot.at + j, places)))]
-        + [pl.BlockSpec((block, x.shape[1]), lambda r, j: (r, 0)) for x in rights],
-        out_specs=[pl.BlockSpec((None, size, columns), lambda r, j: (jnp.where(r == steps - 1, j, 0), 0, 0))],
+        grid=(places,),
+        in_specs=[pl.BlockSpec((rows, size), lambda j: (0, lax.rem(spot.at + j, places)))]
+        + [pl.BlockSpec((rows, x.shape[1]), lambda j: (0, 0)) for x in rights],
+        out_specs=[pl.BlockSpec((None, size, columns), lambda j: (j, 0, 0))],
         _explicit_indices=True,
     )(left, *rights, parts)
+
+
+def turn_weight(source, turned, block):
+    def body(a, out):
+        out[...] = a[...].T
+
+    pltpu.emit_pipeline(
+        body,
+        grid=(source.shape[0] // block,),
+        in_specs=[pl.BlockSpec((block, source.shape[1]), lambda i: (i, 0))],
+        out_specs=[pl.BlockSpec((source.shape[1], block), lambda i: (0, i))],
+    )(source, turned)
 
 
 class ReduceWeight:
@@ -750,8 +748,8 @@
 
 
 def output_rows(total, ins, outs):
-    x_ref, bias_ref = ins
-    outs[0][...] = (x_ref[...].astype(F32) + total + bias_ref[...]).astype(BF)
+    x_ref, dense_ref, fc2_ref = ins
+    outs[0][...] = (x_ref[...].astype(F32) + total + dense_ref[...] + fc2_ref[...]).astype(BF)
 
 
 def norm_rows(sums, total, ins, outs):
@@ -776,13 +774,13 @@
 def layer_kernel(ndp, nt, count, *refs):
     refs = list(refs)
     take = lambda n: [refs.pop(0) for _ in range(n)]
-    x_own, g_own, gain, shift, lens_own, inverse, wq_own, w1_own, wd_own, w2_own, bias_q, bias_1, bias_out = take(13)
+    x_own, g_own, gain, shift, lens_own, inverse, wq_own, w1_own, wd_raw, w2_raw, bias_q, bias_1, b_dense, b_fc2 = take(14)
     output, grad_x, small = take(3)
     g_w2, g_wd, g_wq, g_w1 = take(4)
     weights = [take(6) for _ in range(3)]
     row_buffers = [take(6) for _ in range(2)]
-    h, gb, wq, w1, wd, w2, qkv, o_float, o, lse, act, slope, go, da, cosine, sine, aq, ak, gz = take(19)
-    dk_s, dv_s, dqt_s, lens, acc, sums, biases, line_got, pair_got, local_sem, send, recv = take(12)
+    h, gb, wq, w1, wd, w2, qkv, o_float, o, lse, act, slope, go, da, cosine, sine, aq, ak, gz, wd_own, w2_own = take(21)
+    dk_s, dv_s, dqt_s, lens, sums, biases, line_got, pair_got, local_sem, send, recv = take(11)
     spot = Spot(ndp, nt)
     links = Links(send, recv)
     group = h.shape[0] // 2
@@ -831,8 +829,8 @@
     def attend_back_group(g):
         by_heads(attend_back, [qkv], [o_float, lse, go], [aq, ak, cosine, sine], [da], group, g)
 
-    def outer(left, rights, target, columns, total=None):
-        outer_products(left, rights, target.parts, acc.at[:, :, pl.ds(0, columns)], spot, left.shape[0] // 2, total)
+    def outer(left, rights, target, total=None):
+        outer_products(left, rights, target.parts, spot, total)
 
     lens_given.start()
     gather_q.first()
@@ -841,8 +839,10 @@
     norm_inputs(spot, x_own, g_own, gain, shift, lens_own, h, gb, 2)
     rows_h.first()
     gather_q.second()
+    gather_1.first()
+    turn_weight(wd_raw, wd_own, own)
     gather_d.first()
-    gather_1.first()
+    turn_weight(w2_raw, w2_own, own)
     lens_given.get()
     make_tables(spot, (lens_own, lens), count, inverse, cosine, sine, aq, ak, own)
     gather_q.third()
@@ -873,7 +873,7 @@
     rows_gb.finish()
     output_grads(other)
     gather_2.third()
-    outer(gb, [act, o], reduce_2, f_columns + o.shape[1])
+    outer(gb, [act, o], reduce_2)
     reduce_2.first()
     gather_2.finish()
     branch.run(0, 1)
@@ -881,7 +881,7 @@
     attend_back_group(other)
     reduce_2.third()
     branch.run(1, 1)
-    outer(h, [da], reduce_q, q_columns, biases.at[1:2, pl.ds(0, q_columns)])
+    outer(h, [da], reduce_q, biases.at[1:2, pl.ds(0, q_columns)])
     reduce_q.first()
     by_rows(slope_body, [gb, w2, slope], [gz], own)
     reduce_q.second()
@@ -889,11 +889,11 @@
     reduce_q.third()
     branch.run(2, 1)
     grad.run(1, 1)
-    outer(h, [gz], reduce_1, f_columns, biases.at[0:1, pl.ds(0, f_columns)])
+    outer(h, [gz], reduce_1, biases.at[0:1, pl.ds(0, f_columns)])
     reduce_1.first()
     reduce_2.fourth()
     reduce_1.second()
-    branch.last(output_rows, [x_own, bias_out], [output], 2)
+    branch.last(output_rows, [x_own, b_dense, b_fc2], [output], 2)
     grad.run(2, 1)
     reduce_2.finish()
     reduce_q.fourth()
@@ -935,7 +935,7 @@
     rows = 2 * group
     places = ndp // 2
     size, shard = width // places, width // ndp
-    q3, f, q = [weights[k].shape[1] // 2 for k in (0, 1, 2)]
+    q3, f, q = weights[0].shape[1] // 2, weights[1].shape[1] // 2, weights[2].shape[0] // 2
     shape = lambda *s: jax.ShapeDtypeStruct(s, BF)
     full = lambda *s: jax.ShapeDtypeStruct(s, F32)
     out_shape = [shape(own, width), full(own, width), full(2, SUMMED, width)]
@@ -950,8 +950,9 @@
     out_shape += [shape(rows, q3), full(rows, q), shape(rows, q), full(rows, q)]
     out_shape += [shape(rows, f), shape(rows, f), shape(rows, q), shape(rows, q3)]
     out_shape += [full(rows, LANES), full(rows, LANES), shape(rows, LANES), shape(rows, LANES), shape(rows, f)]
+    out_shape += [shape(shard, 2 * q), shape(shard, 2 * f)]
     anywhere = pl.BlockSpec(memory_space=pl.ANY)
-    in_specs = [anywhere] * 13
+    in_specs = [anywhere] * 14
     in_specs[4] = pl.BlockSpec(memory_space=pltpu.VMEM)
     out_specs = [anywhere] * len(out_shape)
     out_specs[2] = pl.BlockSpec(memory_space=pltpu.VMEM)
@@ -966,7 +967,6 @@
             pltpu.VMEM((group, LANES), F32),
             pltpu.VMEM((LANES, group), F32),
             pltpu.VMEM(lens.shape, F32),
-            pltpu.VMEM((places, size, f + q), F32),
             pltpu.VMEM((SUMMED, width), F32),
             pltpu.VMEM((2, width), F32),
             pltpu.VMEM((places, SUMMED, width), F32),
@@ -1017,7 +1017,7 @@
 
     made = layer_call(
         ndp, nt, count, layer_input, cotangent, ln_gain[None], ln_bias[None], lens, inverse,
-        [wq, w_fc1, w_dense.T, w_fc2.T], [bias_q, bias_1, (b_dense + b_fc2)[None]],
+        [wq, w_fc1, w_dense, w_fc2], [bias_q, bias_1, b_dense[None], b_fc2[None]],
     )
     output, grad_x, small = made[:3]
 

time: 598 us -> 589 us (0.985)
  Pallas kernels: 562 us -> 553 us
    pallas_call x1, Pallas kernels: 562 us -> 553 us  [layer_call(): pl.pallas_call(functools.partial(layer_kernel, ndp, nt, count), in_specs=...]
    unnamed x26 -> x22, local copies, waits for them, and re-layouts: 17.1 us -> 13.9 us
where the time goes in v6:
time: 589 us; the launch traced here: 579 us
  Pallas kernels  553 us (94%)
  local copies, waits for them, and re-layouts  22.3 us (4%)
    pallas_call x1, Pallas kernels, layer_call(): pl.pallas_call(functools.partial(layer_kernel, ndp, nt, count), in_specs=...  553 us
    unnamed x22, local copies, waits for them, and re-layouts  13.9 us

profile of v6, /device:TPU:0, one launch (start us, length us, event | category | flops | bytes accessed | tf_op | source)
XLA Modules:
  0.0 578.6 jit_solution(16267428277303082903)
XLA Ops:
  0.7 0.7 copy-done
  1.3 0.7 convert_element_type.4
  2.0 0.6 concatenate.5
  2.6 0.6 scatter.4.refs_4_
  3.2 0.6 reshape.84.refs_10_
  3.8 0.7 reshape.85
  4.5 0.6 constant_dynamic-slice_fusion.refs_11_
  5.1 1.4 copy.32
  6.6 1.2 copy.35.refs_6_
  7.7 552.9 %shard_map.220 = (bf16[512,2048]{1,0:T(8,128)(2,1)}, f32[512,2048]{1,0:T(8,128)}, f32[2,8,2048]{2,1,0:T(8,128)}, f32[2048,256]{1,0:T(8,128)}, f32[512,256]{1,0:T...) custom-call(bf16[512,2048]{1,0:T(8,128)(2,1)} %refs_0_.1, ...), custom_call_target="tpu_custom_call" | custom-call | tf_op jit(solution)/shard_map/pallas_call | solution.py:960
  560.7 1.6 fusion
  562.3 0.9 broadcast_select_fusion.1
  563.2 0.6 pad_maximum_fusion
  563.8 0.6 reshape_squeeze.6
  564.4 1.9 copy.36
  566.3 0.1 copy.37
  566.4 1.6 copy.38
  568.0 0.6 copy.45
  568.6 3.5 copy.46
  572.1 2.1 copy.47
  574.2 0.8 copy.48
  575.0 0.5 copy-done.4
  575.6 1.3 copy.49
  576.9 1.3 copy.50
  (17 shorter events, 0.1 us)
Async XLA Ops:
  0.6 0.7 copy-start
  562.3 5.8 copy-start.6
  568.0 4.1 copy-start.2
  572.1 2.1 copy-start.5
  572.1 3.5 copy-start.4
  574.2 2.7 copy-start.3
  575.6 2.6 copy-start.1
